TPU v7x, 128 devices: a whole 4x4x4 slice. The times are simulated.
128 devices in a mesh: dp: 8 (over y, z_hi), fsdp: 16 (over x, z_lo, core).
Axes of the slice: x: 4, y: 4, z: 4 (z_hi: 2, z_lo: 2; z = z_hi * 2 + z_lo), core: 2. Of those that a mesh axis runs over, the one named last changes fastest.
Arguments:
- q_in: bfloat16 [16384, 4096], P(('dp', 'fsdp')), may hold values from -6.5 to 6.5
- k_in: bfloat16 [16384, 512], P(('dp', 'fsdp')), may hold values from -6.5 to 6.5
- v_in: bfloat16 [16384, 512], P(('dp', 'fsdp')), may hold values from -6 to 6
- grad_out: bfloat16 [16384, 4096], P(('dp', 'fsdp')), may hold values from -6 to 6
- q_gain: float32 [128], replicated, may hold values from 0.6 to 5.5
- k_gain: float32 [128], replicated, may hold values from 0.6 to 5.5
- shift_plan: int32 [16, 8], P('fsdp'), may hold values from 0 to 7, each once within a row
- segment_ids: int32 [8, 2048], P('dp', 'fsdp'), may hold values from 0 to 7, never falling along the last dimension, each value on 1 to 1024 neighbouring positions
Outputs:
- dq_in: bfloat16 [16384, 4096], P(('dp', 'fsdp'))
- dk_in: bfloat16 [16384, 512], P(('dp', 'fsdp'))
- dv_in: bfloat16 [16384, 512], P(('dp', 'fsdp'))
- q_gain_grad: float32 [128], replicated
- k_gain_grad: float32 [128], replicated
Inputs may be any that keep to these rules, and one draw needn't show every extreme that they name: `shift_plan`: each row of the swap plan names every number from 0 to 7 once. `segment_ids`: each group's ids never fall along its rows; each rollout holds 1 to 1024 tokens and one holds exactly 1024.
All inputs are finite; a program needn't handle non-finite values.
Results may differ from a plain program's by a relative error of at most 0.01.
The roundings to bfloat16 on the way count: a program that leaves them out, or rounds other values in their place, can miss the bound.
Values may be sent and summed in bfloat16 or wider, within the bound.
No kernel may reach another device: no remote copies, remote signals or barrier semaphores. Data moves between devices by JAX's collectives and lax.ppermute only.
A program may use at most 192 MiB of HBM per device.

v0:
```python
import math

import jax
import jax.numpy as jnp
from jax import lax
from jax.sharding import PartitionSpec as P

THETA = 1000000.0
EPS = 1e-06
NEG = -1e30


def carried_in(value, axis, join, neutral):
    count, mine = (lax.axis_size(axis), lax.axis_index(axis))
    pieces = jax.tree.map(lambda part: lax.all_gather(part, axis), value)
    so_far = jax.tree.map(
        lambda part, zero: jnp.full_like(part, 0) + jnp.asarray(zero, part.dtype), value, neutral
    )

    def turn(position, so_far):
        longer = join(so_far, jax.tree.map(lambda part: part[position], pieces))
        return jax.tree.map(lambda new, old: jnp.where(position < mine, new, old), longer, so_far)

    return lax.fori_loop(0, count - 1, turn, so_far)


def rope_tables(positions, head_dim):
    half = head_dim // 2
    freq = THETA ** (-(jnp.arange(half, dtype=jnp.float32) * 2.0 / head_dim))
    angle = positions.astype(jnp.float32)[:, None] * freq[None, :]
    return (jnp.cos(angle), jnp.sin(angle))


def norm_rope(x, gain, cosine, sine):
    values = x.astype(jnp.float32)
    rscale = lax.rsqrt(jnp.mean(values * values, axis=-1, keepdims=True) + EPS)
    normed = values * rscale * gain
    half = x.shape[-1] // 2
    first, second = (normed[..., :half], normed[..., half:])
    cos_b, sin_b = (cosine[:, None, :], sine[:, None, :])
    turned = jnp.concatenate(
        [first * cos_b - second * sin_b, second * cos_b + first * sin_b], axis=-1
    )
    return (turned.astype(jnp.bfloat16), rscale)


def norm_rope_back(grad, x, gain, rscale, cosine, sine):
    half = grad.shape[-1] // 2
    cos_b, sin_b = (cosine[:, None, :], sine[:, None, :])
    upper, lower = (grad[..., :half], grad[..., half:])
    dnormed = jnp.concatenate(
        [upper * cos_b + lower * sin_b, lower * cos_b - upper * sin_b], axis=-1
    )
    values = x.astype(jnp.float32)
    gain_term = jnp.sum(dnormed * values * rscale, axis=(0, 1))
    inner = dnormed * gain
    dx = rscale * inner - values * rscale**3 * jnp.mean(inner * values, axis=-1, keepdims=True)
    return (dx.astype(jnp.bfloat16), gain_term)


def join_runs(earlier, later):
    e_first, e_last, e_start = earlier
    l_first, l_last, l_start = later
    first = jnp.where(e_first < 0, l_first, e_first)
    last = jnp.where(l_last < 0, e_last, l_last)
    carry_on = (l_first == l_last) & (e_last == l_last)
    start = jnp.where(l_last < 0, e_start, jnp.where(carry_on, e_start, l_start))
    return (first, last, start)


def key_blocks(count):
    width = math.gcd(count, 512)
    return (width, count // width)


def stats_step(carry, piece, queries, q_index, q_seg, heads_k, head_dim):
    keys, values, k_seg = piece
    width, nblk = key_blocks(keys.shape[0])
    scale = head_dim ** (-0.5)

    def stats_one(blk, state):
        top, total, acc = state
        first = blk * width
        key_blk = lax.dynamic_slice_in_dim(keys, first, width, 0).reshape(width, heads_k, head_dim)
        val_blk = lax.dynamic_slice_in_dim(values, first, width, 0).reshape(
            width, heads_k, head_dim
        )
        seg_blk = lax.dynamic_slice_in_dim(k_seg, first, width, 0)
        k_index = first + jnp.arange(width, dtype=jnp.int32)
        allowed = (q_seg[:, None] == seg_blk[None, :]) & (k_index[None, :] <= q_index[:, None])
        score = (
            jnp.einsum("qksd,tkd->ksqt", queries, key_blk, preferred_element_type=jnp.float32)
            * scale
        )
        score = jnp.where(allowed, score, NEG)
        new_top = jnp.maximum(top, jnp.max(score, axis=-1))
        weight = jnp.where(allowed, jnp.exp(score - new_top[..., None]), 0.0)
        fade = jnp.exp(top - new_top)
        total = total * fade + jnp.sum(weight, axis=-1)
        acc = acc * fade[..., None] + jnp.einsum(
            "ksqt,tkd->ksqd", weight, val_blk, preferred_element_type=jnp.float32
        )
        return (new_top, total, acc)

    return lax.fori_loop(0, nblk, stats_one, carry)


def grads_step(carry, piece, queries, grads, lse, delta, q_index, q_seg, heads_k, head_dim):
    keys, values, k_seg = piece
    width, nblk = key_blocks(keys.shape[0])
    scale = head_dim ** (-0.5)

    def grads_one(blk, state):
        first = blk * width
        key_blk = lax.dynamic_slice_in_dim(keys, first, width, 0).reshape(width, heads_k, head_dim)
        val_blk = lax.dynamic_slice_in_dim(values, first, width, 0).reshape(
            width, heads_k, head_dim
        )
        seg_blk = lax.dynamic_slice_in_dim(k_seg, first, width, 0)
        k_index = first + jnp.arange(width, dtype=jnp.int32)
        allowed = (q_seg[:, None] == seg_blk[None, :]) & (k_index[None, :] <= q_index[:, None])
        score = (
            jnp.einsum("qksd,tkd->ksqt", queries, key_blk, preferred_element_type=jnp.float32)
            * scale
        )
        prob = jnp.where(allowed, jnp.exp(score - lse[..., None]), 0.0)
        prob_b = prob.astype(jnp.bfloat16)
        dprob = jnp.einsum("qksd,tkd->ksqt", grads, val_blk, preferred_element_type=jnp.float32)
        dscore = (prob * (dprob - delta[..., None])).astype(jnp.bfloat16)
        dq = (
            state[0]
            + jnp.einsum("ksqt,tkd->ksqd", dscore, key_blk, preferred_element_type=jnp.float32)
            * scale
        )
        dk = (
            jnp.einsum("ksqt,qksd->tkd", dscore, queries, preferred_element_type=jnp.float32)
            * scale
        )
        dv = jnp.einsum("ksqt,qksd->tkd", prob_b, grads, preferred_element_type=jnp.float32)
        term = jnp.concatenate([dk.reshape(width, -1), dv.reshape(width, -1)], axis=1)
        old = lax.dynamic_slice_in_dim(state[1], first, width, 0)
        return (dq, lax.dynamic_update_slice_in_dim(state[1], old + term, first, 0))

    return lax.fori_loop(0, nblk, grads_one, carry)


def body(q_in, k_in, v_in, grad_out, q_gain, k_gain, shift_plan, segment_ids):
    groups = lax.axis_size("dp")
    member = lax.axis_index("dp")
    shard = lax.axis_index("fsdp")
    shards = lax.axis_size("fsdp")
    rows = q_in.shape[0]
    run = rows // groups
    head_dim = q_gain.shape[0]
    heads_q = q_in.shape[1] // head_dim
    heads_k = k_in.shape[1] // head_dim
    share = heads_q // heads_k
    plan = shift_plan[0]
    slots = jnp.arange(groups, dtype=jnp.int32)
    inverse = jnp.sum(slots[None, :] * (plan[None, :] == slots[:, None]).astype(jnp.int32), axis=1)
    order = inverse[(slots - member) % groups]
    source = (member - plan) % groups

    def arrange(x):
        return jnp.take(x.reshape(groups, run, x.shape[1]), order, axis=0)

    received = (
        lax.all_to_all(arrange(q_in), "dp", split_axis=0, concat_axis=0, tiled=True),
        lax.all_to_all(arrange(k_in), "dp", split_axis=0, concat_axis=0, tiled=True),
        lax.all_to_all(arrange(v_in), "dp", split_axis=0, concat_axis=0, tiled=True),
    )
    q_rows = jnp.take(received[0], source, axis=0).reshape(rows, q_in.shape[1])
    k_rows = jnp.take(received[1], source, axis=0).reshape(rows, k_in.shape[1])
    v_rows = jnp.take(received[2], source, axis=0).reshape(rows, v_in.shape[1])
    seg = segment_ids[0]
    base = shard * rows
    g_index = base + jnp.arange(rows, dtype=jnp.int32)
    boundary = jnp.concatenate([jnp.ones((1,), jnp.bool_), seg[1:] != seg[:-1]])
    start_local = lax.cummax(jnp.where(boundary, g_index, base), axis=0)
    summary = (seg[0], seg[rows - 1], start_local[rows - 1])
    neutral = (jnp.int32(-1), jnp.int32(-1), jnp.int32(0))
    prev_first, prev_last, prev_start = carried_in(summary, "fsdp", join_runs, neutral)
    starts = jnp.where(seg == prev_last, prev_start, start_local)
    cosine, sine = rope_tables(g_index - starts, head_dim)
    q_raw = q_rows.reshape(rows, heads_q, head_dim)
    k_raw = k_rows.reshape(rows, heads_k, head_dim)
    q_rot, q_scale = norm_rope(q_raw, q_gain, cosine, sine)
    k_rot, k_scale = norm_rope(k_raw, k_gain, cosine, sine)
    queries = q_rot.reshape(rows, heads_k, share, head_dim)
    grads = grad_out.reshape(rows, heads_k, share, head_dim)
    k_flat = k_rot.reshape(rows, heads_k * head_dim)
    init_stats = (
        jnp.full((heads_k, share, rows), NEG, jnp.float32),
        jnp.zeros((heads_k, share, rows), jnp.float32),
        jnp.zeros((heads_k, share, rows, head_dim), jnp.float32),
    )
    zero_dq = jnp.zeros((heads_k, share, rows, head_dim), jnp.float32)
    init_grads = (zero_dq, jnp.zeros((rows * shards, 2 * heads_k * head_dim), jnp.float32))
    top, total, acc = stats_step(
        init_stats,
        (
            lax.all_gather(k_flat, "fsdp", axis=0, tiled=True),
            lax.all_gather(v_rows, "fsdp", axis=0, tiled=True),
            lax.all_gather(seg, "fsdp", axis=0, tiled=True),
        ),
        queries,
        g_index,
        seg,
        heads_k,
        head_dim,
    )
    lse = top + jnp.log(total)
    out = acc / total[..., None]
    delta = jnp.einsum("qksd,ksqd->ksq", grads, out, preferred_element_type=jnp.float32)
    result = grads_step(
        init_grads,
        (
            lax.all_gather(k_flat, "fsdp", axis=0, tiled=True),
            lax.all_gather(v_rows, "fsdp", axis=0, tiled=True),
            lax.all_gather(seg, "fsdp", axis=0, tiled=True),
        ),
        queries,
        grads,
        lse,
        delta,
        g_index,
        seg,
        heads_k,
        head_dim,
    )
    reduced = lax.psum_scatter(result[1], "fsdp", scatter_dimension=0, tiled=True)
    dk_rot = reduced[:, : heads_k * head_dim].reshape(rows, heads_k, head_dim)
    dv_sum = reduced[:, heads_k * head_dim :]
    dq_rot = jnp.transpose(result[0], (2, 0, 1, 3)).reshape(rows, heads_q, head_dim)
    dq_out, q_term = norm_rope_back(dq_rot, q_raw, q_gain, q_scale, cosine, sine)
    dk_out, k_term = norm_rope_back(dk_rot, k_raw, k_gain, k_scale, cosine, sine)
    q_total, k_total = lax.psum((q_term, k_term), ("dp", "fsdp"))
    return (
        dq_out.reshape(rows, heads_q * head_dim),
        dk_out.reshape(rows, heads_k * head_dim),
        dv_sum.astype(jnp.bfloat16),
        q_total,
        k_total,
    )


def solution(mesh):
    return jax.shard_map(
        body,
        mesh=mesh,
        in_specs=(
            P(("dp", "fsdp"), None),
            P(("dp", "fsdp"), None),
            P(("dp", "fsdp"), None),
            P(("dp", "fsdp"), None),
            P(),
            P(),
            P("fsdp", None),
            P("dp", "fsdp"),
        ),
        out_specs=(
            P(("dp", "fsdp"), None),
            P(("dp", "fsdp"), None),
            P(("dp", "fsdp"), None),
            P(),
            P(),
        ),
        check_vma=False,
    )
```

profile of v0, /device:TPU:3, one launch (start us, length us, event | category | flops | bytes accessed | tf_op | source)
XLA Modules:
  0.0 572.0 jit_solution(2457901055720898540)
XLA Ops:
  12.5 14.2 %all_to_all.15 = bf16[8,16,512]{2,1,0:T(8,128)(2,1)S(1)} all-to-all(bf16[8,16,512]{2,1,0:T(8,128)(2,1)S(1)} %get-tuple-element.792), channel_id=1, replica_groups=mesh['dp'=8,'fsdp'=16] {'dp'}, dimensions={0} | all-to-all | bytes 262144 | tf_op jit(solution)/shard_map/all_to_all | solution.py:169
  30.7 6.0 %all-to-all-done.2 = bf16[8,16,512]{2,1,0:T(8,128)(2,1)S(1)} async-done(((bf16[8,16,512]{2,1,0:T(8,128)(2,1)}), bf16[8,16,512]{2,1,0:T(8,128)(2,1)S(1)}, u32[]{:S(2)}, u32[]{:S(2)}) %all-to-all-start.2) | async-done | bytes 131104 | tf_op jit(solution)/shard_map/all_to_all | solution.py:170
  45.3 11.6 %all-reduce.3 = (s32[16]{0:T(128)S(1)}, s32[16]{0:T(128)S(1)}, s32[16]{0:T(128)S(1)}) all-reduce(s32[16]{0:T(128)S(1)} %bitcast_dynamic-update-slice_fusion.2, s32[16]{0:T(128)S(1)} %bitcast_dynamic-update-slice_fusion.1, s32[16]{0:T(128)S(1)} %bitcast_dynamic-update-slice_fusion), channel_id=3, replica_groups=mesh['dp'=8,'fsdp'=16] {'fsdp'}, use_global_device_ids=true, to_apply=%add | all-reduce | flops 48 | bytes 384 | tf_op jit(solution)/shard_map/all_gather | solution.py:15
  57.0 89.9 %while.49 = (s32[]{:T(128)}, s32[]{:T(128)}, s32[]{:T(128)}, s32[]{:T(128)}, s32[16]{0:T(128)S(1)}, /*index=5*/s32[16]{0:T(128)S(1)}, s32[16]{0:T(128)S(1)}, s32[]{:T(128)}, s32[]{:T(128)}) while((s32[]{:T(128)}, s32[]{:T(128)}, s32[]{:T(128)}, s32[]{:T(128)}, s32[16]{0:T(128)S(1)}, /*index=5*/s32[16]{0:T(128)S(1)}, s32[16]{0:T(128)S(1)}, ...), condition=%wide.region_5.8_spmd, body=%wide.region_4.7_spmd.sunk | while | flops 12 | bytes 233 | solution.py:24
  157.0 23.0 %all-gather = s32[1,2048]{1,0:T(1,128)S(1)} all-gather(s32[1,128]{1,0:T(1,128)S(1)} %copy-done.33), channel_id=2, replica_groups=mesh['dp'=8,'fsdp'=16] {'fsdp'}, dimensions={1}, use_global_device_ids=true | all-gather | bytes 8704 | tf_op jit(solution)/shard_map/all_gather | solution.py:220
  192.2 68.5 %while.50 = (s32[]{:T(128)}, f32[4,8,128]{2,1,0:T(8,128)S(1)}, f32[4,8,128]{2,1,0:T(8,128)S(1)}, f32[4,8,128,128]{3,2,1,0:T(8,128)}, s32[1,128]{1,0:T(1,128)S(1)...) while((s32[]{:T(128)}, f32[4,8,128]{2,1,0:T(8,128)S(1)}, ...), condition=%wide.region_9.12_spmd.clone, body=%wide.region_6.11_spmd.clone.sunk | while | flops 1100698240 | bytes 67645160 | solution.py:105
  193.8 4.7 fusion.78
  198.5 4.7 fusion.79
  210.0 4.7 fusion.78
  214.7 4.7 fusion.79
  220.5 5.3 fusion.81
  227.4 4.7 fusion.78
  232.1 4.7 fusion.79
  237.9 5.3 fusion.81
  244.8 4.7 fusion.78
  255.4 5.3 fusion.81
  271.4 125.6 %while.51 = (s32[]{:T(128)}, f32[4,8,128,128]{3,2,1,0:T(8,128)}, f32[2048,1024]{1,0:T(8,128)}, s32[1,128]{1,0:T(1,128)S(1)}, s32[2048]{0:T(1024)S(1)}, /*index=5...) while((s32[]{:T(128)}, f32[4,8,128,128]{3,2,1,0:T(8,128)}, ...), condition=%wide.region_11.14_spmd.clone, body=%wide.region_10.13_spmd.clone.sunk | while | flops 2708406784 | bytes 98299704 | solution.py:144
  304.1 5.4 select_add_fusion.2
  332.5 6.1 %select_add_fusion.2 = f32[4,8,128,128]{3,2,1,0:T(8,128)} fusion(f32[4,8,128,128]{3,2,1,0:T(8,128)} %get-tuple-element.1074, bf16[4,8,128,512]{2,3,1,0:T(8,128)(2,1)} %copy-done.3, bf16[512,4,128,1]{0,2,3,1:T(8,128)(2,1)} %bitcast.239, pred[]{:T(512)S(6)} %compare.15), kind=kOutput, calls=%fused_computation.43.clone.1 | convolution fusion | flops 538443776 | bytes 8912897 | tf_op jit(solution)/shard_map/while/body/eval_jaxpr/ksqt,tkd->ksqd/dot_general | solution.py:132
  361.7 6.1 %select_add_fusion.2 = f32[4,8,128,128]{3,2,1,0:T(8,128)} fusion(f32[4,8,128,128]{3,2,1,0:T(8,128)} %get-tuple-element.1074, bf16[4,8,128,512]{2,3,1,0:T(8,128)(2,1)} %copy-done.3, bf16[512,4,128,1]{0,2,3,1:T(8,128)(2,1)} %bitcast.239, pred[]{:T(512)S(6)} %compare.15), kind=kOutput, calls=%fused_computation.43.clone.1 | convolution fusion | flops 538443776 | bytes 8912897 | tf_op jit(solution)/shard_map/while/body/eval_jaxpr/ksqt,tkd->ksqd/dot_general | solution.py:132
  391.0 6.1 %select_add_fusion.2 = f32[4,8,128,128]{3,2,1,0:T(8,128)} fusion(f32[4,8,128,128]{3,2,1,0:T(8,128)} %get-tuple-element.1074, bf16[4,8,128,512]{2,3,1,0:T(8,128)(2,1)} %copy-done.3, bf16[512,4,128,1]{0,2,3,1:T(8,128)(2,1)} %bitcast.239, pred[]{:T(512)S(6)} %compare.15), kind=kOutput, calls=%fused_computation.43.clone.1 | convolution fusion | flops 538443776 | bytes 8912897 | tf_op jit(solution)/shard_map/while/body/eval_jaxpr/ksqt,tkd->ksqd/dot_general | solution.py:132
  417.3 5.7 fusion.29
  423.1 72.2 %reduce-scatter.2.cloned.1.call-done = f32[128,1024]{1,0:T(8,128)} async-done(((f32[2048,1024]{1,0:T(8,128)}), f32[128,1024]{1,0:T(8,128)}) %reduce-scatter.2.cloned.1.call-update) | async-done | bytes 524304 | tf_op jit(solution)/shard_map/reduce_scatter | solution.py:231
  497.4 65.0 %all-reduce.4 = (f32[128]{0:T(128)}, f32[128]{0:T(128)}) all-reduce(f32[128]{0:T(128)S(1)} %copy-done.43, f32[128]{0:T(128)S(1)} %bitcast_reduce_fusion.1), channel_id=1, replica_groups=mesh['dp'=8,'fsdp'=16] {'dp','fsdp'}, use_global_device_ids=true, to_apply=%region_17.20 | all-reduce | flops 256 | bytes 2048 | tf_op jit(solution)/shard_map/psum | solution.py:237
  (355 shorter events, 216.6 us)
Async XLA Ops:
  7.2 32.1 %copy-start = (bf16[128,4096]{1,0:T(8,128)(2,1)S(1)}, bf16[128,4096]{1,0:T(8,128)(2,1)}, u32[]{:S(2)}) copy-start(bf16[128,4096]{1,0:T(8,128)(2,1)} %param.18) | copy-start | bytes 3145732
  7.2 22.9 %copy-start.44 = (s32[1,8]{1,0:T(1,128)S(1)}, s32[1,8]{1,0:T(1,128)}, u32[]{:S(2)}) copy-start(s32[1,8]{1,0:T(1,128)} %param.24) | copy-start | bytes 100
  7.2 30.9 %copy-start.33 = (s32[1,128]{1,0:T(1,128)S(1)}, s32[1,128]{1,0:T(1,128)}, u32[]{:S(2)}) copy-start(s32[1,128]{1,0:T(1,128)} %param.25) | copy-start | bytes 1540
  12.5 27.5 %copy-start.45 = (u32[128]{0:T(128)S(1)}, u32[128]{0:T(128)}, u32[]{:S(2)}) copy-start(u32[128]{0:T(128)} %constant.207) | copy-start | bytes 1540
  26.6 10.1 %all-to-all-start.2 = ((bf16[8,16,512]{2,1,0:T(8,128)(2,1)}), bf16[8,16,512]{2,1,0:T(8,128)(2,1)S(1)}, u32[]{:S(2)}, u32[]{:S(2)}) async-start(bf16[8,16,512]{2,1,0:T(8,128)(2,1)} %get-tuple-element.791), calls=%async_computation.2 | async-start | bytes 262144 | tf_op jit(solution)/shard_map/all_to_all | solution.py:170
  30.0 158.2 %all-gather.9.cloned.1.call-start = ((), (), s32[]{:S(2)}) async-start(), calls=%async_computation.5 | async-start | bytes 2228224 | tf_op jit(solution)/shard_map/all_gather | solution.py:219
  30.1 150.5 %copy-start.34 = (pred[8]{0:T(512)(128)(4,1)}, pred[8]{0:T(512)(128)(4,1)S(1)}, u32[]{:S(2)}) copy-start(pred[8]{0:T(512)(128)(4,1)S(1)} %get-tuple-element.765) | copy-start | bytes 28
  30.7 8.6 %copy-start.23 = (bf16[8,16,512]{2,1,0:T(8,128)(2,1)}, bf16[8,16,512]{2,1,0:T(8,128)(2,1)S(1)}, u32[]{:S(2)}) copy-start(bf16[8,16,512]{2,1,0:T(8,128)(2,1)S(1)} %gather_fusion.4) | copy-start | bytes 393220
  38.0 110.5 %copy-start.17 = (f32[8,16,512]{2,1,0:T(8,128)}, f32[8,16,512]{2,1,0:T(8,128)S(1)}, u32[]{:S(2)}) copy-start(f32[8,16,512]{2,1,0:T(8,128)S(1)} %get-tuple-element.790) | copy-start | bytes 786436
  38.0 110.3 %copy-start.40 = (f32[128]{0:T(128)S(1)}, f32[128]{0:T(128)}, u32[]{:S(2)}) copy-start(f32[128]{0:T(128)} %param.23) | copy-start | bytes 1540
  38.1 154.1 %all-gather.7.cloned.1.call-start = ((), (), s32[]{:S(2)}) async-start(), calls=%async_computation.4 | async-start | bytes 2228224 | tf_op jit(solution)/shard_map/all_gather | solution.py:218
  147.2 37.2 %copy-start.19 = (f32[128,64]{1,0:T(8,128)}, f32[128,64]{1,0:T(8,128)S(1)}, u32[]{:S(2)}) copy-start(f32[128,64]{1,0:T(8,128)S(1)} %get-tuple-element.787) | copy-start | bytes 98308
  147.2 37.2 %copy-start.21 = (f32[128,64]{1,0:T(8,128)}, f32[128,64]{1,0:T(8,128)S(1)}, u32[]{:S(2)}) copy-start(f32[128,64]{1,0:T(8,128)S(1)} %get-tuple-element.788) | copy-start | bytes 98308
  151.0 28.9 %all-to-all-start = ((bf16[8,16,4096]{2,1,0:T(8,128)(2,1)}), bf16[8,16,4096]{2,1,0:T(8,128)(2,1)S(1)}, u32[]{:S(2)}, u32[]{:S(2)}) async-start(bf16[8,16,4096]{2,1,0:T(8,128)(2,1)} %broadcast_select_fusion), calls=%async_computation | async-start | bytes 2097152 | tf_op jit(solution)/shard_map/all_to_all | solution.py:168
  154.6 340.7 %reduce-scatter.2.cloned.1.call-start = ((), (), s32[]{:S(2)}) async-start(), calls=%async_computation.6 | async-start | bytes 8912896 | tf_op jit(solution)/shard_map/reduce_scatter | solution.py:231
  423.0 73.7 %copy-start.16 = (f32[128,4,128]{2,1,0:T(4,128)S(1)}, f32[128,4,128]{2,1,0:T(4,128)}, u32[]{:S(2)}) copy-start(f32[128,4,128]{2,1,0:T(4,128)} %copy-done.15) | copy-start | bytes 786436
  423.0 73.7 %copy-start.42 = (f32[128]{0:T(128)S(1)}, f32[128]{0:T(128)}, u32[]{:S(2)}) copy-start(f32[128]{0:T(128)} %param.23) | copy-start | bytes 1540
  423.0 74.2 %copy-start.24 = (bf16[8,16,512]{2,1,0:T(8,128)(2,1)S(1)}, bf16[8,16,512]{2,1,0:T(8,128)(2,1)}, u32[]{:S(2)}) copy-start(bf16[8,16,512]{2,1,0:T(8,128)(2,1)} %copy-done.23) | copy-start | bytes 393220
  423.0 74.2 %copy-start.25 = (f32[8,16,512]{2,1,0:T(8,128)S(1)}, f32[8,16,512]{2,1,0:T(8,128)}, u32[]{:S(2)}) copy-start(f32[8,16,512]{2,1,0:T(8,128)} %mul.453) | copy-start | bytes 786436
  423.0 74.2 %copy-start.35 = (pred[8]{0:T(512)(128)(4,1)S(1)}, pred[8]{0:T(512)(128)(4,1)}, u32[]{:S(2)}) copy-start(pred[8]{0:T(512)(128)(4,1)} %copy-done.34) | copy-start | bytes 28
  496.4 66.3 %copy-start.32 = (f32[128,4]{1,0:T(8,128)S(1)}, f32[128,4]{1,0:T(8,128)}, u32[]{:S(2)}) copy-start(f32[128,4]{1,0:T(8,128)} %copy.140) | copy-start | bytes 6148
  496.4 66.5 %copy-start.18 = (f32[8,16,512]{2,1,0:T(8,128)S(1)}, f32[8,16,512]{2,1,0:T(8,128)}, u32[]{:S(2)}) copy-start(f32[8,16,512]{2,1,0:T(8,128)} %copy-done.17) | copy-start | bytes 786436
  496.4 66.5 %copy-start.36 = (f32[512]{0:T(512)S(1)}, f32[512]{0:T(512)}, u32[]{:S(2)}) copy-start(f32[512]{0:T(512)} %broadcast_bitcast_fusion.1) | copy-start | bytes 6148
  496.7 68.6 %copy-start.1 = (bf16[128,4096]{1,0:T(8,128)(2,1)S(1)}, bf16[128,4096]{1,0:T(8,128)(2,1)}, u32[]{:S(2)}) copy-start(bf16[128,4096]{1,0:T(8,128)(2,1)} %param.18) | copy-start | bytes 3145732
  (39 other events, 105.3 us)
Sparse Core Ops, SparseCore 0:
  38.2 34.3 all-gather.8
  150.0 41.6 all-gather.6
  397.2 98.0 reduce-scatter.1
where the time goes:
time: 579 us; the launch traced here: 572 us
  local copies, waits for them, and re-layouts  125 us (22%)
  blocking collectives  114 us (20%)
  matrix products  100 us (17%)
  waiting for transfers between devices  78.3 us (14%)
  loops' own time  70.6 us (12%)
  other arithmetic  62.6 us (11%)
  between operations  14.8 us (3%)
  starting transfers between devices  7.06 us (1%)
    reduce_scatter x1, waiting for transfers between devices, body(): lax.psum_scatter(result[1], 'fsdp', scatter_dimension=0, tiled=True)  72.2 us
    psum x1, blocking collectives, body(): q_total, k_total = lax.psum((q_term, k_term), ('dp', 'fsdp'))  65 us
    another operation x1, loops' own time, carried_in(): return lax.fori_loop(0, count - 1, turn, so_far)  60.6 us
    dynamic_slice x45, local copies, waits for them, and re-layouts, turn(): longer = join(so_far, jax.tree.map(lambda part: part[position], pieces))  29.3 us
    dot_general x4, matrix products, grads_one(): jnp.einsum('ksqt,tkd->ksqd', dscore, key_blk, preferred_element_type=jnp....  23.6 us
    all_gather x1, blocking collectives, body(): lax.all_gather(seg, 'fsdp', axis=0, tiled=True)  23 us
    dynamic_slice x8, local copies, waits for them, and re-layouts, grads_one(): old = lax.dynamic_slice_in_dim(state[1], first, width, 0)  20.6 us
    dot_general x4, matrix products, stats_one(): jnp.einsum('ksqt,tkd->ksqd', weight, val_blk, preferred_element_type=jnp....  19.9 us
  transfers between devices with their start and end apart: 5, of which 2 were waited for; matrix products, arithmetic and copies ran while one was open for 14% of the time, Pallas kernels for 0%

commit v1 on v0

v1 whole, which is shorter than its diff:
```python
import math

import jax
import jax.numpy as jnp
from jax import lax
from jax.experimental import pallas as pl
from jax.experimental.pallas import tpu as pltpu
from jax.sharding import Mesh, PartitionSpec as P

THETA = 1000000.0
EPS = 1e-06
NEG = -1e30
HD = 128
RUN = 16
TILE = 128
BACK = 8
WIN = (BACK + 1) * TILE
ALLW = (BACK + 2) * TILE
SCALE = HD**-0.5
TO_EXP2 = SCALE * math.log2(math.e)
BF = jnp.bfloat16
F32 = jnp.float32
VM = pl.BlockSpec(memory_space=pltpu.VMEM)
SM = pl.BlockSpec(memory_space=pltpu.SMEM)
PARAMS = pltpu.CompilerParams(vmem_limit_bytes=44 * 1024 * 1024)


def sincos(angle):
    turns = jnp.round(angle * (2.0 / math.pi))
    r = ((angle - turns * 1.5703125) - turns * 4.837512969970703e-4) - turns * 7.549789948768648e-8
    r2 = r * r
    sin_r = r + r * r2 * (-1.6666654611e-1 + r2 * (8.3321608736e-3 - 1.9515295891e-4 * r2))
    cos_r = 1.0 - 0.5 * r2 + r2 * r2 * (
        4.166664568298827e-2 + r2 * (-1.388731625493765e-3 + 2.443315711809948e-5 * r2)
    )
    quarter = turns.astype(jnp.int32)
    swap = (quarter & 1) == 1
    s = jnp.where(swap, cos_r, sin_r)
    c = jnp.where(swap, sin_r, cos_r)
    s = jnp.where((quarter & 2) == 2, -s, s)
    c = jnp.where(((quarter + 1) & 2) == 2, -c, c)
    return s, c


def inv_rms(x):
    return lax.rsqrt(jnp.sum(x * x, axis=-1, keepdims=True) * (1.0 / HD) + EPS)


def rope(x, tc, ts):
    return x * tc + pltpu.roll(x, HD // 2, 1) * ts


def rope_back(x, tc, ts):
    return x * tc - pltpu.roll(x, HD // 2, 1) * ts


def norm_back(dn, x, rs, gain):
    w = dn * gain
    return rs * w - x * (rs * rs * rs) * (jnp.sum(w * x, axis=-1, keepdims=True) * (1.0 / HD))


def fold(x, op):
    return op(x.reshape(x.shape[0] // 8, 8, x.shape[1]), axis=0)


def dot(a, b):
    return jnp.dot(a, b, preferred_element_type=F32)


def send_kernel(plan_ref, who_ref, q_ref, k_ref, v_ref, out_ref):
    groups = plan_ref.shape[1]
    wide_q, wide_k = q_ref.shape[1] // 2, k_ref.shape[1] // 2
    for r in range(groups):
        to = lax.rem(who_ref[0] + plan_ref[0, r], groups)
        rows = slice(r * RUN, (r + 1) * RUN)
        for a in range(2):
            out_ref[2 * to + a, :, :wide_q] = q_ref[rows, a * wide_q : (a + 1) * wide_q]
            out_ref[2 * to + a, :, wide_q : wide_q + wide_k] = k_ref[rows, a * wide_k : (a + 1) * wide_k]
            out_ref[2 * to + a, :, wide_q + wide_k :] = v_ref[rows, a * wide_k : (a + 1) * wide_k]


def keys_kernel(src_ref, recv_ref, seg_ref, out_ref):
    for b in range(2):
        for r in range(8):
            rows = slice(b * TILE + r * RUN, b * TILE + (r + 1) * RUN)
            out_ref[rows, :] = recv_ref[src_ref[b * 8 + r]]
    ids = (seg_ref[...] + 1).astype(F32)
    row = jnp.concatenate([ids, jnp.zeros_like(ids)], axis=1)
    out_ref[2 * TILE :, :] = jnp.broadcast_to(row, (RUN, row.shape[1])).astype(BF)


def main_kernel(
    core_ref, src_ref, recv_ref, kv4, kv3, kv2, kv1, kv0, g_own, g_sib, freq_ref, qg_ref, kg_ref,
    dq_own, dq_sib, out1, out2, out3, out4, own_ref, tco_ref, tso_ref, gains_ref,
    tc, ts, kr, kt, vs, xq, q8, g8, bias, sc, dp, pb, db, dk_acc, dv_acc,
):
    core = core_ref[0]
    kvs = (kv4, kv3, kv2, kv1, kv0)
    lane = lax.broadcasted_iota(jnp.int32, (TILE, TILE), 1)
    sub = lax.broadcasted_iota(jnp.int32, (TILE, TILE), 0)
    ids = [kv[2 * TILE :, : 2 * TILE].astype(F32)[:8] for kv in kvs]
    begin = jnp.zeros_like(ids[-1])
    for v in range(1, 9):
        less = sum(jnp.where(one < v, 1.0, 0.0) for one in ids)
        begin = begin + jnp.where(ids[-1] == v, jnp.sum(less, axis=1, keepdims=True), 0.0)
    first = begin[0:1, 0:1]
    subf = sub.astype(F32)
    qgain, kgain = qg_ref[...], kg_ref[...]
    for blk in range(BACK + 2):
        rows = slice(blk * TILE, (blk + 1) * TILE)
        if blk < BACK:
            start = first
        else:
            mine = slice((blk - BACK) * TILE, (blk - BACK + 1) * TILE)
            start = jnp.broadcast_to(begin[0:1, mine], (TILE, TILE)).T
        sine, cosine = sincos((subf + float(blk * TILE) - start) * freq_ref[...])
        sine = jnp.where(lane < HD // 2, -sine, sine)
        tc[rows, :] = cosine
        ts[rows, :] = sine
        if blk >= BACK:
            tco_ref[mine, :] = cosine
            tso_ref[mine, :] = sine
        ref, part = kvs[blk // 2], slice((blk % 2) * TILE, (blk % 2 + 1) * TILE)
        for j in range(2):
            x = ref[part, j * HD : (j + 1) * HD].astype(F32)
            turned = rope(x * inv_rms(x) * kgain, cosine, sine)
            kr[j, rows, :] = turned.astype(BF)
            kt[j, :, rows] = turned.T.astype(BF)
            vs[j, rows, :] = ref[part, (2 + j) * HD : (3 + j) * HD]
    dk_acc[...] = jnp.zeros_like(dk_acc)
    dv_acc[...] = jnp.zeros_like(dv_acc)
    q_term = jnp.zeros((8, HD), F32)
    for turn, (g_ref, dq_ref) in enumerate(((g_own, dq_own), (g_sib, dq_sib))):
        tile = core if turn == 0 else 1 - core
        base = pl.multiple_of(tile * TILE, TILE)
        for r in range(8):
            xq[r * RUN : (r + 1) * RUN, :] = recv_ref[src_ref[tile * 8 + r]]
        st = jnp.where(tile == 0, begin[0:1, :TILE], begin[0:1, TILE:]) - (tile * TILE).astype(F32)
        for kb in range(BACK + 1):
            ok = (subf + float(kb * TILE)) >= st
            if kb == BACK:
                ok = ok & (sub <= lane)
            bias[kb * TILE : (kb + 1) * TILE, :] = jnp.where(ok, 0.0, NEG)
        own_rows = pl.ds(pl.multiple_of(BACK * TILE + base, TILE), TILE)

        def head(j, q_term):
            def pair(hp, q_term):
                raws, scales, qts, gts = [], [], [], []
                for hh in range(2):
                    cols = pl.ds(pl.multiple_of((j * 8 + hp * 2 + hh) * HD, HD), HD)
                    x = xq[:, cols].astype(F32)
                    rs = inv_rms(x)
                    turned = rope(x * rs * qgain, tc[own_rows, :], ts[own_rows, :])
                    grad = g_ref[:, cols]
                    slot = pl.ds(pl.multiple_of((hp * 2 + hh) * TILE, TILE), TILE)
                    q8[slot, :] = turned.astype(BF)
                    g8[slot, :] = grad
                    raws.append(x)
                    scales.append(rs)
                    qts.append(turned.T.astype(BF))
                    gts.append(grad.astype(F32).T.astype(BF))
                qt = jnp.concatenate(qts, axis=1)
                gt = jnp.concatenate(gts, axis=1)
                top = jnp.full((8, 2 * TILE), NEG, F32)
                for kb in range(BACK + 1):
                    rows = slice(kb * TILE, (kb + 1) * TILE)
                    keys = pl.ds(pl.multiple_of(base + kb * TILE, TILE), TILE)
                    b = bias[rows, :]
                    s = dot(kr[j, keys, :], qt) + jnp.concatenate([b, b], axis=1)
                    sc[rows, :] = s
                    top = jnp.maximum(top, fold(s, jnp.max))
                    dp[rows, :] = dot(vs[j, keys, :], gt)
                top = jnp.max(top, axis=0, keepdims=True) * TO_EXP2
                total = jnp.zeros((8, 2 * TILE), F32)
                inner = jnp.zeros((8, 2 * TILE), F32)
                for kb in range(BACK + 1):
                    rows = slice(kb * TILE, (kb + 1) * TILE)
                    e = jnp.exp2(sc[rows, :] * TO_EXP2 - top)
                    sc[rows, :] = e
                    total = total + fold(e, jnp.sum)
                    inner = inner + fold(e * dp[rows, :], jnp.sum)
                inv = 1.0 / jnp.sum(total, axis=0, keepdims=True)
                delta = jnp.sum(inner, axis=0, keepdims=True) * inv
                two = pl.ds(pl.multiple_of(hp * 2 * TILE, 2 * TILE), 2 * TILE)
                for kb in range(BACK + 1):
                    rows = slice(kb * TILE, (kb + 1) * TILE)
                    p = sc[rows, :] * inv
                    pb[rows, two] = p.astype(BF)
                    db[rows, two] = (p * (dp[rows, :] - delta)).astype(BF)
                dqt = dot(kt[j, :, pl.ds(base, WIN)], db[:, two]) * SCALE
                for hh in range(2):
                    cols = pl.ds(pl.multiple_of((j * 8 + hp * 2 + hh) * HD, HD), HD)
                    dn = rope_back(dqt[:, hh * TILE : (hh + 1) * TILE].T, tc[own_rows, :], ts[own_rows, :])
                    x, rs = raws[hh], scales[hh]
                    q_term = q_term + fold(dn * x * rs, jnp.sum)
                    dq_ref[:, cols] = norm_back(dn, x, rs, qgain).astype(BF)
                return q_term

            q_term = lax.fori_loop(0, 4, pair, q_term)
            keys = pl.ds(base, WIN)
            dv_acc[j, keys, :] += dot(pb[...], g8[...])
            dk_acc[j, keys, :] += dot(db[...], q8[...])
            return q_term

        q_term = lax.fori_loop(0, 2, head, q_term)
    k_term = jnp.zeros((8, HD), F32)
    outs = (out4, out3, out2, out1)
    for blk in range(BACK + 2):
        rows = slice(blk * TILE, (blk + 1) * TILE)
        part = slice((blk % 2) * TILE, (blk % 2 + 1) * TILE)
        for j in range(2):
            dk = dk_acc[j, rows, :] * SCALE
            dv = dv_acc[j, rows, :]
            x = kvs[blk // 2][part, j * HD : (j + 1) * HD].astype(F32)
            dn = rope_back(dk, tc[rows, :], ts[rows, :])
            k_term = k_term + fold(dn * x * inv_rms(x), jnp.sum)
            dk_cols, dv_cols = slice(j * HD, (j + 1) * HD), slice((2 + j) * HD, (3 + j) * HD)
            if blk < BACK:
                outs[blk // 2][part, dk_cols] = dk.astype(BF)
                outs[blk // 2][part, dv_cols] = dv.astype(BF)
            else:
                own_ref[part, dk_cols] = dk
                own_ref[part, dv_cols] = dv
    gains_ref[0:1, :] = jnp.sum(q_term, axis=0, keepdims=True)
    gains_ref[1:2, :] = jnp.sum(k_term, axis=0, keepdims=True)


def finish_kernel(core_ref, own_ref, r1, r2, r3, r4, kv_ref, tc_ref, ts_ref, kg_ref, mine_ref, other_ref, both):
    core = core_ref[0]
    for b in range(2):
        rows = slice(b * TILE, (b + 1) * TILE)
        total = own_ref[rows, :]
        for r in (r1, r2, r3, r4):
            total = total + r[rows, :].astype(F32)
        for j in range(2):
            cols = slice(j * HD, (j + 1) * HD)
            x = kv_ref[rows, cols].astype(F32)
            dn = rope_back(total[:, cols], tc_ref[rows, :], ts_ref[rows, :])
            both[b, :, cols] = norm_back(dn, x, inv_rms(x), kg_ref[...]).astype(BF)
        both[b, :, 2 * HD :] = total[:, 2 * HD :].astype(BF)
    mine_ref[...] = both[core]
    other_ref[...] = both[1 - core]


def body(q_in, k_in, v_in, grad_out, q_gain, k_gain, shift_plan, segment_ids):
    groups = lax.axis_size("dp")
    chips = lax.axis_size("chip")
    member = lax.axis_index("dp").astype(jnp.int32)
    core = lax.axis_index("core").astype(jnp.int32)
    core1 = core.reshape(1)
    wide = q_in.shape[1] // 2
    sds = jax.ShapeDtypeStruct

    def to_sibling(x):
        return lax.ppermute(x, "core", [(0, 1), (1, 0)])

    def by_core(mine, other, axis):
        return jnp.where(
            core == 0,
            jnp.concatenate([mine, other], axis=axis),
            jnp.concatenate([other, mine], axis=axis),
        )

    packed = pl.pallas_call(
        send_kernel,
        out_shape=sds((2 * groups, RUN, 2560), BF),
        in_specs=[SM, SM, VM, VM, VM],
        out_specs=VM,
        compiler_params=PARAMS,
        name="pack_runs",
    )(shift_plan, member.reshape(1), q_in, k_in, v_in)
    small = jnp.concatenate([shift_plan, segment_ids], axis=1)
    small2 = by_core(small, to_sibling(small), 0)
    g_sib = to_sibling(lax.dynamic_slice_in_dim(grad_out, (1 - core) * wide, wide, 1))
    recv = lax.all_to_all(packed, ("dp", "core"), 0, 0, tiled=True)
    src = 2 * ((member - small2[:, :groups]) % groups) + jnp.arange(2, dtype=jnp.int32)[:, None]
    src = src.reshape(2 * groups)
    segs = small2[:, groups:].reshape(1, 2 * TILE)
    kv0 = pl.pallas_call(
        keys_kernel,
        out_shape=sds((2 * TILE + RUN, 4 * HD), BF),
        grid=(1,),
        in_specs=[SM, pl.BlockSpec((2 * groups, RUN, 4 * HD), lambda i: (0, 0, 4)), VM],
        out_specs=VM,
        compiler_params=PARAMS,
        name="own_keys",
    )(src, recv, segs)
    kv = [lax.ppermute(kv0, "chip", [(i, i + d) for i in range(chips - d)]) for d in range(1, 5)]
    half = jnp.arange(HD // 2, dtype=F32)
    freq = THETA ** (-(half * 2.0 / HD))
    freq = jnp.concatenate([freq, freq]).reshape(1, HD)
    rows2 = 2 * TILE
    res = pl.pallas_call(
        main_kernel,
        out_shape=(
            [sds((TILE, wide), BF)] * 2
            + [sds((rows2, 4 * HD), BF)] * 4
            + [sds((rows2, 4 * HD), F32)]
            + [sds((rows2, HD), F32)] * 2
            + [sds((2, HD), F32)]
        ),
        grid_spec=pltpu.PrefetchScalarGridSpec(
            num_scalar_prefetch=2,
            grid=(1,),
            in_specs=[pl.BlockSpec((2 * groups, RUN, wide), lambda i, c, s: (0, 0, 0))]
            + [VM] * 5
            + [pl.BlockSpec((TILE, wide), lambda i, c, s: (0, c[0]))]
            + [VM] * 4,
            out_specs=[VM] * 10,
            scratch_shapes=[
                pltpu.VMEM((ALLW, HD), F32),
                pltpu.VMEM((ALLW, HD), F32),
                pltpu.VMEM((2, ALLW, HD), BF),
                pltpu.VMEM((2, HD, ALLW), BF),
                pltpu.VMEM((2, ALLW, HD), BF),
                pltpu.VMEM((TILE, wide), BF),
                pltpu.VMEM((8 * TILE, HD), BF),
                pltpu.VMEM((8 * TILE, HD), BF),
                pltpu.VMEM((WIN, TILE), F32),
                pltpu.VMEM((WIN, 2 * TILE), F32),
                pltpu.VMEM((WIN, 2 * TILE), F32),
                pltpu.VMEM((WIN, 8 * TILE), BF),
                pltpu.VMEM((WIN, 8 * TILE), BF),
                pltpu.VMEM((2, ALLW, HD), F32),
                pltpu.VMEM((2, ALLW, HD), F32),
            ],
        ),
        compiler_params=PARAMS,
        name="attention_grads",
    )(
        core1, src, recv, kv[3], kv[2], kv[1], kv[0], kv0, grad_out, g_sib,
        freq, q_gain.reshape(1, HD), k_gain.reshape(1, HD),
    )
    dq_mine, dq_other, parts, own, tco, tso, gains = res[0], res[1], res[2:6], *res[6:]
    back = [
        lax.ppermute(part, "chip", [(i, i - d) for i in range(d, chips)])
        for d, part in zip(range(1, 5), parts)
    ]
    dq_got = to_sibling(dq_other)
    every = 2 * groups * chips
    spread = jnp.broadcast_to(gains.reshape(1, 1, 2 * HD), (every, 1, 2 * HD))
    terms = jnp.sum(lax.all_to_all(spread, ("dp", "chip", "core"), 0, 0, tiled=True), axis=(0, 1))
    mine, other = pl.pallas_call(
        finish_kernel,
        out_shape=[sds((TILE, 4 * HD), BF)] * 2,
        in_specs=[SM] + [VM] * 9,
        out_specs=[VM] * 2,
        scratch_shapes=[pltpu.VMEM((2, TILE, 4 * HD), BF)],
        compiler_params=PARAMS,
        name="finish_keys",
    )(core1, own, *back, kv0, tco, tso, k_gain.reshape(1, HD))
    got = to_sibling(other)
    dq = by_core(dq_mine, dq_got, 1)
    dk = by_core(mine[:, : 2 * HD], got[:, : 2 * HD], 1)
    dv = by_core(mine[:, 2 * HD :], got[:, 2 * HD :], 1)
    return dq, dk, dv, terms[:HD], terms[HD:]


def solution(mesh):
    fine = Mesh(mesh.devices.reshape(mesh.shape["dp"], -1, 2), ("dp", "chip", "core"))
    rows = P(("dp", "chip", "core"), None)
    return jax.shard_map(
        body,
        mesh=fine,
        in_specs=(rows, rows, rows, rows, P(), P(), P(("chip", "core"), None), P("dp", ("chip", "core"))),
        out_specs=(rows, rows, rows, P(), P()),
        check_vma=False,
    )
```

time: 579 us -> 155 us (0.27); the launches traced: 572 us -> 154 us
  blocking collectives: 114 us -> 0 us
  local copies, waits for them, and re-layouts: 125 us -> 13.2 us
  matrix products: 100 us -> 0 us
  loops' own time: 70.6 us -> 0 us
  other arithmetic: 62.6 us -> 2.44 us
  Pallas kernels: 0 us -> 45.7 us
  starting transfers between devices: 7.06 us -> 47.7 us
  waiting for transfers between devices: 78.3 us -> 44.1 us
  between operations: 14.8 us -> 0.81 us
    dot_general x28 -> x0, matrix products: 100 us -> none  [the longest x4 23.6 us: grads_one(): jnp.einsum('ksqt,tkd->ksqd', dscore, key_blk, preferred_element_type=jnp....]
    reduce_scatter x1 -> x0, waiting for transfers between devices: 72.2 us -> none  [body(): lax.psum_scatter(result[1], 'fsdp', scatter_dimension=0, tiled=True)]
    another operation x3 -> x0, loops' own time: 70.6 us -> none  [the longest x1 60.6 us: carried_in(): return lax.fori_loop(0, count - 1, turn, so_far)]
    psum x1 -> x0, blocking collectives: 65 us -> none  [body(): q_total, k_total = lax.psum((q_term, k_term), ('dp', 'fsdp'))]
    dynamic_slice x69 -> x1, local copies, waits for them, and re-layouts: 60.7 us -> 0.84 us  [body(): lax.dynamic_slice_in_dim(grad_out, (1 - core) * wide, wide, 1)]
    pallas_call x0 -> x4, Pallas kernels: none -> 45.7 us  [the longest x1 42.9 us: body(): pl.pallas_call(main_kernel, out_shape=[sds((TILE, wide), BF)] * 2 + [sds(...]
    all_gather x2 -> x0, blocking collectives: 34.6 us -> none  [the longest x1 23 us: body(): lax.all_gather(seg, 'fsdp', axis=0, tiled=True)]
    reduce_sum x13 -> x1, other arithmetic: 26 us -> 0.15 us  [body(): jnp.sum(lax.all_to_all(spread, ('dp', 'chip', 'core'), 0, 0, tiled=True),...]
  transfers between devices with their start and end apart: 5 -> 14, of which waited for: 2 -> 9; matrix products, arithmetic and copies ran while one was open for 14% -> 2% of each run, Pallas kernels for 0% -> 1%
where the time goes in v1:
time: 155 us; the launch traced here: 154 us
  starting transfers between devices  47.7 us (31%)
  Pallas kernels  45.7 us (29%)
  waiting for transfers between devices  44.1 us (28%)
  local copies, waits for them, and re-layouts  13.2 us (9%)
  other arithmetic  2.44 us (2%)
    pallas_call x1, Pallas kernels, body(): pl.pallas_call(main_kernel, out_shape=[sds((TILE, wide), BF)] * 2 + [sds(...  42.9 us
    all_to_all x1, starting transfers between devices, body(): lax.all_to_all(spread, ('dp', 'chip', 'core'), 0, 0, tiled=True)  18.8 us
    ppermute x4, waiting for transfers between devices, body(): lax.ppermute(part, 'chip', [(i, i - d) for i in range(d, chips)])  18.7 us
    all_to_all x1, waiting for transfers between devices, body(): recv = lax.all_to_all(packed, ('dp', 'core'), 0, 0, tiled=True)  18.3 us
    unnamed x36, local copies, waits for them, and re-layouts  10.9 us
    ppermute x4, starting transfers between devices, body(): lax.ppermute(kv0, 'chip', [(i, i + d) for i in range(chips - d)])  10.1 us
    all_to_all x1, starting transfers between devices, body(): recv = lax.all_to_all(packed, ('dp', 'core'), 0, 0, tiled=True)  8.6 us
    ppermute x4, starting transfers between devices, body(): lax.ppermute(part, 'chip', [(i, i - d) for i in range(d, chips)])  7.72 us
  transfers between devices with their start and end apart: 14, of which 9 were waited for; matrix products, arithmetic and copies ran while one was open for 2% of the time, Pallas kernels for 1%

profile of v1, /device:TPU:3, one launch (start us, length us, event | category | flops | bytes accessed | tf_op | source)
XLA Modules:
  0.0 153.9 jit_solution(180837198927411214)
XLA Ops:
  0.6 1.2 copy-done.1
  2.8 0.9 copy-done.7
  4.3 1.7 %pack_runs.1 = bf16[16,16,2560]{2,1,0:T(8,128)(2,1)} custom-call(s32[1,8]{1,0:T(1,128)S(1)} %copy-done.8, s32[1]{0:T(128)} %bitcast.1.who_ref, bf16[128,4096]{1,0:T(8,128)(2,1)S(1)} %copy-done.1, bf16[128,512]{1,0:T(8,128)(2,1)S(1)} %copy-done.6, bf16[128,512]{1,0:T(8,128)(2,1)S(1)} %copy-done.7), custom_call_target="tpu_custom_call" | custom-call | tf_op jit(solution)/shard_map/pack_runs/pallas_call | solution.py:264
  6.0 8.6 %all-to-all-start = ((bf16[16,16,2560]{2,1,0:T(8,128)(2,1)}), bf16[16,16,2560]{2,1,0:T(8,128)(2,1)S(1)}, u32[]{:S(2)}, u32[]{:S(2)}) async-start(bf16[16,16,2560]{2,1,0:T(8,128)(2,1)} %pack_runs.1), calls=%async_computation | async-start | bytes 2621440 | tf_op jit(solution)/shard_map/all_to_all | solution.py:275
  16.4 18.3 %all-to-all-done.recv_ref = bf16[16,16,2560]{2,1,0:T(8,128)(2,1)S(1)} async-done(((bf16[16,16,2560]{2,1,0:T(8,128)(2,1)}), bf16[16,16,2560]{2,1,0:T(8,128)(2,1)S(1)}, u32[]{:S(2)}, u32[]{:S(2)}) %all-to-all-start) | async-done | bytes 1310752 | tf_op jit(solution)/shard_map/all_to_all | solution.py:275
  35.2 2.6 %collective-permute-start.4 = (bf16[272,512]{1,0:T(8,128)(2,1)S(1)}, bf16[272,512]{1,0:T(8,128)(2,1)S(1)}, u32[]{:S(2)}, u32[]{:S(2)}) collective-permute-start(bf16[272,512]{1,0:T(8,128)(2,1)S(1)} %own_keys.1.kv0.kv_ref), channel_id=1, source_target_pairs={{0,2},{2,4},{4,6},{6,8},{8,10},{10,12},{12,14},{1,3},{3,5},{5,7},{... | collective-permute-start | bytes 835592 | tf_op jit(solution)/shard_map/ppermute | solution.py:288
  37.9 3.1 %collective-permute-start.3 = (bf16[272,512]{1,0:T(8,128)(2,1)S(1)}, bf16[272,512]{1,0:T(8,128)(2,1)S(1)}, u32[]{:S(2)}, u32[]{:S(2)}) collective-permute-start(bf16[272,512]{1,0:T(8,128)(2,1)S(1)} %own_keys.1.kv0.kv_ref), channel_id=1, source_target_pairs={{0,4},{2,6},{4,8},{6,10},{8,12},{10,14},{1,5},{3,7},{5,9},{7,11},{... | collective-permute-start | bytes 835592 | tf_op jit(solution)/shard_map/ppermute | solution.py:288
  41.0 3.0 %collective-permute-start.2 = (bf16[272,512]{1,0:T(8,128)(2,1)S(1)}, bf16[272,512]{1,0:T(8,128)(2,1)S(1)}, u32[]{:S(2)}, u32[]{:S(2)}) collective-permute-start(bf16[272,512]{1,0:T(8,128)(2,1)S(1)} %own_keys.1.kv0.kv_ref), channel_id=1, source_target_pairs={{0,6},{2,8},{4,10},{6,12},{8,14},{1,7},{3,9},{5,11},{7,13},{9,15},... | collective-permute-start | bytes 835592 | tf_op jit(solution)/shard_map/ppermute | solution.py:288
  44.0 1.3 collective-permute-start.1
  46.8 5.0 %collective-permute-done.2.kv3 = bf16[272,512]{1,0:T(8,128)(2,1)S(1)} collective-permute-done((bf16[272,512]{1,0:T(8,128)(2,1)S(1)}, bf16[272,512]{1,0:T(8,128)(2,1)S(1)}, u32[]{:S(2)}, u32[]{:S(2)}) %collective-permute-start.2) | collective-permute-done | bytes 278560 | tf_op jit(solution)/shard_map/ppermute | solution.py:288
  51.8 1.0 copy-done.5
  52.8 42.9 %attention_grads.1 = (bf16[128,2048]{1,0:T(8,128)(2,1)S(1)}, bf16[128,2048]{1,0:T(8,128)(2,1)S(1)}, bf16[256,512]{1,0:T(8,128)(2,1)S(1)}, bf16[256,512]{1,0:T(8,...) custom-call(s32[1]{0:T(128)} %bitcast.core_ref, ...), custom_call_target="tpu_custom_call" | custom-call | tf_op jit(solution)/shard_map/attention_grads/pallas_call | solution.py:293
  100.8 18.8 %all-to-all-start.1 = ((f32[128,1,256]{2,1,0:T(1,128)}), f32[128,1,256]{2,1,0:T(1,128)S(1)}, u32[]{:S(2)}, u32[]{:S(2)}) async-start(f32[128,1,256]{2,1,0:T(1,128)} %broadcast_in_dim.9), calls=%async_computation.1 | async-start | bytes 262144 | tf_op jit(solution)/shard_map/all_to_all | solution.py:342
  119.6 3.2 %collective-permute-start.7 = (bf16[256,512]{1,0:T(8,128)(2,1)}, bf16[256,512]{1,0:T(8,128)(2,1)S(1)}, u32[]{:S(2)}, u32[]{:S(2)}) collective-permute-start(bf16[256,512]{1,0:T(8,128)(2,1)} %copy-done.16), channel_id=1, source_target_pairs={{2,0},{4,2},{6,4},{8,6},{10,8},{12,10},{14,12},{3,1},{5,3},{7,5},{... | collective-permute-start | bytes 786440 | tf_op jit(solution)/shard_map/ppermute | solution.py:336
  122.8 1.9 %collective-permute-start.8 = (bf16[256,512]{1,0:T(8,128)(2,1)}, bf16[256,512]{1,0:T(8,128)(2,1)S(1)}, u32[]{:S(2)}, u32[]{:S(2)}) collective-permute-start(bf16[256,512]{1,0:T(8,128)(2,1)} %copy-done.15), channel_id=1, source_target_pairs={{4,0},{6,2},{8,4},{10,6},{12,8},{14,10},{5,1},{7,3},{9,5},{11,7},{... | collective-permute-start | bytes 786440 | tf_op jit(solution)/shard_map/ppermute | solution.py:336
  124.8 1.3 collective-permute-start.9
  126.1 1.3 collective-permute-start.10
  130.2 5.7 %collective-permute-done.8.r2 = bf16[256,512]{1,0:T(8,128)(2,1)S(1)} collective-permute-done((bf16[256,512]{1,0:T(8,128)(2,1)}, bf16[256,512]{1,0:T(8,128)(2,1)S(1)}, u32[]{:S(2)}, u32[]{:S(2)}) %collective-permute-start.8) | collective-permute-done | bytes 262176 | tf_op jit(solution)/shard_map/ppermute | solution.py:336
  135.9 1.7 %collective-permute-done.9.r3 = bf16[256,512]{1,0:T(8,128)(2,1)S(1)} collective-permute-done((bf16[256,512]{1,0:T(8,128)(2,1)}, bf16[256,512]{1,0:T(8,128)(2,1)S(1)}, u32[]{:S(2)}, u32[]{:S(2)}) %collective-permute-start.9) | collective-permute-done | bytes 262176 | tf_op jit(solution)/shard_map/ppermute | solution.py:336
  137.6 10.4 %collective-permute-done.10.r4 = bf16[256,512]{1,0:T(8,128)(2,1)S(1)} collective-permute-done((bf16[256,512]{1,0:T(8,128)(2,1)}, bf16[256,512]{1,0:T(8,128)(2,1)S(1)}, u32[]{:S(2)}, u32[]{:S(2)}) %collective-permute-start.10) | collective-permute-done | bytes 262176 | tf_op jit(solution)/shard_map/ppermute | solution.py:336
  148.1 1.0 copy-done.3
  149.6 1.3 collective-permute-start.11
  150.9 1.0 collective-permute-done.11
  152.7 1.2 maximum_select_fusion
  (59 shorter events, 14.6 us)
Async XLA Ops:
  0.6 1.2 copy-start.1
  1.9 0.9 copy-start.6
  2.8 0.9 copy-start.7
  6.0 8.6 %copy-start.9 = (s32[1,8]{1,0:T(1,128)S(1)}, s32[1,8]{1,0:T(1,128)}, u32[]{:S(2)}) copy-start(s32[1,8]{1,0:T(1,128)} %plan_ref.1) | copy-start | bytes 100
  6.0 8.6 %copy-start.17 = (s32[1,128]{1,0:T(1,128)S(1)}, s32[1,128]{1,0:T(1,128)}, u32[]{:S(2)}) copy-start(s32[1,128]{1,0:T(1,128)} %param.15) | copy-start | bytes 1540
  6.0 8.8 %copy-start = (bf16[128,4096]{1,0:T(8,128)(2,1)S(1)}, bf16[128,4096]{1,0:T(8,128)(2,1)}, u32[]{:S(2)}) copy-start(bf16[128,4096]{1,0:T(8,128)(2,1)} %g_own.1) | copy-start | bytes 3145732
  6.0 28.6 %all-to-all-start = ((bf16[16,16,2560]{2,1,0:T(8,128)(2,1)}), bf16[16,16,2560]{2,1,0:T(8,128)(2,1)S(1)}, u32[]{:S(2)}, u32[]{:S(2)}) async-start(bf16[16,16,2560]{2,1,0:T(8,128)(2,1)} %pack_runs.1), calls=%async_computation | async-start | bytes 2621440 | tf_op jit(solution)/shard_map/all_to_all | solution.py:275
  14.7 1.4 collective-permute-start
  14.9 36.9 %copy-start.10 = (f32[128]{0:T(128)S(1)}, f32[128]{0:T(128)}, u32[]{:S(2)}) copy-start(f32[128]{0:T(128)} %param.13) | copy-start | bytes 1540
  14.9 36.9 %copy-start.11 = (f32[128]{0:T(128)S(1)}, f32[128]{0:T(128)}, u32[]{:S(2)}) copy-start(f32[128]{0:T(128)} %param.12) | copy-start | bytes 1540
  15.7 29.7 %collective-permute-start.5 = (bf16[128,2048]{1,0:T(8,128)(2,1)}, bf16[128,2048]{1,0:T(8,128)(2,1)S(1)}, u32[]{:S(2)}, u32[]{:S(2)}) collective-permute-start(bf16[128,2048]{1,0:T(8,128)(2,1)} %constant_dynamic-slice_fusion), channel_id=1, source_target_pairs={{0,1},{1,0},{2,3},{3,2},{4,5},{5,4},{6,7},{7,6},{8,9},{9,8},{10,11... | collective-permute-start | bytes 1572872 | tf_op jit(solution)/shard_map/ppermute | solution.py:255
  35.2 11.0 %collective-permute-start.4 = (bf16[272,512]{1,0:T(8,128)(2,1)S(1)}, bf16[272,512]{1,0:T(8,128)(2,1)S(1)}, u32[]{:S(2)}, u32[]{:S(2)}) collective-permute-start(bf16[272,512]{1,0:T(8,128)(2,1)S(1)} %own_keys.1.kv0.kv_ref), channel_id=1, source_target_pairs={{0,2},{2,4},{4,6},{6,8},{8,10},{10,12},{12,14},{1,3},{3,5},{5,7},{... | collective-permute-start | bytes 835592 | tf_op jit(solution)/shard_map/ppermute | solution.py:288
  37.9 8.9 %collective-permute-start.3 = (bf16[272,512]{1,0:T(8,128)(2,1)S(1)}, bf16[272,512]{1,0:T(8,128)(2,1)S(1)}, u32[]{:S(2)}, u32[]{:S(2)}) collective-permute-start(bf16[272,512]{1,0:T(8,128)(2,1)S(1)} %own_keys.1.kv0.kv_ref), channel_id=1, source_target_pairs={{0,4},{2,6},{4,8},{6,10},{8,12},{10,14},{1,5},{3,7},{5,9},{7,11},{... | collective-permute-start | bytes 835592 | tf_op jit(solution)/shard_map/ppermute | solution.py:288
  41.0 10.7 %collective-permute-start.2 = (bf16[272,512]{1,0:T(8,128)(2,1)S(1)}, bf16[272,512]{1,0:T(8,128)(2,1)S(1)}, u32[]{:S(2)}, u32[]{:S(2)}) collective-permute-start(bf16[272,512]{1,0:T(8,128)(2,1)S(1)} %own_keys.1.kv0.kv_ref), channel_id=1, source_target_pairs={{0,6},{2,8},{4,10},{6,12},{8,14},{1,7},{3,9},{5,11},{7,13},{9,15},... | collective-permute-start | bytes 835592 | tf_op jit(solution)/shard_map/ppermute | solution.py:288
  44.0 7.7 %collective-permute-start.1 = (bf16[272,512]{1,0:T(8,128)(2,1)S(1)}, bf16[272,512]{1,0:T(8,128)(2,1)S(1)}, u32[]{:S(2)}, u32[]{:S(2)}) collective-permute-start(bf16[272,512]{1,0:T(8,128)(2,1)S(1)} %own_keys.1.kv0.kv_ref), channel_id=1, source_target_pairs={{0,8},{2,10},{4,12},{6,14},{1,9},{3,11},{5,13},{7,15},{16,24},{18,... | collective-permute-start | bytes 835592 | tf_op jit(solution)/shard_map/ppermute | solution.py:288
  51.8 1.0 copy-start.5
  100.8 27.9 %all-to-all-start.1 = ((f32[128,1,256]{2,1,0:T(1,128)}), f32[128,1,256]{2,1,0:T(1,128)S(1)}, u32[]{:S(2)}, u32[]{:S(2)}) async-start(f32[128,1,256]{2,1,0:T(1,128)} %broadcast_in_dim.9), calls=%async_computation.1 | async-start | bytes 262144 | tf_op jit(solution)/shard_map/all_to_all | solution.py:342
  119.6 10.6 %collective-permute-start.7 = (bf16[256,512]{1,0:T(8,128)(2,1)}, bf16[256,512]{1,0:T(8,128)(2,1)S(1)}, u32[]{:S(2)}, u32[]{:S(2)}) collective-permute-start(bf16[256,512]{1,0:T(8,128)(2,1)} %copy-done.16), channel_id=1, source_target_pairs={{2,0},{4,2},{6,4},{8,6},{10,8},{12,10},{14,12},{3,1},{5,3},{7,5},{... | collective-permute-start | bytes 786440 | tf_op jit(solution)/shard_map/ppermute | solution.py:336
  122.8 13.1 %collective-permute-start.8 = (bf16[256,512]{1,0:T(8,128)(2,1)}, bf16[256,512]{1,0:T(8,128)(2,1)S(1)}, u32[]{:S(2)}, u32[]{:S(2)}) collective-permute-start(bf16[256,512]{1,0:T(8,128)(2,1)} %copy-done.15), channel_id=1, source_target_pairs={{4,0},{6,2},{8,4},{10,6},{12,8},{14,10},{5,1},{7,3},{9,5},{11,7},{... | collective-permute-start | bytes 786440 | tf_op jit(solution)/shard_map/ppermute | solution.py:336
  124.8 12.9 %collective-permute-start.9 = (bf16[256,512]{1,0:T(8,128)(2,1)}, bf16[256,512]{1,0:T(8,128)(2,1)S(1)}, u32[]{:S(2)}, u32[]{:S(2)}) collective-permute-start(bf16[256,512]{1,0:T(8,128)(2,1)} %copy-done.14), channel_id=1, source_target_pairs={{6,0},{8,2},{10,4},{12,6},{14,8},{7,1},{9,3},{11,5},{13,7},{15,9},... | collective-permute-start | bytes 786440 | tf_op jit(solution)/shard_map/ppermute | solution.py:336
  126.1 22.0 %collective-permute-start.10 = (bf16[256,512]{1,0:T(8,128)(2,1)}, bf16[256,512]{1,0:T(8,128)(2,1)S(1)}, u32[]{:S(2)}, u32[]{:S(2)}) collective-permute-start(bf16[256,512]{1,0:T(8,128)(2,1)} %copy-done.13), channel_id=1, source_target_pairs={{8,0},{10,2},{12,4},{14,6},{9,1},{11,3},{13,5},{15,7},{24,16},{26,... | collective-permute-start | bytes 786440 | tf_op jit(solution)/shard_map/ppermute | solution.py:336
  127.4 25.4 %collective-permute-start.6 = (bf16[128,2048]{1,0:T(8,128)(2,1)}, bf16[128,2048]{1,0:T(8,128)(2,1)S(1)}, u32[]{:S(2)}, u32[]{:S(2)}) collective-permute-start(bf16[128,2048]{1,0:T(8,128)(2,1)} %copy-done.12), channel_id=1, source_target_pairs={{0,1},{1,0},{2,3},{3,2},{4,5},{5,4},{6,7},{7,6},{8,9},{9,8},{10,11... | collective-permute-start | bytes 1572872 | tf_op jit(solution)/shard_map/ppermute | solution.py:255
  148.1 1.0 copy-start.3
  149.6 2.3 %collective-permute-start.11 = (bf16[128,512]{1,0:T(8,128)(2,1)S(1)}, bf16[128,512]{1,0:T(8,128)(2,1)S(1)}, u32[]{:S(2)}, u32[]{:S(2)}) collective-permute-start(bf16[128,512]{1,0:T(8,128)(2,1)S(1)} %get-tuple-element.27), channel_id=1, source_target_pairs={{0,1},{1,0},{2,3},{3,2},{4,5},{5,4},{6,7},{7,6},{8,9},{9,8},{10,11... | collective-permute-start | bytes 393224 | tf_op jit(solution)/shard_map/ppermute | solution.py:255
  (8 other events, 5.8 us)

commit v2 on v1

v2 whole, which is shorter than its diff:
```python
import math

import jax
import jax.numpy as jnp
from jax import lax
from jax.experimental import pallas as pl
from jax.experimental.pallas import tpu as pltpu
from jax.sharding import Mesh, PartitionSpec as P

THETA = 1000000.0
EPS = 1e-06
NEG = -1e30
HG = 4
HD = 128
RUN = 16
TILE = 128
BACK = 8
WIN = (BACK + 1) * TILE
ALLW = (BACK + 2) * TILE
SCALE = HD**-0.5
TO_EXP2 = SCALE * math.log2(math.e)
BF = jnp.bfloat16
F32 = jnp.float32
SM = pl.BlockSpec(memory_space=pltpu.SMEM)
PARAMS = pltpu.CompilerParams(vmem_limit_bytes=48 * 1024 * 1024)


def whole(*shape):
    return pl.BlockSpec(shape, lambda i, *scalars: (0,) * len(shape))


def sincos(angle):
    turns = jnp.round(angle * (2.0 / math.pi))
    r = ((angle - turns * 1.5703125) - turns * 4.837512969970703e-4) - turns * 7.549789948768648e-8
    r2 = r * r
    sin_r = r + r * r2 * (-1.6666654611e-1 + r2 * (8.3321608736e-3 - 1.9515295891e-4 * r2))
    cos_r = 1.0 - 0.5 * r2 + r2 * r2 * (
        4.166664568298827e-2 + r2 * (-1.388731625493765e-3 + 2.443315711809948e-5 * r2)
    )
    quarter = turns.astype(jnp.int32)
    swap = (quarter & 1) == 1
    s = jnp.where(swap, cos_r, sin_r)
    c = jnp.where(swap, sin_r, cos_r)
    s = jnp.where((quarter & 2) == 2, -s, s)
    c = jnp.where(((quarter + 1) & 2) == 2, -c, c)
    return s, c


def inv_rms(x):
    return lax.rsqrt(jnp.sum(x * x, axis=-1, keepdims=True) * (1.0 / HD) + EPS)


def rope(x, tc, ts):
    return x * tc + pltpu.roll(x, HD // 2, 1) * ts


def rope_back(x, tc, ts):
    return x * tc - pltpu.roll(x, HD // 2, 1) * ts


def norm_back(dn, x, rs, gain):
    w = dn * gain
    return rs * w - x * (rs * rs * rs) * (jnp.sum(w * x, axis=-1, keepdims=True) * (1.0 / HD))


def fold(x, op):
    return op(x.reshape(x.shape[0] // 8, 8, x.shape[1]), axis=0)


def dot(a, b):
    return jnp.dot(a, b, preferred_element_type=F32)


def send_kernel(plan_ref, who_ref, q_ref, k_ref, v_ref, out_ref):
    groups = plan_ref.shape[1]
    wide_q, wide_k = q_ref.shape[1] // 2, k_ref.shape[1] // 2
    for r in range(groups):
        to = lax.rem(who_ref[0] + plan_ref[0, r], groups)
        rows = slice(r * RUN, (r + 1) * RUN)
        for a in range(2):
            out_ref[2 * to + a, :, :wide_q] = q_ref[rows, a * wide_q : (a + 1) * wide_q]
            out_ref[2 * to + a, :, wide_q : wide_q + wide_k] = k_ref[rows, a * wide_k : (a + 1) * wide_k]
            out_ref[2 * to + a, :, wide_q + wide_k :] = v_ref[rows, a * wide_k : (a + 1) * wide_k]


def keys_kernel(src_ref, recv_ref, *out_refs):
    for b in range(2):
        for r in range(8):
            rows = slice(b * TILE + r * RUN, b * TILE + (r + 1) * RUN)
            one = recv_ref[src_ref[b * 8 + r]]
            for j, out_ref in enumerate(out_refs):
                out_ref[rows, :HD] = one[:, j * HD : (j + 1) * HD]
                out_ref[rows, HD:] = one[:, (2 + j) * HD : (3 + j) * HD]


def tables_kernel(core_ref, id4, id3, id2, id1, id0, freq_ref, tc, ts, bias):
    core = core_ref[0]
    lane = lax.broadcasted_iota(jnp.int32, (TILE, TILE), 1)
    sub = lax.broadcasted_iota(jnp.int32, (TILE, TILE), 0)
    subf = sub.astype(F32)
    ids = [jnp.broadcast_to(one[...], (8, 2 * TILE)) for one in (id4, id3, id2, id1, id0)]
    begin = jnp.zeros((8, 2 * TILE), F32)
    for v in range(1, 9):
        less = sum(jnp.where(one < v, 1.0, 0.0) for one in ids)
        begin = begin + jnp.where(ids[-1] == v, jnp.sum(less, axis=1, keepdims=True), 0.0)
    for blk in range(BACK + 2):
        rows = slice(blk * TILE, (blk + 1) * TILE)
        if blk < BACK:
            start = begin[0:1, 0:1]
        else:
            mine = slice((blk - BACK) * TILE, (blk - BACK + 1) * TILE)
            start = jnp.broadcast_to(begin[0:1, mine], (TILE, TILE)).T
        sine, cosine = sincos((subf + float(blk * TILE) - start) * freq_ref[...])
        tc[rows, :] = cosine
        ts[rows, :] = jnp.where(lane < HD // 2, -sine, sine)
    for turn in range(2):
        tile = core if turn == 0 else 1 - core
        st = jnp.where(tile == 0, begin[0:1, :TILE], begin[0:1, TILE:]) - (tile * TILE).astype(F32)
        for kb in range(BACK + 1):
            ok = (subf + float(kb * TILE)) >= st
            if kb == BACK:
                ok = ok & (sub <= lane)
            bias[turn, kb * TILE : (kb + 1) * TILE, :] = jnp.where(ok, 0.0, NEG).astype(BF)


def heads_kernel(
    core_ref, src_ref, recv_ref, kv4, kv3, kv2, kv1, kv0, g_own, g_sib, tc, ts, bias, qg_ref, kg_ref,
    dq_own, dq_sib, out1, out2, out3, out4, own_ref, gains_ref,
    kr, kt, vs, xq, q8s, g8s, sc0, sc1, dp0, dp1, pb0, pb1, db0, db1, dk_acc, dv_acc,
):
    core = core_ref[0]
    kvs = (kv4, kv3, kv2, kv1, kv0)
    lane = lax.broadcasted_iota(jnp.int32, (TILE, TILE), 1)
    sub = lax.broadcasted_iota(jnp.int32, (TILE, TILE), 0)
    eye = jnp.where(sub == lane, 1.0, 0.0).astype(BF)
    qgain, kgain = qg_ref[...], kg_ref[...]
    for blk in range(BACK + 2):
        rows = slice(blk * TILE, (blk + 1) * TILE)
        ref, part = kvs[blk // 2], slice((blk % 2) * TILE, (blk % 2 + 1) * TILE)
        x = ref[part, :HD].astype(F32)
        turned = rope(x * inv_rms(x) * kgain, tc[rows, :], ts[rows, :])
        kr[rows, :] = turned.astype(BF)
        kt[:, rows] = turned.T.astype(BF)
        vs[rows, :] = ref[part, HD:]
    dk_acc[...] = jnp.zeros_like(dk_acc)
    dv_acc[...] = jnp.zeros_like(dv_acc)
    bases, own_rows = [], []
    for turn in range(2):
        tile = core if turn == 0 else 1 - core
        base = pl.multiple_of(tile * TILE, TILE)
        bases.append(base)
        own_rows.append(pl.ds(pl.multiple_of(BACK * TILE + base, TILE), TILE))
        for r in range(8):
            xq[turn, r * RUN : (r + 1) * RUN, :] = recv_ref[src_ref[tile * 8 + r]]
    gs, dqs = (g_own, g_sib), (dq_own, dq_sib)
    scs, dps, pbs, dbs = (sc0, sc1), (dp0, dp1), (pb0, pb1), (db0, db1)
    units = [(turn, h) for turn in range(2) for h in range(0, 8, HG)]

    def front(u):
        turn, h0 = units[u]
        qts, gts = [], []
        for h in range(h0, h0 + HG):
            cols = slice(h * HD, (h + 1) * HD)
            x = xq[turn, :, cols].astype(F32)
            turned = rope(x * inv_rms(x) * qgain, tc[own_rows[turn], :], ts[own_rows[turn], :])
            grad = gs[turn][:, cols]
            q8s[turn, h * TILE : (h + 1) * TILE, :] = turned.astype(BF)
            g8s[turn, h * TILE : (h + 1) * TILE, :] = grad
            qts.append(turned.T.astype(BF))
            gts.append(grad.astype(F32).T.astype(BF))
        qt = jnp.concatenate(
            [jnp.concatenate(qts, axis=1), jnp.concatenate([eye] * HG, axis=1)], axis=0
        )
        win = pl.ds(bases[turn], WIN)
        scs[u % 2][...] = dot(jnp.concatenate([kr[win, :], bias[turn]], axis=1), qt)
        dps[u % 2][...] = dot(vs[win, :], jnp.concatenate(gts, axis=1))

    def middle(u):
        sc, dp, pb, db = scs[u % 2], dps[u % 2], pbs[u % 2], dbs[u % 2]
        for lt in range(HG // 2):
            ls = slice(lt * 2 * TILE, (lt + 1) * 2 * TILE)
            top = jnp.full((8, 2 * TILE), NEG, F32)
            for kb in range(BACK + 1):
                rows = slice(kb * TILE, (kb + 1) * TILE)
                top = jnp.maximum(top, fold(sc[rows, ls], jnp.max))
            top = jnp.max(top, axis=0, keepdims=True) * TO_EXP2
            total = jnp.zeros((8, 2 * TILE), F32)
            inner = jnp.zeros((8, 2 * TILE), F32)
            for kb in range(BACK + 1):
                rows = slice(kb * TILE, (kb + 1) * TILE)
                e = jnp.exp2(sc[rows, ls] * TO_EXP2 - top)
                sc[rows, ls] = e
                total = total + fold(e, jnp.sum)
                inner = inner + fold(e * dp[rows, ls], jnp.sum)
            inv = 1.0 / jnp.sum(total, axis=0, keepdims=True)
            delta = jnp.sum(inner, axis=0, keepdims=True) * inv
            for kb in range(BACK + 1):
                rows = slice(kb * TILE, (kb + 1) * TILE)
                p = sc[rows, ls] * inv
                pb[rows, ls] = p.astype(BF)
                db[rows, ls] = (p * (dp[rows, ls] - delta)).astype(BF)

    def tail(u, q_term):
        turn, h0 = units[u]
        pb, db = pbs[u % 2], dbs[u % 2]
        keys = pl.ds(bases[turn], WIN)
        dqt = dot(kt[:, keys], db[...]) * SCALE
        for i, h in enumerate(range(h0, h0 + HG)):
            cols = slice(h * HD, (h + 1) * HD)
            dn = rope_back(
                dqt[:, i * TILE : (i + 1) * TILE].T, tc[own_rows[turn], :], ts[own_rows[turn], :]
            )
            x = xq[turn, :, cols].astype(F32)
            rs = inv_rms(x)
            q_term = q_term + fold(dn * x * rs, jnp.sum)
            dqs[turn][:, cols] = norm_back(dn, x, rs, qgain).astype(BF)
        mine = slice(h0 * TILE, (h0 + HG) * TILE)
        dv_acc[keys, :] += dot(pb[...], g8s[turn, mine, :])
        dk_acc[keys, :] += dot(db[...], q8s[turn, mine, :])
        return q_term

    q_term = jnp.zeros((8, HD), F32)
    front(0)
    for u in range(len(units)):
        if u + 1 < len(units):
            front(u + 1)
        middle(u)
        q_term = tail(u, q_term)
    k_term = jnp.zeros((8, HD), F32)
    outs = (out4, out3, out2, out1, own_ref)
    for blk in range(BACK + 2):
        rows = slice(blk * TILE, (blk + 1) * TILE)
        part = slice((blk % 2) * TILE, (blk % 2 + 1) * TILE)
        dk = dk_acc[rows, :] * SCALE
        x = kvs[blk // 2][part, :HD].astype(F32)
        dn = rope_back(dk, tc[rows, :], ts[rows, :])
        k_term = k_term + fold(dn * x * inv_rms(x), jnp.sum)
        out = outs[blk // 2]
        out[part, :HD] = dk.astype(out.dtype)
        out[part, HD:] = dv_acc[rows, :].astype(out.dtype)
    gains_ref[0:1, :] = jnp.sum(q_term, axis=0, keepdims=True)
    gains_ref[1:2, :] = jnp.sum(k_term, axis=0, keepdims=True)


def finish_kernel(core_ref, own_ref, r1, r2, r3, r4, kv_ref, tc_ref, ts_ref, kg_ref, mine_ref, other_ref, both):
    core = core_ref[0]
    for b in range(2):
        rows = slice(b * TILE, (b + 1) * TILE)
        total = own_ref[rows, :]
        for r in (r1, r2, r3, r4):
            total = total + r[rows, :].astype(F32)
        x = kv_ref[rows, :HD].astype(F32)
        dn = rope_back(total[:, :HD], tc_ref[rows, :], ts_ref[rows, :])
        both[b, :, :HD] = norm_back(dn, x, inv_rms(x), kg_ref[...]).astype(BF)
        both[b, :, HD:] = total[:, HD:].astype(BF)
    mine_ref[...] = both[core]
    other_ref[...] = both[1 - core]


def head_grads(j, core1, src, recv, kv4, kv3, kv2, kv1, kv0, grad_out, g_sib, tc, ts, bias, q_gain, k_gain):
    sds = jax.ShapeDtypeStruct
    groups, wide = recv.shape[0] // 2, 8 * HD
    rows2 = 2 * TILE
    unit = HG * TILE
    return pl.pallas_call(
        heads_kernel,
        out_shape=(
            [sds((TILE, wide), BF)] * 2
            + [sds((rows2, 2 * HD), BF)] * 4
            + [sds((rows2, 2 * HD), F32), sds((2, HD), F32)]
        ),
        grid_spec=pltpu.PrefetchScalarGridSpec(
            num_scalar_prefetch=2,
            grid=(1,),
            in_specs=[pl.BlockSpec((2 * groups, RUN, wide), lambda i, c, s: (0, 0, j))]
            + [whole(rows2, 2 * HD)] * 5
            + [pl.BlockSpec((TILE, wide), lambda i, c, s: (0, 2 * c[0] + j))]
            + [pl.BlockSpec((TILE, wide), lambda i, c, s: (0, j))]
            + [whole(ALLW, HD)] * 2
            + [whole(2, WIN, TILE)]
            + [whole(1, HD)] * 2,
            out_specs=[whole(TILE, wide)] * 2 + [whole(rows2, 2 * HD)] * 5 + [whole(2, HD)],
            scratch_shapes=[
                pltpu.VMEM((ALLW, HD), BF),
                pltpu.VMEM((HD, ALLW), BF),
                pltpu.VMEM((ALLW, HD), BF),
                pltpu.VMEM((2, TILE, wide), BF),
                pltpu.VMEM((2, wide, HD), BF),
                pltpu.VMEM((2, wide, HD), BF),
            ]
            + [pltpu.VMEM((WIN, unit), F32)] * 4
            + [pltpu.VMEM((WIN, unit), BF)] * 4
            + [pltpu.VMEM((ALLW, HD), F32)] * 2,
        ),
        compiler_params=PARAMS,
        cost_estimate=pl.CostEstimate(flops=3 * 10**9, bytes_accessed=6 * 10**6, transcendentals=3 * 10**6),
        name="head_grads",
    )(
        core1, src, recv, kv4, kv3, kv2, kv1, kv0, grad_out, g_sib, tc, ts, bias,
        q_gain.reshape(1, HD), k_gain.reshape(1, HD),
    )


def body(q_in, k_in, v_in, grad_out, q_gain, k_gain, shift_plan, segment_ids):
    groups = lax.axis_size("dp")
    chips = lax.axis_size("chip")
    member = lax.axis_index("dp").astype(jnp.int32)
    core = lax.axis_index("core").astype(jnp.int32)
    core1 = core.reshape(1)
    wide = q_in.shape[1] // 2
    rows2 = 2 * TILE
    sds = jax.ShapeDtypeStruct

    def to_sibling(x):
        return lax.ppermute(x, "core", [(0, 1), (1, 0)])

    def ahead(x, d):
        return lax.ppermute(x, "chip", [(i, i + d) for i in range(chips - d)])

    def behind(x, d):
        return lax.ppermute(x, "chip", [(i, i - d) for i in range(d, chips)])

    def by_core(mine, other, axis):
        return jnp.where(
            core == 0,
            jnp.concatenate([mine, other], axis=axis),
            jnp.concatenate([other, mine], axis=axis),
        )

    packed = pl.pallas_call(
        send_kernel,
        out_shape=sds((2 * groups, RUN, 2560), BF),
        grid=(1,),
        in_specs=[SM, SM, whole(*q_in.shape), whole(*k_in.shape), whole(*v_in.shape)],
        out_specs=whole(2 * groups, RUN, 2560),
        compiler_params=PARAMS,
        name="pack_runs",
    )(shift_plan, member.reshape(1), q_in, k_in, v_in)
    recv = lax.all_to_all(packed, ("dp", "core"), 0, 0, tiled=True)
    small = jnp.concatenate([shift_plan, segment_ids + 1], axis=1)
    small2 = by_core(small, to_sibling(small), 0)
    src = 2 * ((member - small2[:, :groups]) % groups) + jnp.arange(2, dtype=jnp.int32)[:, None]
    src = src.reshape(2 * groups)
    ids = small2[:, groups:].reshape(1, rows2)
    id_win = [ahead(ids, d) for d in range(1, 5)]
    half = jnp.arange(HD // 2, dtype=F32)
    freq = THETA ** (-(half * 2.0 / HD))
    freq = jnp.concatenate([freq, freq]).reshape(1, HD)
    tc, ts, bias = pl.pallas_call(
        tables_kernel,
        out_shape=[sds((ALLW, HD), F32), sds((ALLW, HD), F32), sds((2, WIN, TILE), BF)],
        grid=(1,),
        in_specs=[SM] + [whole(1, rows2)] * 5 + [whole(1, HD)],
        out_specs=[whole(ALLW, HD)] * 2 + [whole(2, WIN, TILE)],
        compiler_params=PARAMS,
        name="rope_tables",
    )(core1, *id_win[::-1], ids, freq)
    g_sib = to_sibling(lax.dynamic_slice_in_dim(grad_out, (1 - core) * wide, wide, 1))
    kv0 = pl.pallas_call(
        keys_kernel,
        out_shape=[sds((rows2, 2 * HD), BF)] * 2,
        grid=(1,),
        in_specs=[SM, pl.BlockSpec((2 * groups, RUN, 4 * HD), lambda i: (0, 0, 4))],
        out_specs=[whole(rows2, 2 * HD)] * 2,
        compiler_params=PARAMS,
        name="own_keys",
    )(src, recv)
    kv = [[ahead(kv0[j], d) for d in range(1, 5)] for j in range(2)]
    dq_mine, dq_got, gains, done = [], [], 0.0, []
    for j in range(2):
        mine, other, *parts, own, gain = head_grads(
            j, core1, src, recv, *kv[j][::-1], kv0[j], grad_out, g_sib, tc, ts, bias, q_gain, k_gain
        )
        back = [behind(part, d) for d, part in zip(range(1, 5), parts)]
        dq_mine.append(mine)
        dq_got.append(to_sibling(other))
        gains = gains + gain
        done.append((own, back))
    gains, dq_got[1] = lax.optimization_barrier((gains, dq_got[1]))
    every = 2 * groups * chips
    spread = jnp.broadcast_to(gains.reshape(1, 1, 2 * HD), (every, 1, 2 * HD))
    terms = jnp.sum(lax.all_to_all(spread, ("dp", "chip", "core"), 0, 0, tiled=True), axis=(0, 1))
    mine, got = [], []
    for j, (own, back) in enumerate(done):
        if j == 1:
            terms, own = lax.optimization_barrier((terms, own))
        a, b = pl.pallas_call(
            finish_kernel,
            out_shape=[sds((TILE, 2 * HD), BF)] * 2,
            grid=(1,),
            in_specs=[SM]
            + [whole(rows2, 2 * HD)] * 6
            + [pl.BlockSpec((rows2, HD), lambda i: (BACK // 2, 0))] * 2
            + [whole(1, HD)],
            out_specs=[whole(TILE, 2 * HD)] * 2,
            scratch_shapes=[pltpu.VMEM((2, TILE, 2 * HD), BF)],
            compiler_params=PARAMS,
            name="finish_keys",
        )(core1, own, *back, kv0[j], tc, ts, k_gain.reshape(1, HD))
        mine.append(a)
        got.append(to_sibling(b))

    def joined(part):
        return by_core(
            jnp.concatenate([part(one) for one in mine], axis=1),
            jnp.concatenate([part(one) for one in got], axis=1),
            1,
        )

    dq = by_core(jnp.concatenate(dq_mine, axis=1), jnp.concatenate(dq_got, axis=1), 1)
    dk = joined(lambda one: one[:, :HD])
    dv = joined(lambda one: one[:, HD:])
    return dq, dk, dv, terms[:HD], terms[HD:]


def solution(mesh):
    fine = Mesh(mesh.devices.reshape(mesh.shape["dp"], -1, 2), ("dp", "chip", "core"))
    rows = P(("dp", "chip", "core"), None)
    return jax.shard_map(
        body,
        mesh=fine,
        in_specs=(rows, rows, rows, rows, P(), P(), P(("chip", "core"), None), P("dp", ("chip", "core"))),
        out_specs=(rows, rows, rows, P(), P()),
        check_vma=False,
    )
```

time: 155 us -> 124 us (0.80)
  the two profiles are of different devices: /device:TPU:3 before, /device:TPU:1 now
where the time goes in v2:
time: 124 us
  starting transfers between devices  67.7 us (55%)
  Pallas kernels  27.9 us (22%)
  waiting for transfers between devices  16.1 us (13%)
  local copies, waits for them, and re-layouts  7.17 us (6%)
  other arithmetic  3.44 us (3%)
    ppermute x12, starting transfers between devices, ahead(): return lax.ppermute(x, 'chip', [(i, i + d) for i in range(chips - d)])  30.7 us
    pallas_call x2, Pallas kernels, head_grads(): pl.pallas_call(heads_kernel, out_shape=[sds((TILE, wide), BF)] * 2 + [sds...  23.7 us
    all_to_all x1, starting transfers between devices, body(): lax.all_to_all(spread, ('dp', 'chip', 'core'), 0, 0, tiled=True)  13.5 us
    ppermute x8, starting transfers between devices, behind(): return lax.ppermute(x, 'chip', [(i, i - d) for i in range(d, chips)])  10.5 us
    all_to_all x1, starting transfers between devices, body(): recv = lax.all_to_all(packed, ('dp', 'core'), 0, 0, tiled=True)  9.43 us
    all_to_all x1, waiting for transfers between devices, body(): lax.all_to_all(spread, ('dp', 'chip', 'core'), 0, 0, tiled=True)  7.95 us
    all_to_all x1, waiting for transfers between devices, body(): recv = lax.all_to_all(packed, ('dp', 'core'), 0, 0, tiled=True)  6.8 us
    unnamed x24, local copies, waits for them, and re-layouts  4.93 us
  transfers between devices with their start and end apart: 28, of which 4 were waited for; matrix products, arithmetic and copies ran while one was open for 4% of the time, Pallas kernels for 21%

profile of v2, /device:TPU:1, one launch (start us, length us, event | category | flops | bytes accessed | tf_op | source)
XLA Modules:
  0.0 123.5 jit_solution(4699619461315741983)
XLA Ops:
  4.3 1.7 %pack_runs.1 = bf16[16,16,2560]{2,1,0:T(8,128)(2,1)} custom-call(s32[1,8]{1,0:T(1,128)S(1)} %copy-done.7, s32[1]{0:T(128)} %bitcast.1.who_ref, bf16[128,4096]{1,0:T(8,128)(2,1)S(1)} %copy-done.1, bf16[128,512]{1,0:T(8,128)(2,1)S(1)} %copy-done.5, bf16[128,512]{1,0:T(8,128)(2,1)S(1)} %copy-done.6), custom_call_target="tpu_custom_call" | custom-call | tf_op jit(solution)/shard_map/pack_runs/pallas_call | solution.py:330
  6.1 9.4 %all-to-all-start = ((bf16[16,16,2560]{2,1,0:T(8,128)(2,1)}), bf16[16,16,2560]{2,1,0:T(8,128)(2,1)S(1)}, u32[]{:S(2)}, u32[]{:S(2)}) async-start(bf16[16,16,2560]{2,1,0:T(8,128)(2,1)} %pack_runs.1), calls=%async_computation | async-start | bytes 2621440 | tf_op jit(solution)/shard_map/all_to_all | solution.py:339
  17.1 4.7 %collective-permute-start.6 = (s32[1,256]{1,0:T(1,128)S(1)}, s32[1,256]{1,0:T(1,128)S(1)}, u32[]{:S(2)}, u32[]{:S(2)}) collective-permute-start(s32[1,256]{1,0:T(1,128)S(1)} %bitcast.8), channel_id=1, source_target_pairs={{0,8},{2,10},{4,12},{6,14},{1,9},{3,11},{5,13},{7,15},{16,24},{18,... | collective-permute-start | bytes 3080 | tf_op jit(solution)/shard_map/ppermute | solution.py:318
  21.8 2.7 %collective-permute-start.7 = (s32[1,256]{1,0:T(1,128)S(1)}, s32[1,256]{1,0:T(1,128)S(1)}, u32[]{:S(2)}, u32[]{:S(2)}) collective-permute-start(s32[1,256]{1,0:T(1,128)S(1)} %bitcast.9), channel_id=1, source_target_pairs={{0,6},{2,8},{4,10},{6,12},{8,14},{1,7},{3,9},{5,11},{7,13},{9,15},... | collective-permute-start | bytes 3080 | tf_op jit(solution)/shard_map/ppermute | solution.py:318
  25.8 2.8 %collective-permute-start.9 = (s32[1,256]{1,0:T(1,128)S(1)}, s32[1,256]{1,0:T(1,128)S(1)}, u32[]{:S(2)}, u32[]{:S(2)}) collective-permute-start(s32[1,256]{1,0:T(1,128)S(1)} %bitcast.11), channel_id=1, source_target_pairs={{0,2},{2,4},{4,6},{6,8},{8,10},{10,12},{12,14},{1,3},{3,5},{5,7},{... | collective-permute-start | bytes 3080 | tf_op jit(solution)/shard_map/ppermute | solution.py:318
  28.7 6.8 %all-to-all-done.recv_ref = bf16[16,16,2560]{2,1,0:T(8,128)(2,1)S(1)} async-done(((bf16[16,16,2560]{2,1,0:T(8,128)(2,1)}), bf16[16,16,2560]{2,1,0:T(8,128)(2,1)S(1)}, u32[]{:S(2)}, u32[]{:S(2)}) %all-to-all-start) | async-done | bytes 1310752 | tf_op jit(solution)/shard_map/all_to_all | solution.py:339
  36.1 4.7 %collective-permute-start.1 = (bf16[256,256]{1,0:T(8,128)(2,1)S(1)}, bf16[256,256]{1,0:T(8,128)(2,1)S(1)}, u32[]{:S(2)}, u32[]{:S(2)}) collective-permute-start(bf16[256,256]{1,0:T(8,128)(2,1)S(1)} %get-tuple-element.34.kv0.kv_ref), channel_id=1, source_target_pairs={{0,8},{2,10},{4,12},{6,14},{1,9},{3,11},{5,13},{7,15},{16,24},{18,... | collective-permute-start | bytes 393224 | tf_op jit(solution)/shard_map/ppermute | solution.py:318
  40.8 2.7 %collective-permute-start.2 = (bf16[256,256]{1,0:T(8,128)(2,1)S(1)}, bf16[256,256]{1,0:T(8,128)(2,1)S(1)}, u32[]{:S(2)}, u32[]{:S(2)}) collective-permute-start(bf16[256,256]{1,0:T(8,128)(2,1)S(1)} %get-tuple-element.34.kv0.kv_ref), channel_id=1, source_target_pairs={{0,6},{2,8},{4,10},{6,12},{8,14},{1,7},{3,9},{5,11},{7,13},{9,15},... | collective-permute-start | bytes 393224 | tf_op jit(solution)/shard_map/ppermute | solution.py:318
  43.5 1.3 %collective-permute-start.3 = (bf16[256,256]{1,0:T(8,128)(2,1)S(1)}, bf16[256,256]{1,0:T(8,128)(2,1)S(1)}, u32[]{:S(2)}, u32[]{:S(2)}) collective-permute-start(bf16[256,256]{1,0:T(8,128)(2,1)S(1)} %get-tuple-element.34.kv0.kv_ref), channel_id=1, source_target_pairs={{0,4},{2,6},{4,8},{6,10},{8,12},{10,14},{1,5},{3,7},{5,9},{7,11},{... | collective-permute-start | bytes 393224 | tf_op jit(solution)/shard_map/ppermute | solution.py:318
  44.8 2.8 %collective-permute-start.4 = (bf16[256,256]{1,0:T(8,128)(2,1)S(1)}, bf16[256,256]{1,0:T(8,128)(2,1)S(1)}, u32[]{:S(2)}, u32[]{:S(2)}) collective-permute-start(bf16[256,256]{1,0:T(8,128)(2,1)S(1)} %get-tuple-element.34.kv0.kv_ref), channel_id=1, source_target_pairs={{0,2},{2,4},{4,6},{6,8},{8,10},{10,12},{12,14},{1,3},{3,5},{5,7},{... | collective-permute-start | bytes 393224 | tf_op jit(solution)/shard_map/ppermute | solution.py:318
  47.7 1.4 %rope_tables.1 = (f32[1280,128]{1,0:T(8,128)S(1)}, f32[1280,128]{1,0:T(8,128)S(1)}, bf16[2,1152,128]{2,1,0:T(8,128)(2,1)S(1)}) custom-call(s32[1]{0:T(128)} %bitcast.core_ref, s32[1,256]{1,0:T(1,128)S(1)} %collective-permute-done.6.id4, s32[1,256]{1,0:T(1,128)S(1)} %collective-permute-done.7.id3, s32[1,256]{1,0:T(1,128)S(1)} %collective-permute-done.8.id2, ...), custom_call_target="tpu_custom_call" | custom-call | tf_op jit(solution)/shard_map/rope_tables/pallas_call | solution.py:349
  49.1 1.6 %collective-permute-start.10 = (bf16[256,256]{1,0:T(8,128)(2,1)S(1)}, bf16[256,256]{1,0:T(8,128)(2,1)S(1)}, u32[]{:S(2)}, u32[]{:S(2)}) collective-permute-start(bf16[256,256]{1,0:T(8,128)(2,1)S(1)} %get-tuple-element.39.kv0.kv_ref), channel_id=1, source_target_pairs={{0,8},{2,10},{4,12},{6,14},{1,9},{3,11},{5,13},{7,15},{16,24},{18,... | collective-permute-start | bytes 393224 | tf_op jit(solution)/shard_map/ppermute | solution.py:318
  50.8 1.9 %collective-permute-start.11 = (bf16[256,256]{1,0:T(8,128)(2,1)S(1)}, bf16[256,256]{1,0:T(8,128)(2,1)S(1)}, u32[]{:S(2)}, u32[]{:S(2)}) collective-permute-start(bf16[256,256]{1,0:T(8,128)(2,1)S(1)} %get-tuple-element.39.kv0.kv_ref), channel_id=1, source_target_pairs={{0,6},{2,8},{4,10},{6,12},{8,14},{1,7},{3,9},{5,11},{7,13},{9,15},... | collective-permute-start | bytes 393224 | tf_op jit(solution)/shard_map/ppermute | solution.py:318
  52.6 1.3 %collective-permute-start.12 = (bf16[256,256]{1,0:T(8,128)(2,1)S(1)}, bf16[256,256]{1,0:T(8,128)(2,1)S(1)}, u32[]{:S(2)}, u32[]{:S(2)}) collective-permute-start(bf16[256,256]{1,0:T(8,128)(2,1)S(1)} %get-tuple-element.39.kv0.kv_ref), channel_id=1, source_target_pairs={{0,4},{2,6},{4,8},{6,10},{8,12},{10,14},{1,5},{3,7},{5,9},{7,11},{... | collective-permute-start | bytes 393224 | tf_op jit(solution)/shard_map/ppermute | solution.py:318
  53.9 3.0 %collective-permute-start.13 = (bf16[256,256]{1,0:T(8,128)(2,1)S(1)}, bf16[256,256]{1,0:T(8,128)(2,1)S(1)}, u32[]{:S(2)}, u32[]{:S(2)}) collective-permute-start(bf16[256,256]{1,0:T(8,128)(2,1)S(1)} %get-tuple-element.39.kv0.kv_ref), channel_id=1, source_target_pairs={{0,2},{2,4},{4,6},{6,8},{8,10},{10,12},{12,14},{1,3},{3,5},{5,7},{... | collective-permute-start | bytes 393224 | tf_op jit(solution)/shard_map/ppermute | solution.py:318
  58.2 11.8 %head_grads.2 = (bf16[128,1024]{1,0:T(8,128)(2,1)S(1)}, bf16[128,1024]{1,0:T(8,128)(2,1)}, bf16[256,256]{1,0:T(8,128)(2,1)S(1)}, bf16[256,256]{1,0:T(8,128)(2,1)...) custom-call(s32[1]{0:T(128)} %bitcast.core_ref, ...), custom_call_target="tpu_custom_call" | custom-call | flops 3000000000 | bytes 6000000 | tf_op jit(solution)/shard_map/head_grads/pallas_call | solution.py:265
  74.0 1.5 %collective-permute-start.19 = (bf16[256,256]{1,0:T(8,128)(2,1)S(1)}, bf16[256,256]{1,0:T(8,128)(2,1)S(1)}, u32[]{:S(2)}, u32[]{:S(2)}) collective-permute-start(bf16[256,256]{1,0:T(8,128)(2,1)S(1)} %get-tuple-element.50), channel_id=1, source_target_pairs={{8,0},{10,2},{12,4},{14,6},{9,1},{11,3},{13,5},{15,7},{24,16},{26,... | collective-permute-start | bytes 393224 | tf_op jit(solution)/shard_map/ppermute | solution.py:321
  75.5 11.9 %head_grads.3 = (bf16[128,1024]{1,0:T(8,128)(2,1)S(1)}, bf16[128,1024]{1,0:T(8,128)(2,1)S(1)}, bf16[256,256]{1,0:T(8,128)(2,1)}, bf16[256,256]{1,0:T(8,128)(2,1)...) custom-call(s32[1]{0:T(128)} %bitcast.core_ref, ...), custom_call_target="tpu_custom_call" | custom-call | flops 3000000000 | bytes 6000000 | tf_op jit(solution)/shard_map/head_grads/pallas_call | solution.py:265
  87.4 2.0 %collective-permute-start.15 = (bf16[128,1024]{1,0:T(8,128)(2,1)S(1)}, bf16[128,1024]{1,0:T(8,128)(2,1)S(1)}, u32[]{:S(2)}, u32[]{:S(2)}) collective-permute-start(bf16[128,1024]{1,0:T(8,128)(2,1)S(1)} %get-tuple-element.44), channel_id=1, source_target_pairs={{0,1},{1,0},{2,3},{3,2},{4,5},{5,4},{6,7},{7,6},{8,9},{9,8},{10,11... | collective-permute-start | bytes 786440 | tf_op jit(solution)/shard_map/ppermute | solution.py:315
  90.7 1.3 %collective-permute-start.21 = (bf16[256,256]{1,0:T(8,128)(2,1)}, bf16[256,256]{1,0:T(8,128)(2,1)S(1)}, u32[]{:S(2)}, u32[]{:S(2)}) collective-permute-start(bf16[256,256]{1,0:T(8,128)(2,1)} %get-tuple-element.56), channel_id=1, source_target_pairs={{4,0},{6,2},{8,4},{10,6},{12,8},{14,10},{5,1},{7,3},{9,5},{11,7},{... | collective-permute-start | bytes 393224 | tf_op jit(solution)/shard_map/ppermute | solution.py:321
  95.2 1.3 %collective-permute-start.23 = (bf16[256,256]{1,0:T(8,128)(2,1)S(1)}, bf16[256,256]{1,0:T(8,128)(2,1)S(1)}, u32[]{:S(2)}, u32[]{:S(2)}) collective-permute-start(bf16[256,256]{1,0:T(8,128)(2,1)S(1)} %get-tuple-element.58), channel_id=1, source_target_pairs={{8,0},{10,2},{12,4},{14,6},{9,1},{11,3},{13,5},{15,7},{24,16},{26,... | collective-permute-start | bytes 393224 | tf_op jit(solution)/shard_map/ppermute | solution.py:321
  97.2 13.5 %all-to-all-start.1 = ((f32[128,1,256]{2,1,0:T(1,128)}), f32[128,1,256]{2,1,0:T(1,128)S(1)}, u32[]{:S(2)}, u32[]{:S(2)}) async-start(f32[128,1,256]{2,1,0:T(1,128)} %broadcast_in_dim.9), calls=%async_computation.1 | async-start | bytes 262144 | tf_op jit(solution)/shard_map/all_to_all | solution.py:382
  110.7 2.3 %maximum_select_fusion = bf16[128,4096]{1,0:T(8,128)(2,1)} fusion(bf16[128,1024]{1,0:T(8,128)(2,1)S(1)} %collective-permute-done.15, bf16[128,1024]{1,0:T(8,128)(2,1)} %collective-permute-done.14, bf16[128,1024]{1,0:T(8,128)(2,1)S(1)} %get-tuple-element.40, bf16[128,1024]{1,0:T(8,128)(2,1)S(1)} %get-tuple-element.38, pred[]{:T(512)S(6)} %eq.4), kind=kLoop, calls=%fused_computation | loop fusion | flops 8912896 | bytes 2097153 | tf_op jit(solution)/shard_map/jit(_where)/select_n | solution.py:324
  112.9 8.0 %all-to-all-done.1 = f32[128,1,256]{2,1,0:T(1,128)S(1)} async-done(((f32[128,1,256]{2,1,0:T(1,128)}), f32[128,1,256]{2,1,0:T(1,128)S(1)}, u32[]{:S(2)}, u32[]{:S(2)}) %all-to-all-start.1) | async-done | bytes 131104 | tf_op jit(solution)/shard_map/all_to_all | solution.py:382
  (82 shorter events, 20.2 us)
Async XLA Ops:
  6.1 29.4 %all-to-all-start = ((bf16[16,16,2560]{2,1,0:T(8,128)(2,1)}), bf16[16,16,2560]{2,1,0:T(8,128)(2,1)S(1)}, u32[]{:S(2)}, u32[]{:S(2)}) async-start(bf16[16,16,2560]{2,1,0:T(8,128)(2,1)} %pack_runs.1), calls=%async_computation | async-start | bytes 2621440 | tf_op jit(solution)/shard_map/all_to_all | solution.py:339
  16.6 32.5 %collective-permute-start.5 = (bf16[128,2048]{1,0:T(8,128)(2,1)}, bf16[128,2048]{1,0:T(8,128)(2,1)S(1)}, u32[]{:S(2)}, u32[]{:S(2)}) collective-permute-start(bf16[128,2048]{1,0:T(8,128)(2,1)} %constant_dynamic-slice_fusion), channel_id=1, source_target_pairs={{0,1},{1,0},{2,3},{3,2},{4,5},{5,4},{6,7},{7,6},{8,9},{9,8},{10,11... | collective-permute-start | bytes 1572872 | tf_op jit(solution)/shard_map/ppermute | solution.py:315
  17.1 19.0 %collective-permute-start.6 = (s32[1,256]{1,0:T(1,128)S(1)}, s32[1,256]{1,0:T(1,128)S(1)}, u32[]{:S(2)}, u32[]{:S(2)}) collective-permute-start(s32[1,256]{1,0:T(1,128)S(1)} %bitcast.8), channel_id=1, source_target_pairs={{0,8},{2,10},{4,12},{6,14},{1,9},{3,11},{5,13},{7,15},{16,24},{18,... | collective-permute-start | bytes 3080 | tf_op jit(solution)/shard_map/ppermute | solution.py:318
  21.8 19.0 %collective-permute-start.7 = (s32[1,256]{1,0:T(1,128)S(1)}, s32[1,256]{1,0:T(1,128)S(1)}, u32[]{:S(2)}, u32[]{:S(2)}) collective-permute-start(s32[1,256]{1,0:T(1,128)S(1)} %bitcast.9), channel_id=1, source_target_pairs={{0,6},{2,8},{4,10},{6,12},{8,14},{1,7},{3,9},{5,11},{7,13},{9,15},... | collective-permute-start | bytes 3080 | tf_op jit(solution)/shard_map/ppermute | solution.py:318
  24.5 19.0 %collective-permute-start.8 = (s32[1,256]{1,0:T(1,128)S(1)}, s32[1,256]{1,0:T(1,128)S(1)}, u32[]{:S(2)}, u32[]{:S(2)}) collective-permute-start(s32[1,256]{1,0:T(1,128)S(1)} %bitcast.10), channel_id=1, source_target_pairs={{0,4},{2,6},{4,8},{6,10},{8,12},{10,14},{1,5},{3,7},{5,9},{7,11},{... | collective-permute-start | bytes 3080 | tf_op jit(solution)/shard_map/ppermute | solution.py:318
  25.8 19.0 %collective-permute-start.9 = (s32[1,256]{1,0:T(1,128)S(1)}, s32[1,256]{1,0:T(1,128)S(1)}, u32[]{:S(2)}, u32[]{:S(2)}) collective-permute-start(s32[1,256]{1,0:T(1,128)S(1)} %bitcast.11), channel_id=1, source_target_pairs={{0,2},{2,4},{4,6},{6,8},{8,10},{10,12},{12,14},{1,3},{3,5},{5,7},{... | collective-permute-start | bytes 3080 | tf_op jit(solution)/shard_map/ppermute | solution.py:318
  36.1 14.6 %collective-permute-start.1 = (bf16[256,256]{1,0:T(8,128)(2,1)S(1)}, bf16[256,256]{1,0:T(8,128)(2,1)S(1)}, u32[]{:S(2)}, u32[]{:S(2)}) collective-permute-start(bf16[256,256]{1,0:T(8,128)(2,1)S(1)} %get-tuple-element.34.kv0.kv_ref), channel_id=1, source_target_pairs={{0,8},{2,10},{4,12},{6,14},{1,9},{3,11},{5,13},{7,15},{16,24},{18,... | collective-permute-start | bytes 393224 | tf_op jit(solution)/shard_map/ppermute | solution.py:318
  40.8 11.8 %collective-permute-start.2 = (bf16[256,256]{1,0:T(8,128)(2,1)S(1)}, bf16[256,256]{1,0:T(8,128)(2,1)S(1)}, u32[]{:S(2)}, u32[]{:S(2)}) collective-permute-start(bf16[256,256]{1,0:T(8,128)(2,1)S(1)} %get-tuple-element.34.kv0.kv_ref), channel_id=1, source_target_pairs={{0,6},{2,8},{4,10},{6,12},{8,14},{1,7},{3,9},{5,11},{7,13},{9,15},... | collective-permute-start | bytes 393224 | tf_op jit(solution)/shard_map/ppermute | solution.py:318
  43.5 10.5 %collective-permute-start.3 = (bf16[256,256]{1,0:T(8,128)(2,1)S(1)}, bf16[256,256]{1,0:T(8,128)(2,1)S(1)}, u32[]{:S(2)}, u32[]{:S(2)}) collective-permute-start(bf16[256,256]{1,0:T(8,128)(2,1)S(1)} %get-tuple-element.34.kv0.kv_ref), channel_id=1, source_target_pairs={{0,4},{2,6},{4,8},{6,10},{8,12},{10,14},{1,5},{3,7},{5,9},{7,11},{... | collective-permute-start | bytes 393224 | tf_op jit(solution)/shard_map/ppermute | solution.py:318
  44.8 12.2 %collective-permute-start.4 = (bf16[256,256]{1,0:T(8,128)(2,1)S(1)}, bf16[256,256]{1,0:T(8,128)(2,1)S(1)}, u32[]{:S(2)}, u32[]{:S(2)}) collective-permute-start(bf16[256,256]{1,0:T(8,128)(2,1)S(1)} %get-tuple-element.34.kv0.kv_ref), channel_id=1, source_target_pairs={{0,2},{2,4},{4,6},{6,8},{8,10},{10,12},{12,14},{1,3},{3,5},{5,7},{... | collective-permute-start | bytes 393224 | tf_op jit(solution)/shard_map/ppermute | solution.py:318
  49.1 22.2 %collective-permute-start.10 = (bf16[256,256]{1,0:T(8,128)(2,1)S(1)}, bf16[256,256]{1,0:T(8,128)(2,1)S(1)}, u32[]{:S(2)}, u32[]{:S(2)}) collective-permute-start(bf16[256,256]{1,0:T(8,128)(2,1)S(1)} %get-tuple-element.39.kv0.kv_ref), channel_id=1, source_target_pairs={{0,8},{2,10},{4,12},{6,14},{1,9},{3,11},{5,13},{7,15},{16,24},{18,... | collective-permute-start | bytes 393224 | tf_op jit(solution)/shard_map/ppermute | solution.py:318
  50.8 21.9 %collective-permute-start.11 = (bf16[256,256]{1,0:T(8,128)(2,1)S(1)}, bf16[256,256]{1,0:T(8,128)(2,1)S(1)}, u32[]{:S(2)}, u32[]{:S(2)}) collective-permute-start(bf16[256,256]{1,0:T(8,128)(2,1)S(1)} %get-tuple-element.39.kv0.kv_ref), channel_id=1, source_target_pairs={{0,6},{2,8},{4,10},{6,12},{8,14},{1,7},{3,9},{5,11},{7,13},{9,15},... | collective-permute-start | bytes 393224 | tf_op jit(solution)/shard_map/ppermute | solution.py:318
  52.6 21.3 %collective-permute-start.12 = (bf16[256,256]{1,0:T(8,128)(2,1)S(1)}, bf16[256,256]{1,0:T(8,128)(2,1)S(1)}, u32[]{:S(2)}, u32[]{:S(2)}) collective-permute-start(bf16[256,256]{1,0:T(8,128)(2,1)S(1)} %get-tuple-element.39.kv0.kv_ref), channel_id=1, source_target_pairs={{0,4},{2,6},{4,8},{6,10},{8,12},{10,14},{1,5},{3,7},{5,9},{7,11},{... | collective-permute-start | bytes 393224 | tf_op jit(solution)/shard_map/ppermute | solution.py:318
  53.9 21.6 %collective-permute-start.13 = (bf16[256,256]{1,0:T(8,128)(2,1)S(1)}, bf16[256,256]{1,0:T(8,128)(2,1)S(1)}, u32[]{:S(2)}, u32[]{:S(2)}) collective-permute-start(bf16[256,256]{1,0:T(8,128)(2,1)S(1)} %get-tuple-element.39.kv0.kv_ref), channel_id=1, source_target_pairs={{0,2},{2,4},{4,6},{6,8},{8,10},{10,12},{12,14},{1,3},{3,5},{5,7},{... | collective-permute-start | bytes 393224 | tf_op jit(solution)/shard_map/ppermute | solution.py:318
  70.1 19.4 %collective-permute-start.16 = (bf16[256,256]{1,0:T(8,128)(2,1)S(1)}, bf16[256,256]{1,0:T(8,128)(2,1)S(1)}, u32[]{:S(2)}, u32[]{:S(2)}) collective-permute-start(bf16[256,256]{1,0:T(8,128)(2,1)S(1)} %get-tuple-element.47), channel_id=1, source_target_pairs={{2,0},{4,2},{6,4},{8,6},{10,8},{12,10},{14,12},{3,1},{5,3},{7,5},{... | collective-permute-start | bytes 393224 | tf_op jit(solution)/shard_map/ppermute | solution.py:321
  71.4 19.4 %collective-permute-start.17 = (bf16[256,256]{1,0:T(8,128)(2,1)S(1)}, bf16[256,256]{1,0:T(8,128)(2,1)S(1)}, u32[]{:S(2)}, u32[]{:S(2)}) collective-permute-start(bf16[256,256]{1,0:T(8,128)(2,1)S(1)} %get-tuple-element.48), channel_id=1, source_target_pairs={{4,0},{6,2},{8,4},{10,6},{12,8},{14,10},{5,1},{7,3},{9,5},{11,7},{... | collective-permute-start | bytes 393224 | tf_op jit(solution)/shard_map/ppermute | solution.py:321
  72.7 19.4 %collective-permute-start.18 = (bf16[256,256]{1,0:T(8,128)(2,1)S(1)}, bf16[256,256]{1,0:T(8,128)(2,1)S(1)}, u32[]{:S(2)}, u32[]{:S(2)}) collective-permute-start(bf16[256,256]{1,0:T(8,128)(2,1)S(1)} %get-tuple-element.49), channel_id=1, source_target_pairs={{6,0},{8,2},{10,4},{12,6},{14,8},{7,1},{9,3},{11,5},{13,7},{15,9},... | collective-permute-start | bytes 393224 | tf_op jit(solution)/shard_map/ppermute | solution.py:321
  74.0 18.2 %collective-permute-start.19 = (bf16[256,256]{1,0:T(8,128)(2,1)S(1)}, bf16[256,256]{1,0:T(8,128)(2,1)S(1)}, u32[]{:S(2)}, u32[]{:S(2)}) collective-permute-start(bf16[256,256]{1,0:T(8,128)(2,1)S(1)} %get-tuple-element.50), channel_id=1, source_target_pairs={{8,0},{10,2},{12,4},{14,6},{9,1},{11,3},{13,5},{15,7},{24,16},{26,... | collective-permute-start | bytes 393224 | tf_op jit(solution)/shard_map/ppermute | solution.py:321
  89.4 31.6 %collective-permute-start.20 = (bf16[256,256]{1,0:T(8,128)(2,1)}, bf16[256,256]{1,0:T(8,128)(2,1)S(1)}, u32[]{:S(2)}, u32[]{:S(2)}) collective-permute-start(bf16[256,256]{1,0:T(8,128)(2,1)} %get-tuple-element.55), channel_id=1, source_target_pairs={{2,0},{4,2},{6,4},{8,6},{10,8},{12,10},{14,12},{3,1},{5,3},{7,5},{... | collective-permute-start | bytes 393224 | tf_op jit(solution)/shard_map/ppermute | solution.py:321
  90.7 30.3 %collective-permute-start.21 = (bf16[256,256]{1,0:T(8,128)(2,1)}, bf16[256,256]{1,0:T(8,128)(2,1)S(1)}, u32[]{:S(2)}, u32[]{:S(2)}) collective-permute-start(bf16[256,256]{1,0:T(8,128)(2,1)} %get-tuple-element.56), channel_id=1, source_target_pairs={{4,0},{6,2},{8,4},{10,6},{12,8},{14,10},{5,1},{7,3},{9,5},{11,7},{... | collective-permute-start | bytes 393224 | tf_op jit(solution)/shard_map/ppermute | solution.py:321
  92.0 18.6 %collective-permute-start.14 = (bf16[128,1024]{1,0:T(8,128)(2,1)}, bf16[128,1024]{1,0:T(8,128)(2,1)}, u32[]{:S(2)}, u32[]{:S(2)}) collective-permute-start(bf16[128,1024]{1,0:T(8,128)(2,1)} %get-tuple-element.41), channel_id=1, source_target_pairs={{0,1},{1,0},{2,3},{3,2},{4,5},{5,4},{6,7},{7,6},{8,9},{9,8},{10,11... | collective-permute-start | bytes 786440 | tf_op jit(solution)/shard_map/ppermute | solution.py:315
  93.9 27.2 %collective-permute-start.22 = (bf16[256,256]{1,0:T(8,128)(2,1)S(1)}, bf16[256,256]{1,0:T(8,128)(2,1)S(1)}, u32[]{:S(2)}, u32[]{:S(2)}) collective-permute-start(bf16[256,256]{1,0:T(8,128)(2,1)S(1)} %get-tuple-element.57), channel_id=1, source_target_pairs={{6,0},{8,2},{10,4},{12,6},{14,8},{7,1},{9,3},{11,5},{13,7},{15,9},... | collective-permute-start | bytes 393224 | tf_op jit(solution)/shard_map/ppermute | solution.py:321
  95.2 25.9 %collective-permute-start.23 = (bf16[256,256]{1,0:T(8,128)(2,1)S(1)}, bf16[256,256]{1,0:T(8,128)(2,1)S(1)}, u32[]{:S(2)}, u32[]{:S(2)}) collective-permute-start(bf16[256,256]{1,0:T(8,128)(2,1)S(1)} %get-tuple-element.58), channel_id=1, source_target_pairs={{8,0},{10,2},{12,4},{14,6},{9,1},{11,3},{13,5},{15,7},{24,16},{26,... | collective-permute-start | bytes 393224 | tf_op jit(solution)/shard_map/ppermute | solution.py:321
  97.2 23.7 %all-to-all-start.1 = ((f32[128,1,256]{2,1,0:T(1,128)}), f32[128,1,256]{2,1,0:T(1,128)S(1)}, u32[]{:S(2)}, u32[]{:S(2)}) async-start(f32[128,1,256]{2,1,0:T(1,128)} %broadcast_in_dim.9), calls=%async_computation.1 | async-start | bytes 262144 | tf_op jit(solution)/shard_map/all_to_all | solution.py:382
  (16 other events, 167.2 us)

commit v3 on v2

--- a/solution.py
+++ b/solution.py
@@ -23,6 +23,7 @@
 F32 = jnp.float32
 SM = pl.BlockSpec(memory_space=pltpu.SMEM)
 PARAMS = pltpu.CompilerParams(vmem_limit_bytes=48 * 1024 * 1024)
+ALL_VMEM = pltpu.CompilerParams(vmem_limit_bytes=60 * 1024 * 1024)
 
 
 def whole(*shape):
@@ -83,14 +84,11 @@
             out_ref[2 * to + a, :, wide_q + wide_k :] = v_ref[rows, a * wide_k : (a + 1) * wide_k]
 
 
-def keys_kernel(src_ref, recv_ref, *out_refs):
+def keys_kernel(src_ref, recv_ref, out_ref):
     for b in range(2):
         for r in range(8):
             rows = slice(b * TILE + r * RUN, b * TILE + (r + 1) * RUN)
-            one = recv_ref[src_ref[b * 8 + r]]
-            for j, out_ref in enumerate(out_refs):
-                out_ref[rows, :HD] = one[:, j * HD : (j + 1) * HD]
-                out_ref[rows, HD:] = one[:, (2 + j) * HD : (3 + j) * HD]
+            out_ref[rows, :] = recv_ref[src_ref[b * 8 + r]]
 
 
 def tables_kernel(core_ref, id4, id3, id2, id1, id0, freq_ref, tc, ts, bias):
@@ -137,11 +135,12 @@
     for blk in range(BACK + 2):
         rows = slice(blk * TILE, (blk + 1) * TILE)
         ref, part = kvs[blk // 2], slice((blk % 2) * TILE, (blk % 2 + 1) * TILE)
-        x = ref[part, :HD].astype(F32)
-        turned = rope(x * inv_rms(x) * kgain, tc[rows, :], ts[rows, :])
-        kr[rows, :] = turned.astype(BF)
-        kt[:, rows] = turned.T.astype(BF)
-        vs[rows, :] = ref[part, HD:]
+        for j in range(2):
+            x = ref[part, j * HD : (j + 1) * HD].astype(F32)
+            turned = rope(x * inv_rms(x) * kgain, tc[rows, :], ts[rows, :])
+            kr[j, rows, :] = turned.astype(BF)
+            kt[j, :, rows] = turned.T.astype(BF)
+            vs[j, rows, :] = ref[part, (2 + j) * HD : (3 + j) * HD]
     dk_acc[...] = jnp.zeros_like(dk_acc)
     dv_acc[...] = jnp.zeros_like(dv_acc)
     bases, own_rows = [], []
@@ -154,11 +153,11 @@
             xq[turn, r * RUN : (r + 1) * RUN, :] = recv_ref[src_ref[tile * 8 + r]]
     gs, dqs = (g_own, g_sib), (dq_own, dq_sib)
     scs, dps, pbs, dbs = (sc0, sc1), (dp0, dp1), (pb0, pb1), (db0, db1)
-    units = [(turn, h) for turn in range(2) for h in range(0, 8, HG)]
+    units = [(turn, h) for turn in range(2) for h in range(0, 16, HG)]
 
     def front(u):
         turn, h0 = units[u]
-        qts, gts = [], []
+        j, qts, gts = h0 // 8, [], []
         for h in range(h0, h0 + HG):
             cols = slice(h * HD, (h + 1) * HD)
             x = xq[turn, :, cols].astype(F32)
@@ -172,8 +171,8 @@
             [jnp.concatenate(qts, axis=1), jnp.concatenate([eye] * HG, axis=1)], axis=0
         )
         win = pl.ds(bases[turn], WIN)
-        scs[u % 2][...] = dot(jnp.concatenate([kr[win, :], bias[turn]], axis=1), qt)
-        dps[u % 2][...] = dot(vs[win, :], jnp.concatenate(gts, axis=1))
+        scs[u % 2][...] = dot(jnp.concatenate([kr[j, win, :], bias[turn]], axis=1), qt)
+        dps[u % 2][...] = dot(vs[j, win, :], jnp.concatenate(gts, axis=1))
 
     def middle(u):
         sc, dp, pb, db = scs[u % 2], dps[u % 2], pbs[u % 2], dbs[u % 2]
@@ -202,9 +201,10 @@
 
     def tail(u, q_term):
         turn, h0 = units[u]
+        j = h0 // 8
         pb, db = pbs[u % 2], dbs[u % 2]
         keys = pl.ds(bases[turn], WIN)
-        dqt = dot(kt[:, keys], db[...]) * SCALE
+        dqt = dot(kt[j, :, keys], db[...]) * SCALE
         for i, h in enumerate(range(h0, h0 + HG)):
             cols = slice(h * HD, (h + 1) * HD)
             dn = rope_back(
@@ -215,8 +215,8 @@
             q_term = q_term + fold(dn * x * rs, jnp.sum)
             dqs[turn][:, cols] = norm_back(dn, x, rs, qgain).astype(BF)
         mine = slice(h0 * TILE, (h0 + HG) * TILE)
-        dv_acc[keys, :] += dot(pb[...], g8s[turn, mine, :])
-        dk_acc[keys, :] += dot(db[...], q8s[turn, mine, :])
+        dv_acc[j, keys, :] += dot(pb[...], g8s[turn, mine, :])
+        dk_acc[j, keys, :] += dot(db[...], q8s[turn, mine, :])
         return q_term
 
     q_term = jnp.zeros((8, HD), F32)
@@ -231,13 +231,15 @@
     for blk in range(BACK + 2):
         rows = slice(blk * TILE, (blk + 1) * TILE)
         part = slice((blk % 2) * TILE, (blk % 2 + 1) * TILE)
-        dk = dk_acc[rows, :] * SCALE
-        x = kvs[blk // 2][part, :HD].astype(F32)
-        dn = rope_back(dk, tc[rows, :], ts[rows, :])
-        k_term = k_term + fold(dn * x * inv_rms(x), jnp.sum)
         out = outs[blk // 2]
-        out[part, :HD] = dk.astype(out.dtype)
-        out[part, HD:] = dv_acc[rows, :].astype(out.dtype)
+        for j in range(2):
+            dk_cols, dv_cols = slice(j * HD, (j + 1) * HD), slice((2 + j) * HD, (3 + j) * HD)
+            dk = dk_acc[j, rows, :] * SCALE
+            x = kvs[blk // 2][part, dk_cols].astype(F32)
+            dn = rope_back(dk, tc[rows, :], ts[rows, :])
+            k_term = k_term + fold(dn * x * inv_rms(x), jnp.sum)
+            out[part, dk_cols] = dk.astype(out.dtype)
+            out[part, dv_cols] = dv_acc[j, rows, :].astype(out.dtype)
     gains_ref[0:1, :] = jnp.sum(q_term, axis=0, keepdims=True)
     gains_ref[1:2, :] = jnp.sum(k_term, axis=0, keepdims=True)
 
@@ -249,51 +251,53 @@
         total = own_ref[rows, :]
         for r in (r1, r2, r3, r4):
             total = total + r[rows, :].astype(F32)
-        x = kv_ref[rows, :HD].astype(F32)
-        dn = rope_back(total[:, :HD], tc_ref[rows, :], ts_ref[rows, :])
-        both[b, :, :HD] = norm_back(dn, x, inv_rms(x), kg_ref[...]).astype(BF)
-        both[b, :, HD:] = total[:, HD:].astype(BF)
+        for j in range(2):
+            cols = slice(j * HD, (j + 1) * HD)
+            x = kv_ref[rows, cols].astype(F32)
+            dn = rope_back(total[:, cols], tc_ref[rows, :], ts_ref[rows, :])
+            both[b, :, cols] = norm_back(dn, x, inv_rms(x), kg_ref[...]).astype(BF)
+        both[b, :, 2 * HD :] = total[:, 2 * HD :].astype(BF)
     mine_ref[...] = both[core]
     other_ref[...] = both[1 - core]
 
 
-def head_grads(j, core1, src, recv, kv4, kv3, kv2, kv1, kv0, grad_out, g_sib, tc, ts, bias, q_gain, k_gain):
+def head_grads(core1, src, recv, kv4, kv3, kv2, kv1, kv0, grad_out, g_sib, tc, ts, bias, q_gain, k_gain):
     sds = jax.ShapeDtypeStruct
-    groups, wide = recv.shape[0] // 2, 8 * HD
+    groups, wide = recv.shape[0] // 2, 16 * HD
     rows2 = 2 * TILE
     unit = HG * TILE
     return pl.pallas_call(
         heads_kernel,
         out_shape=(
             [sds((TILE, wide), BF)] * 2
-            + [sds((rows2, 2 * HD), BF)] * 4
-            + [sds((rows2, 2 * HD), F32), sds((2, HD), F32)]
+            + [sds((rows2, 4 * HD), BF)] * 4
+            + [sds((rows2, 4 * HD), F32), sds((2, HD), F32)]
         ),
         grid_spec=pltpu.PrefetchScalarGridSpec(
             num_scalar_prefetch=2,
             grid=(1,),
-            in_specs=[pl.BlockSpec((2 * groups, RUN, wide), lambda i, c, s: (0, 0, j))]
-            + [whole(rows2, 2 * HD)] * 5
-            + [pl.BlockSpec((TILE, wide), lambda i, c, s: (0, 2 * c[0] + j))]
-            + [pl.BlockSpec((TILE, wide), lambda i, c, s: (0, j))]
+            in_specs=[pl.BlockSpec((2 * groups, RUN, wide), lambda i, c, s: (0, 0, 0))]
+            + [whole(rows2, 4 * HD)] * 5
+            + [pl.BlockSpec((TILE, wide), lambda i, c, s: (0, c[0]))]
+            + [whole(TILE, wide)]
             + [whole(ALLW, HD)] * 2
             + [whole(2, WIN, TILE)]
             + [whole(1, HD)] * 2,
-            out_specs=[whole(TILE, wide)] * 2 + [whole(rows2, 2 * HD)] * 5 + [whole(2, HD)],
+            out_specs=[whole(TILE, wide)] * 2 + [whole(rows2, 4 * HD)] * 5 + [whole(2, HD)],
             scratch_shapes=[
-                pltpu.VMEM((ALLW, HD), BF),
-                pltpu.VMEM((HD, ALLW), BF),
-                pltpu.VMEM((ALLW, HD), BF),
+                pltpu.VMEM((2, ALLW, HD), BF),
+                pltpu.VMEM((2, HD, ALLW), BF),
+                pltpu.VMEM((2, ALLW, HD), BF),
                 pltpu.VMEM((2, TILE, wide), BF),
                 pltpu.VMEM((2, wide, HD), BF),
                 pltpu.VMEM((2, wide, HD), BF),
             ]
             + [pltpu.VMEM((WIN, unit), F32)] * 4
             + [pltpu.VMEM((WIN, unit), BF)] * 4
-            + [pltpu.VMEM((ALLW, HD), F32)] * 2,
+            + [pltpu.VMEM((2, ALLW, HD), F32)] * 2,
         ),
-        compiler_params=PARAMS,
-        cost_estimate=pl.CostEstimate(flops=3 * 10**9, bytes_accessed=6 * 10**6, transcendentals=3 * 10**6),
+        compiler_params=ALL_VMEM,
+        cost_estimate=pl.CostEstimate(flops=6 * 10**9, bytes_accessed=12 * 10**6, transcendentals=5 * 10**6),
         name="head_grads",
     )(
         core1, src, recv, kv4, kv3, kv2, kv1, kv0, grad_out, g_sib, tc, ts, bias,
@@ -333,7 +337,7 @@
         grid=(1,),
         in_specs=[SM, SM, whole(*q_in.shape), whole(*k_in.shape), whole(*v_in.shape)],
         out_specs=whole(2 * groups, RUN, 2560),
-        compiler_params=PARAMS,
+        compiler_params=ALL_VMEM,
         name="pack_runs",
     )(shift_plan, member.reshape(1), q_in, k_in, v_in)
     recv = lax.all_to_all(packed, ("dp", "core"), 0, 0, tiled=True)
@@ -358,58 +362,42 @@
     g_sib = to_sibling(lax.dynamic_slice_in_dim(grad_out, (1 - core) * wide, wide, 1))
     kv0 = pl.pallas_call(
         keys_kernel,
-        out_shape=[sds((rows2, 2 * HD), BF)] * 2,
+        out_shape=sds((rows2, 4 * HD), BF),
         grid=(1,),
         in_specs=[SM, pl.BlockSpec((2 * groups, RUN, 4 * HD), lambda i: (0, 0, 4))],
-        out_specs=[whole(rows2, 2 * HD)] * 2,
+        out_specs=whole(rows2, 4 * HD),
         compiler_params=PARAMS,
         name="own_keys",
     )(src, recv)
-    kv = [[ahead(kv0[j], d) for d in range(1, 5)] for j in range(2)]
-    dq_mine, dq_got, gains, done = [], [], 0.0, []
-    for j in range(2):
-        mine, other, *parts, own, gain = head_grads(
-            j, core1, src, recv, *kv[j][::-1], kv0[j], grad_out, g_sib, tc, ts, bias, q_gain, k_gain
-        )
-        back = [behind(part, d) for d, part in zip(range(1, 5), parts)]
-        dq_mine.append(mine)
-        dq_got.append(to_sibling(other))
-        gains = gains + gain
-        done.append((own, back))
-    gains, dq_got[1] = lax.optimization_barrier((gains, dq_got[1]))
-    every = 2 * groups * chips
+    kv = [ahead(kv0, d) for d in range(1, 5)]
+    dq_mine, dq_other, *parts, own, gains = head_grads(
+        core1, src, recv, *kv[::-1], kv0, grad_out, g_sib, tc, ts, bias, q_gain, k_gain
+    )
+    back = [behind(part, d) for d, part in zip(range(1, 5), parts)]
+    dq_got = to_sibling(dq_other)
+    gains = gains + to_sibling(gains)
+    gains, dq_got = lax.optimization_barrier((gains, dq_got))
+    every = groups * chips
     spread = jnp.broadcast_to(gains.reshape(1, 1, 2 * HD), (every, 1, 2 * HD))
-    terms = jnp.sum(lax.all_to_all(spread, ("dp", "chip", "core"), 0, 0, tiled=True), axis=(0, 1))
-    mine, got = [], []
-    for j, (own, back) in enumerate(done):
-        if j == 1:
-            terms, own = lax.optimization_barrier((terms, own))
-        a, b = pl.pallas_call(
-            finish_kernel,
-            out_shape=[sds((TILE, 2 * HD), BF)] * 2,
-            grid=(1,),
-            in_specs=[SM]
-            + [whole(rows2, 2 * HD)] * 6
-            + [pl.BlockSpec((rows2, HD), lambda i: (BACK // 2, 0))] * 2
-            + [whole(1, HD)],
-            out_specs=[whole(TILE, 2 * HD)] * 2,
-            scratch_shapes=[pltpu.VMEM((2, TILE, 2 * HD), BF)],
-            compiler_params=PARAMS,
-            name="finish_keys",
-        )(core1, own, *back, kv0[j], tc, ts, k_gain.reshape(1, HD))
-        mine.append(a)
-        got.append(to_sibling(b))
-
-    def joined(part):
-        return by_core(
-            jnp.concatenate([part(one) for one in mine], axis=1),
-            jnp.concatenate([part(one) for one in got], axis=1),
-            1,
-        )
-
-    dq = by_core(jnp.concatenate(dq_mine, axis=1), jnp.concatenate(dq_got, axis=1), 1)
-    dk = joined(lambda one: one[:, :HD])
-    dv = joined(lambda one: one[:, HD:])
+    terms = jnp.sum(lax.all_to_all(spread, ("dp", "chip"), 0, 0, tiled=True), axis=(0, 1))
+    own, terms = lax.optimization_barrier((own, terms))
+    mine, other = pl.pallas_call(
+        finish_kernel,
+        out_shape=[sds((TILE, 4 * HD), BF)] * 2,
+        grid=(1,),
+        in_specs=[SM]
+        + [whole(rows2, 4 * HD)] * 6
+        + [pl.BlockSpec((rows2, HD), lambda i: (BACK // 2, 0))] * 2
+        + [whole(1, HD)],
+        out_specs=[whole(TILE, 4 * HD)] * 2,
+        scratch_shapes=[pltpu.VMEM((2, TILE, 4 * HD), BF)],
+        compiler_params=PARAMS,
+        name="finish_keys",
+    )(core1, own, *back, kv0, tc, ts, k_gain.reshape(1, HD))
+    got = to_sibling(other)
+    dq = by_core(dq_mine, dq_got, 1)
+    dk = by_core(mine[:, : 2 * HD], got[:, : 2 * HD], 1)
+    dv = by_core(mine[:, 2 * HD :], got[:, 2 * HD :], 1)
     return dq, dk, dv, terms[:HD], terms[HD:]
 
 

time: 124 us -> 120 us (0.968)
  the two profiles are of different devices: /device:TPU:1 before, /device:TPU:3 now
where the time goes in v3:
time: 120 us; the launch traced here: 119 us
  starting transfers between devices  58.3 us (49%)
  Pallas kernels  28.5 us (24%)
  waiting for transfers between devices  21.9 us (18%)
  local copies, waits for them, and re-layouts  4.72 us (4%)
  other arithmetic  4.71 us (4%)
    pallas_call x1, Pallas kernels, head_grads(): pl.pallas_call(heads_kernel, out_shape=[sds((TILE, wide), BF)] * 2 + [sds...  23.6 us
    ppermute x8, starting transfers between devices, ahead(): return lax.ppermute(x, 'chip', [(i, i + d) for i in range(chips - d)])  20.1 us
    ppermute x4, starting transfers between devices, behind(): return lax.ppermute(x, 'chip', [(i, i - d) for i in range(d, chips)])  14.8 us
    all_to_all x1, waiting for transfers between devices, body(): lax.all_to_all(spread, ('dp', 'chip'), 0, 0, tiled=True)  10.8 us
    all_to_all x1, starting transfers between devices, body(): lax.all_to_all(spread, ('dp', 'chip'), 0, 0, tiled=True)  8.72 us
    all_to_all x1, starting transfers between devices, body(): recv = lax.all_to_all(packed, ('dp', 'core'), 0, 0, tiled=True)  8.61 us
    all_to_all x1, waiting for transfers between devices, body(): recv = lax.all_to_all(packed, ('dp', 'core'), 0, 0, tiled=True)  8.43 us
    ppermute x5, starting transfers between devices, to_sibling(): return lax.ppermute(x, 'core', [(0, 1), (1, 0)])  6.13 us
  transfers between devices with their start and end apart: 19, of which 5 were waited for; matrix products, arithmetic and copies ran while one was open for 4% of the time, Pallas kernels for 2%

profile of v3, /device:TPU:3, one launch (start us, length us, event | category | flops | bytes accessed | tf_op | source)
XLA Modules:
  0.0 119.3 jit_solution(5187005069831632087)
XLA Ops:
  0.6 2.5 %pack_runs.1 = bf16[16,16,2560]{2,1,0:T(8,128)(2,1)} custom-call(s32[1,8]{1,0:T(1,128)} %plan_ref.1, s32[1]{0:T(128)} %bitcast.1.who_ref, bf16[128,4096]{1,0:T(8,128)(2,1)} %q_ref.1, bf16[128,512]{1,0:T(8,128)(2,1)} %k_ref.1, bf16[128,512]{1,0:T(8,128)(2,1)} %v_ref.1), custom_call_target="tpu_custom_call" | custom-call | tf_op jit(solution)/shard_map/pack_runs/pallas_call | solution.py:334
  3.1 8.6 %all-to-all-start = ((bf16[16,16,2560]{2,1,0:T(8,128)(2,1)}), bf16[16,16,2560]{2,1,0:T(8,128)(2,1)S(1)}, u32[]{:S(2)}, u32[]{:S(2)}) async-start(bf16[16,16,2560]{2,1,0:T(8,128)(2,1)} %pack_runs.1), calls=%async_computation | async-start | bytes 2621440 | tf_op jit(solution)/shard_map/all_to_all | solution.py:343
  13.2 2.6 %collective-permute-start.9 = (s32[1,256]{1,0:T(1,128)S(1)}, s32[1,256]{1,0:T(1,128)S(1)}, u32[]{:S(2)}, u32[]{:S(2)}) collective-permute-start(s32[1,256]{1,0:T(1,128)S(1)} %bitcast.8), channel_id=1, source_target_pairs={{0,2},{2,4},{4,6},{6,8},{8,10},{10,12},{12,14},{1,3},{3,5},{5,7},{... | collective-permute-start | bytes 3080 | tf_op jit(solution)/shard_map/ppermute | solution.py:322
  15.8 3.1 %collective-permute-start.8 = (s32[1,256]{1,0:T(1,128)S(1)}, s32[1,256]{1,0:T(1,128)S(1)}, u32[]{:S(2)}, u32[]{:S(2)}) collective-permute-start(s32[1,256]{1,0:T(1,128)S(1)} %bitcast.9), channel_id=1, source_target_pairs={{0,4},{2,6},{4,8},{6,10},{8,12},{10,14},{1,5},{3,7},{5,9},{7,11},{... | collective-permute-start | bytes 3080 | tf_op jit(solution)/shard_map/ppermute | solution.py:322
  18.9 3.0 %collective-permute-start.7 = (s32[1,256]{1,0:T(1,128)S(1)}, s32[1,256]{1,0:T(1,128)S(1)}, u32[]{:S(2)}, u32[]{:S(2)}) collective-permute-start(s32[1,256]{1,0:T(1,128)S(1)} %bitcast.10), channel_id=1, source_target_pairs={{0,6},{2,8},{4,10},{6,12},{8,14},{1,7},{3,9},{5,11},{7,13},{9,15},... | collective-permute-start | bytes 3080 | tf_op jit(solution)/shard_map/ppermute | solution.py:322
  21.9 1.3 %collective-permute-start.6 = (s32[1,256]{1,0:T(1,128)S(1)}, s32[1,256]{1,0:T(1,128)S(1)}, u32[]{:S(2)}, u32[]{:S(2)}) collective-permute-start(s32[1,256]{1,0:T(1,128)S(1)} %bitcast.11), channel_id=1, source_target_pairs={{0,8},{2,10},{4,12},{6,14},{1,9},{3,11},{5,13},{7,15},{16,24},{18,... | collective-permute-start | bytes 3080 | tf_op jit(solution)/shard_map/ppermute | solution.py:322
  23.3 8.4 %all-to-all-done.recv_ref = bf16[16,16,2560]{2,1,0:T(8,128)(2,1)S(1)} async-done(((bf16[16,16,2560]{2,1,0:T(8,128)(2,1)}), bf16[16,16,2560]{2,1,0:T(8,128)(2,1)S(1)}, u32[]{:S(2)}, u32[]{:S(2)}) %all-to-all-start) | async-done | bytes 1310752 | tf_op jit(solution)/shard_map/all_to_all | solution.py:343
  32.4 2.6 %collective-permute-start.4 = (bf16[256,512]{1,0:T(8,128)(2,1)S(1)}, bf16[256,512]{1,0:T(8,128)(2,1)S(1)}, u32[]{:S(2)}, u32[]{:S(2)}) collective-permute-start(bf16[256,512]{1,0:T(8,128)(2,1)S(1)} %own_keys.1.kv0.kv_ref), channel_id=1, source_target_pairs={{0,2},{2,4},{4,6},{6,8},{8,10},{10,12},{12,14},{1,3},{3,5},{5,7},{... | collective-permute-start | bytes 786440 | tf_op jit(solution)/shard_map/ppermute | solution.py:322
  35.0 3.1 %collective-permute-start.3 = (bf16[256,512]{1,0:T(8,128)(2,1)S(1)}, bf16[256,512]{1,0:T(8,128)(2,1)S(1)}, u32[]{:S(2)}, u32[]{:S(2)}) collective-permute-start(bf16[256,512]{1,0:T(8,128)(2,1)S(1)} %own_keys.1.kv0.kv_ref), channel_id=1, source_target_pairs={{0,4},{2,6},{4,8},{6,10},{8,12},{10,14},{1,5},{3,7},{5,9},{7,11},{... | collective-permute-start | bytes 786440 | tf_op jit(solution)/shard_map/ppermute | solution.py:322
  38.2 3.0 %collective-permute-start.2 = (bf16[256,512]{1,0:T(8,128)(2,1)S(1)}, bf16[256,512]{1,0:T(8,128)(2,1)S(1)}, u32[]{:S(2)}, u32[]{:S(2)}) collective-permute-start(bf16[256,512]{1,0:T(8,128)(2,1)S(1)} %own_keys.1.kv0.kv_ref), channel_id=1, source_target_pairs={{0,6},{2,8},{4,10},{6,12},{8,14},{1,7},{3,9},{5,11},{7,13},{9,15},... | collective-permute-start | bytes 786440 | tf_op jit(solution)/shard_map/ppermute | solution.py:322
  41.2 1.3 %collective-permute-start.1 = (bf16[256,512]{1,0:T(8,128)(2,1)S(1)}, bf16[256,512]{1,0:T(8,128)(2,1)S(1)}, u32[]{:S(2)}, u32[]{:S(2)}) collective-permute-start(bf16[256,512]{1,0:T(8,128)(2,1)S(1)} %own_keys.1.kv0.kv_ref), channel_id=1, source_target_pairs={{0,8},{2,10},{4,12},{6,14},{1,9},{3,11},{5,13},{7,15},{16,24},{18,... | collective-permute-start | bytes 786440 | tf_op jit(solution)/shard_map/ppermute | solution.py:322
  42.6 1.4 %rope_tables.1 = (f32[1280,128]{1,0:T(8,128)S(1)}, f32[1280,128]{1,0:T(8,128)S(1)}, bf16[2,1152,128]{2,1,0:T(8,128)(2,1)S(1)}) custom-call(s32[1]{0:T(128)} %bitcast.core_ref, s32[1,256]{1,0:T(1,128)S(1)} %collective-permute-done.6.id4, s32[1,256]{1,0:T(1,128)S(1)} %collective-permute-done.7.id3, s32[1,256]{1,0:T(1,128)S(1)} %collective-permute-done.8.id2, ...), custom_call_target="tpu_custom_call" | custom-call | tf_op jit(solution)/shard_map/rope_tables/pallas_call | solution.py:353
  44.8 0.8 copy-done.5
  46.5 1.7 %collective-permute-done.2.kv3 = bf16[256,512]{1,0:T(8,128)(2,1)S(1)} collective-permute-done((bf16[256,512]{1,0:T(8,128)(2,1)S(1)}, bf16[256,512]{1,0:T(8,128)(2,1)S(1)}, u32[]{:S(2)}, u32[]{:S(2)}) %collective-permute-start.2) | collective-permute-done | bytes 262176 | tf_op jit(solution)/shard_map/ppermute | solution.py:322
  49.0 23.6 %head_grads.1 = (bf16[128,2048]{1,0:T(8,128)(2,1)}, bf16[128,2048]{1,0:T(8,128)(2,1)}, bf16[256,512]{1,0:T(8,128)(2,1)}, bf16[256,512]{1,0:T(8,128)(2,1)}, bf16[...) custom-call(s32[1]{0:T(128)} %bitcast.core_ref, s32[16]{0:T(128)} %copy-done.9, ...), custom_call_target="tpu_custom_call" | custom-call | flops 6000000000 | bytes 12000000 | tf_op jit(solution)/shard_map/head_grads/pallas_call | solution.py:269
  72.7 3.4 %collective-permute-start.11 = (bf16[128,2048]{1,0:T(8,128)(2,1)}, bf16[128,2048]{1,0:T(8,128)(2,1)}, u32[]{:S(2)}, u32[]{:S(2)}) collective-permute-start(bf16[128,2048]{1,0:T(8,128)(2,1)} %get-tuple-element.27), channel_id=1, source_target_pairs={{0,1},{1,0},{2,3},{3,2},{4,5},{5,4},{6,7},{7,6},{8,9},{9,8},{10,11... | collective-permute-start | bytes 1572872 | tf_op jit(solution)/shard_map/ppermute | solution.py:319
  76.1 10.3 %collective-permute-start.12 = (bf16[256,512]{1,0:T(8,128)(2,1)}, bf16[256,512]{1,0:T(8,128)(2,1)S(1)}, u32[]{:S(2)}, u32[]{:S(2)}) collective-permute-start(bf16[256,512]{1,0:T(8,128)(2,1)} %get-tuple-element.32), channel_id=1, source_target_pairs={{2,0},{4,2},{6,4},{8,6},{10,8},{12,10},{14,12},{3,1},{5,3},{7,5},{... | collective-permute-start | bytes 786440 | tf_op jit(solution)/shard_map/ppermute | solution.py:325
  86.4 1.9 %collective-permute-start.13 = (bf16[256,512]{1,0:T(8,128)(2,1)}, bf16[256,512]{1,0:T(8,128)(2,1)S(1)}, u32[]{:S(2)}, u32[]{:S(2)}) collective-permute-start(bf16[256,512]{1,0:T(8,128)(2,1)} %get-tuple-element.33), channel_id=1, source_target_pairs={{4,0},{6,2},{8,4},{10,6},{12,8},{14,10},{5,1},{7,3},{9,5},{11,7},{... | collective-permute-start | bytes 786440 | tf_op jit(solution)/shard_map/ppermute | solution.py:325
  88.3 1.3 %collective-permute-start.14 = (bf16[256,512]{1,0:T(8,128)(2,1)}, bf16[256,512]{1,0:T(8,128)(2,1)S(1)}, u32[]{:S(2)}, u32[]{:S(2)}) collective-permute-start(bf16[256,512]{1,0:T(8,128)(2,1)} %get-tuple-element.34), channel_id=1, source_target_pairs={{6,0},{8,2},{10,4},{12,6},{14,8},{7,1},{9,3},{11,5},{13,7},{15,9},... | collective-permute-start | bytes 786440 | tf_op jit(solution)/shard_map/ppermute | solution.py:325
  89.6 1.3 %collective-permute-start.15 = (bf16[256,512]{1,0:T(8,128)(2,1)}, bf16[256,512]{1,0:T(8,128)(2,1)S(1)}, u32[]{:S(2)}, u32[]{:S(2)}) collective-permute-start(bf16[256,512]{1,0:T(8,128)(2,1)} %get-tuple-element.35), channel_id=1, source_target_pairs={{8,0},{10,2},{12,4},{14,6},{9,1},{11,3},{13,5},{15,7},{24,16},{26,... | collective-permute-start | bytes 786440 | tf_op jit(solution)/shard_map/ppermute | solution.py:325
  92.3 8.7 %all-to-all-start.1 = ((f32[64,1,256]{2,1,0:T(1,128)}), f32[64,1,256]{2,1,0:T(1,128)S(1)}, u32[]{:S(2)}, u32[]{:S(2)}) async-start(f32[64,1,256]{2,1,0:T(1,128)} %broadcast_in_dim.9), calls=%async_computation.1 | async-start | bytes 131072 | tf_op jit(solution)/shard_map/all_to_all | solution.py:382
  101.0 2.9 %maximum_select_fusion = bf16[128,4096]{1,0:T(8,128)(2,1)} fusion(bf16[128,2048]{1,0:T(8,128)(2,1)} %collective-permute-done.11, bf16[128,2048]{1,0:T(8,128)(2,1)} %get-tuple-element.25, pred[]{:T(512)S(6)} %eq.4), kind=kLoop, calls=%fused_computation | loop fusion | flops 4718592 | bytes 2097153 | tf_op jit(solution)/shard_map/jit(_where)/select_n | solution.py:328
  103.9 10.8 %all-to-all-done.1 = f32[64,1,256]{2,1,0:T(1,128)S(1)} async-done(((f32[64,1,256]{2,1,0:T(1,128)}), f32[64,1,256]{2,1,0:T(1,128)S(1)}, u32[]{:S(2)}, u32[]{:S(2)}) %all-to-all-start.1) | async-done | bytes 65568 | tf_op jit(solution)/shard_map/all_to_all | solution.py:382
  115.4 2.1 %collective-permute-start.16 = (bf16[128,512]{1,0:T(8,128)(2,1)S(1)}, bf16[128,512]{1,0:T(8,128)(2,1)S(1)}, u32[]{:S(2)}, u32[]{:S(2)}) collective-permute-start(bf16[128,512]{1,0:T(8,128)(2,1)S(1)} %get-tuple-element.37), channel_id=1, source_target_pairs={{0,1},{1,0},{2,3},{3,2},{4,5},{5,4},{6,7},{7,6},{8,9},{9,8},{10,11... | collective-permute-start | bytes 393224 | tf_op jit(solution)/shard_map/ppermute | solution.py:319
  (74 shorter events, 8.5 us)
Async XLA Ops:
  3.1 28.6 %all-to-all-start = ((bf16[16,16,2560]{2,1,0:T(8,128)(2,1)}), bf16[16,16,2560]{2,1,0:T(8,128)(2,1)S(1)}, u32[]{:S(2)}, u32[]{:S(2)}) async-start(bf16[16,16,2560]{2,1,0:T(8,128)(2,1)} %pack_runs.1), calls=%async_computation | async-start | bytes 2621440 | tf_op jit(solution)/shard_map/all_to_all | solution.py:343
  11.9 1.2 collective-permute-start
  12.0 34.5 %collective-permute-start.5 = (bf16[128,2048]{1,0:T(8,128)(2,1)S(1)}, bf16[128,2048]{1,0:T(8,128)(2,1)S(1)}, u32[]{:S(2)}, u32[]{:S(2)}) collective-permute-start(bf16[128,2048]{1,0:T(8,128)(2,1)S(1)} %constant_dynamic-slice_fusion), channel_id=1, source_target_pairs={{0,1},{1,0},{2,3},{3,2},{4,5},{5,4},{6,7},{7,6},{8,9},{9,8},{10,11... | collective-permute-start | bytes 1572872 | tf_op jit(solution)/shard_map/ppermute | solution.py:319
  13.2 19.2 %collective-permute-start.9 = (s32[1,256]{1,0:T(1,128)S(1)}, s32[1,256]{1,0:T(1,128)S(1)}, u32[]{:S(2)}, u32[]{:S(2)}) collective-permute-start(s32[1,256]{1,0:T(1,128)S(1)} %bitcast.8), channel_id=1, source_target_pairs={{0,2},{2,4},{4,6},{6,8},{8,10},{10,12},{12,14},{1,3},{3,5},{5,7},{... | collective-permute-start | bytes 3080 | tf_op jit(solution)/shard_map/ppermute | solution.py:322
  15.8 19.2 %collective-permute-start.8 = (s32[1,256]{1,0:T(1,128)S(1)}, s32[1,256]{1,0:T(1,128)S(1)}, u32[]{:S(2)}, u32[]{:S(2)}) collective-permute-start(s32[1,256]{1,0:T(1,128)S(1)} %bitcast.9), channel_id=1, source_target_pairs={{0,4},{2,6},{4,8},{6,10},{8,12},{10,14},{1,5},{3,7},{5,9},{7,11},{... | collective-permute-start | bytes 3080 | tf_op jit(solution)/shard_map/ppermute | solution.py:322
  18.9 19.2 %collective-permute-start.7 = (s32[1,256]{1,0:T(1,128)S(1)}, s32[1,256]{1,0:T(1,128)S(1)}, u32[]{:S(2)}, u32[]{:S(2)}) collective-permute-start(s32[1,256]{1,0:T(1,128)S(1)} %bitcast.10), channel_id=1, source_target_pairs={{0,6},{2,8},{4,10},{6,12},{8,14},{1,7},{3,9},{5,11},{7,13},{9,15},... | collective-permute-start | bytes 3080 | tf_op jit(solution)/shard_map/ppermute | solution.py:322
  21.9 19.2 %collective-permute-start.6 = (s32[1,256]{1,0:T(1,128)S(1)}, s32[1,256]{1,0:T(1,128)S(1)}, u32[]{:S(2)}, u32[]{:S(2)}) collective-permute-start(s32[1,256]{1,0:T(1,128)S(1)} %bitcast.11), channel_id=1, source_target_pairs={{0,8},{2,10},{4,12},{6,14},{1,9},{3,11},{5,13},{7,15},{16,24},{18,... | collective-permute-start | bytes 3080 | tf_op jit(solution)/shard_map/ppermute | solution.py:322
  32.4 14.1 %collective-permute-start.4 = (bf16[256,512]{1,0:T(8,128)(2,1)S(1)}, bf16[256,512]{1,0:T(8,128)(2,1)S(1)}, u32[]{:S(2)}, u32[]{:S(2)}) collective-permute-start(bf16[256,512]{1,0:T(8,128)(2,1)S(1)} %own_keys.1.kv0.kv_ref), channel_id=1, source_target_pairs={{0,2},{2,4},{4,6},{6,8},{8,10},{10,12},{12,14},{1,3},{3,5},{5,7},{... | collective-permute-start | bytes 786440 | tf_op jit(solution)/shard_map/ppermute | solution.py:322
  35.0 11.5 %collective-permute-start.3 = (bf16[256,512]{1,0:T(8,128)(2,1)S(1)}, bf16[256,512]{1,0:T(8,128)(2,1)S(1)}, u32[]{:S(2)}, u32[]{:S(2)}) collective-permute-start(bf16[256,512]{1,0:T(8,128)(2,1)S(1)} %own_keys.1.kv0.kv_ref), channel_id=1, source_target_pairs={{0,4},{2,6},{4,8},{6,10},{8,12},{10,14},{1,5},{3,7},{5,9},{7,11},{... | collective-permute-start | bytes 786440 | tf_op jit(solution)/shard_map/ppermute | solution.py:322
  38.2 10.0 %collective-permute-start.2 = (bf16[256,512]{1,0:T(8,128)(2,1)S(1)}, bf16[256,512]{1,0:T(8,128)(2,1)S(1)}, u32[]{:S(2)}, u32[]{:S(2)}) collective-permute-start(bf16[256,512]{1,0:T(8,128)(2,1)S(1)} %own_keys.1.kv0.kv_ref), channel_id=1, source_target_pairs={{0,6},{2,8},{4,10},{6,12},{8,14},{1,7},{3,9},{5,11},{7,13},{9,15},... | collective-permute-start | bytes 786440 | tf_op jit(solution)/shard_map/ppermute | solution.py:322
  41.2 7.0 %collective-permute-start.1 = (bf16[256,512]{1,0:T(8,128)(2,1)S(1)}, bf16[256,512]{1,0:T(8,128)(2,1)S(1)}, u32[]{:S(2)}, u32[]{:S(2)}) collective-permute-start(bf16[256,512]{1,0:T(8,128)(2,1)S(1)} %own_keys.1.kv0.kv_ref), channel_id=1, source_target_pairs={{0,8},{2,10},{4,12},{6,14},{1,9},{3,11},{5,13},{7,15},{16,24},{18,... | collective-permute-start | bytes 786440 | tf_op jit(solution)/shard_map/ppermute | solution.py:322
  72.6 42.2 %copy-start.2 = (bf16[256,512]{1,0:T(8,128)(2,1)S(1)}, bf16[256,512]{1,0:T(8,128)(2,1)}, u32[]{:S(2)}) copy-start(bf16[256,512]{1,0:T(8,128)(2,1)} %copy-done.1) | copy-start | bytes 786436
  72.6 42.2 %copy-start.4 = (f32[1280,128]{1,0:T(8,128)S(1)}, f32[1280,128]{1,0:T(8,128)}, u32[]{:S(2)}) copy-start(f32[1280,128]{1,0:T(8,128)} %copy-done.3) | copy-start | bytes 1966084
  72.6 42.2 %copy-start.6 = (f32[1280,128]{1,0:T(8,128)S(1)}, f32[1280,128]{1,0:T(8,128)}, u32[]{:S(2)}) copy-start(f32[1280,128]{1,0:T(8,128)} %copy-done.5) | copy-start | bytes 1966084
  72.6 42.2 %copy-start.7 = (f32[256,512]{1,0:T(8,128)S(1)}, f32[256,512]{1,0:T(8,128)}, u32[]{:S(2)}) copy-start(f32[256,512]{1,0:T(8,128)} %get-tuple-element.31.own_ref) | copy-start | bytes 1572868
  72.7 42.2 %copy-start.8 = (f32[128]{0:T(128)S(1)}, f32[128]{0:T(128)}, u32[]{:S(2)}) copy-start(f32[128]{0:T(128)} %param.13) | copy-start | bytes 1540
  72.7 19.0 %collective-permute-start.11 = (bf16[128,2048]{1,0:T(8,128)(2,1)}, bf16[128,2048]{1,0:T(8,128)(2,1)}, u32[]{:S(2)}, u32[]{:S(2)}) collective-permute-start(bf16[128,2048]{1,0:T(8,128)(2,1)} %get-tuple-element.27), channel_id=1, source_target_pairs={{0,1},{1,0},{2,3},{3,2},{4,5},{5,4},{6,7},{7,6},{8,9},{9,8},{10,11... | collective-permute-start | bytes 1572872 | tf_op jit(solution)/shard_map/ppermute | solution.py:319
  76.0 13.6 %collective-permute-start.10 = (f32[2,128]{1,0:T(2,128)}, f32[2,128]{1,0:T(2,128)S(1)}, u32[]{:S(2)}, u32[]{:S(2)}) collective-permute-start(f32[2,128]{1,0:T(2,128)} %get-tuple-element.26), channel_id=1, source_target_pairs={{0,1},{1,0},{2,3},{3,2},{4,5},{5,4},{6,7},{7,6},{8,9},{9,8},{10,11... | collective-permute-start | bytes 3080 | tf_op jit(solution)/shard_map/ppermute | solution.py:319
  76.1 38.6 %collective-permute-start.12 = (bf16[256,512]{1,0:T(8,128)(2,1)}, bf16[256,512]{1,0:T(8,128)(2,1)S(1)}, u32[]{:S(2)}, u32[]{:S(2)}) collective-permute-start(bf16[256,512]{1,0:T(8,128)(2,1)} %get-tuple-element.32), channel_id=1, source_target_pairs={{2,0},{4,2},{6,4},{8,6},{10,8},{12,10},{14,12},{3,1},{5,3},{7,5},{... | collective-permute-start | bytes 786440 | tf_op jit(solution)/shard_map/ppermute | solution.py:325
  86.4 28.4 %collective-permute-start.13 = (bf16[256,512]{1,0:T(8,128)(2,1)}, bf16[256,512]{1,0:T(8,128)(2,1)S(1)}, u32[]{:S(2)}, u32[]{:S(2)}) collective-permute-start(bf16[256,512]{1,0:T(8,128)(2,1)} %get-tuple-element.33), channel_id=1, source_target_pairs={{4,0},{6,2},{8,4},{10,6},{12,8},{14,10},{5,1},{7,3},{9,5},{11,7},{... | collective-permute-start | bytes 786440 | tf_op jit(solution)/shard_map/ppermute | solution.py:325
  88.3 26.4 %collective-permute-start.14 = (bf16[256,512]{1,0:T(8,128)(2,1)}, bf16[256,512]{1,0:T(8,128)(2,1)S(1)}, u32[]{:S(2)}, u32[]{:S(2)}) collective-permute-start(bf16[256,512]{1,0:T(8,128)(2,1)} %get-tuple-element.34), channel_id=1, source_target_pairs={{6,0},{8,2},{10,4},{12,6},{14,8},{7,1},{9,3},{11,5},{13,7},{15,9},... | collective-permute-start | bytes 786440 | tf_op jit(solution)/shard_map/ppermute | solution.py:325
  89.6 25.1 %collective-permute-start.15 = (bf16[256,512]{1,0:T(8,128)(2,1)}, bf16[256,512]{1,0:T(8,128)(2,1)S(1)}, u32[]{:S(2)}, u32[]{:S(2)}) collective-permute-start(bf16[256,512]{1,0:T(8,128)(2,1)} %get-tuple-element.35), channel_id=1, source_target_pairs={{8,0},{10,2},{12,4},{14,6},{9,1},{11,3},{13,5},{15,7},{24,16},{26,... | collective-permute-start | bytes 786440 | tf_op jit(solution)/shard_map/ppermute | solution.py:325
  92.3 22.4 %all-to-all-start.1 = ((f32[64,1,256]{2,1,0:T(1,128)}), f32[64,1,256]{2,1,0:T(1,128)S(1)}, u32[]{:S(2)}, u32[]{:S(2)}) async-start(f32[64,1,256]{2,1,0:T(1,128)} %broadcast_in_dim.9), calls=%async_computation.1 | async-start | bytes 131072 | tf_op jit(solution)/shard_map/all_to_all | solution.py:382
  115.4 3.0 %collective-permute-start.16 = (bf16[128,512]{1,0:T(8,128)(2,1)S(1)}, bf16[128,512]{1,0:T(8,128)(2,1)S(1)}, u32[]{:S(2)}, u32[]{:S(2)}) collective-permute-start(bf16[128,512]{1,0:T(8,128)(2,1)S(1)} %get-tuple-element.37), channel_id=1, source_target_pairs={{0,1},{1,0},{2,3},{3,2},{4,5},{5,4},{6,7},{7,6},{8,9},{9,8},{10,11... | collective-permute-start | bytes 393224 | tf_op jit(solution)/shard_map/ppermute | solution.py:319
  (14 other events, 92.6 us)

commit v4 on v3

--- a/solution.py
+++ b/solution.py
@@ -122,11 +122,12 @@
 
 
 def heads_kernel(
-    core_ref, src_ref, recv_ref, kv4, kv3, kv2, kv1, kv0, g_own, g_sib, tc, ts, bias, qg_ref, kg_ref,
+    core_ref, src_ref, recv_ref, kv4, kv3a, kv3b, kv2, kv1, kv0, g_own, g_sib, tc, ts, bias, qg_ref, kg_ref,
     dq_own, dq_sib, out1, out2, out3, out4, own_ref, gains_ref,
-    kr, kt, vs, xq, q8s, g8s, sc0, sc1, dp0, dp1, pb0, pb1, db0, db1, dk_acc, dv_acc,
+    kv3, kr, kt, vs, xq, q8s, g8s, sc0, sc1, dp0, dp1, pb0, pb1, db0, db1, dk_acc, dv_acc,
 ):
     core = core_ref[0]
+    kv3[...] = kv3a[...] + kv3b[...]
     kvs = (kv4, kv3, kv2, kv1, kv0)
     lane = lax.broadcasted_iota(jnp.int32, (TILE, TILE), 1)
     sub = lax.broadcasted_iota(jnp.int32, (TILE, TILE), 0)
@@ -261,7 +262,7 @@
     other_ref[...] = both[1 - core]
 
 
-def head_grads(core1, src, recv, kv4, kv3, kv2, kv1, kv0, grad_out, g_sib, tc, ts, bias, q_gain, k_gain):
+def head_grads(core1, src, recv, kv4, kv3, kv3r, kv2, kv1, kv0, grad_out, g_sib, tc, ts, bias, q_gain, k_gain):
     sds = jax.ShapeDtypeStruct
     groups, wide = recv.shape[0] // 2, 16 * HD
     rows2 = 2 * TILE
@@ -277,7 +278,7 @@
             num_scalar_prefetch=2,
             grid=(1,),
             in_specs=[pl.BlockSpec((2 * groups, RUN, wide), lambda i, c, s: (0, 0, 0))]
-            + [whole(rows2, 4 * HD)] * 5
+            + [whole(rows2, 4 * HD)] * 6
             + [pl.BlockSpec((TILE, wide), lambda i, c, s: (0, c[0]))]
             + [whole(TILE, wide)]
             + [whole(ALLW, HD)] * 2
@@ -285,6 +286,7 @@
             + [whole(1, HD)] * 2,
             out_specs=[whole(TILE, wide)] * 2 + [whole(rows2, 4 * HD)] * 5 + [whole(2, HD)],
             scratch_shapes=[
+                pltpu.VMEM((rows2, 4 * HD), BF),
                 pltpu.VMEM((2, ALLW, HD), BF),
                 pltpu.VMEM((2, HD, ALLW), BF),
                 pltpu.VMEM((2, ALLW, HD), BF),
@@ -300,7 +302,7 @@
         cost_estimate=pl.CostEstimate(flops=6 * 10**9, bytes_accessed=12 * 10**6, transcendentals=5 * 10**6),
         name="head_grads",
     )(
-        core1, src, recv, kv4, kv3, kv2, kv1, kv0, grad_out, g_sib, tc, ts, bias,
+        core1, src, recv, kv4, kv3, kv3r, kv2, kv1, kv0, grad_out, g_sib, tc, ts, bias,
         q_gain.reshape(1, HD), k_gain.reshape(1, HD),
     )
 
@@ -360,6 +362,7 @@
         name="rope_tables",
     )(core1, *id_win[::-1], ids, freq)
     g_sib = to_sibling(lax.dynamic_slice_in_dim(grad_out, (1 - core) * wide, wide, 1))
+    recv, tc, ts, bias = lax.optimization_barrier((recv, tc, ts, bias))
     kv0 = pl.pallas_call(
         keys_kernel,
         out_shape=sds((rows2, 4 * HD), BF),
@@ -369,9 +372,11 @@
         compiler_params=PARAMS,
         name="own_keys",
     )(src, recv)
-    kv = [ahead(kv0, d) for d in range(1, 5)]
+    kv = {d: ahead(kv0, d) for d in (4, 2, 1)}
+    straight = lax.ppermute(kv0, "chip", [(i, i + 3) for i in range(0, chips - 3, 2)])
+    relayed = lax.ppermute(kv[4], "chip", [(i + 1, i) for i in range(4, chips, 2)])
     dq_mine, dq_other, *parts, own, gains = head_grads(
-        core1, src, recv, *kv[::-1], kv0, grad_out, g_sib, tc, ts, bias, q_gain, k_gain
+        core1, src, recv, kv[4], straight, relayed, kv[2], kv[1], kv0, grad_out, g_sib, tc, ts, bias, q_gain, k_gain
     )
     back = [behind(part, d) for d, part in zip(range(1, 5), parts)]
     dq_got = to_sibling(dq_other)

time: 120 us -> 118 us (0.983)
  starting transfers between devices: 58.3 us -> 50.8 us
  waiting for transfers between devices: 21.9 us -> 27.6 us
    ppermute x4, starting transfers between devices: 14.8 us -> 7.27 us  [behind(): return lax.ppermute(x, 'chip', [(i, i - d) for i in range(d, chips)])]
    ppermute x0 -> x2, waiting for transfers between devices: none -> 5.29 us  [the longest x1 5.28 us: body(): lax.ppermute(kv0, 'chip', [(i, i + 3) for i in range(0, chips - 3, 2)])]
    all_to_all x1, waiting for transfers between devices: 8.43 us -> 3.95 us  [body(): recv = lax.all_to_all(packed, ('dp', 'core'), 0, 0, tiled=True)]
    ppermute x8 -> x7, waiting for transfers between devices: 1.7 us -> 6.09 us  [ahead(): return lax.ppermute(x, 'chip', [(i, i + d) for i in range(chips - d)])]
    ppermute x5, starting transfers between devices: 6.13 us -> 2.11 us  [to_sibling(): return lax.ppermute(x, 'core', [(0, 1), (1, 0)])]
    all_to_all x1, starting transfers between devices: 8.72 us -> 11.9 us  [body(): lax.all_to_all(spread, ('dp', 'chip'), 0, 0, tiled=True)]
    ppermute x0 -> x2, starting transfers between devices: none -> 2.59 us  [the longest x1 1.74 us: body(): lax.ppermute(kv0, 'chip', [(i, i + 3) for i in range(0, chips - 3, 2)])]
    ppermute x8 -> x7, starting transfers between devices: 20.1 us -> 18.4 us  [ahead(): return lax.ppermute(x, 'chip', [(i, i + d) for i in range(chips - d)])]
  transfers between devices with their start and end apart: 19 -> 20, of which waited for: 5 -> 7; matrix products, arithmetic and copies ran while one was open for 4% -> 4% of each run, Pallas kernels for 2% -> 2%
where the time goes in v4:
time: 118 us; the launch traced here: 117 us
  starting transfers between devices  50.8 us (43%)
  Pallas kernels  28.7 us (24%)
  waiting for transfers between devices  27.6 us (23%)
  local copies, waits for them, and re-layouts  4.67 us (4%)
  other arithmetic  4.66 us (4%)
    pallas_call x1, Pallas kernels, head_grads(): pl.pallas_call(heads_kernel, out_shape=[sds((TILE, wide), BF)] * 2 + [sds...  23.7 us
    ppermute x7, starting transfers between devices, ahead(): return lax.ppermute(x, 'chip', [(i, i + d) for i in range(chips - d)])  18.4 us
    all_to_all x1, starting transfers between devices, body(): lax.all_to_all(spread, ('dp', 'chip'), 0, 0, tiled=True)  11.9 us
    all_to_all x1, waiting for transfers between devices, body(): lax.all_to_all(spread, ('dp', 'chip'), 0, 0, tiled=True)  11.4 us
    all_to_all x1, starting transfers between devices, body(): recv = lax.all_to_all(packed, ('dp', 'core'), 0, 0, tiled=True)  8.61 us
    ppermute x4, starting transfers between devices, behind(): return lax.ppermute(x, 'chip', [(i, i - d) for i in range(d, chips)])  7.27 us
    ppermute x7, waiting for transfers between devices, ahead(): return lax.ppermute(x, 'chip', [(i, i + d) for i in range(chips - d)])  6.09 us
    ppermute x1, waiting for transfers between devices, body(): lax.ppermute(kv0, 'chip', [(i, i + 3) for i in range(0, chips - 3, 2)])  5.28 us
  transfers between devices with their start and end apart: 20, of which 7 were waited for; matrix products, arithmetic and copies ran while one was open for 4% of the time, Pallas kernels for 2%

profile of v4, /device:TPU:3, one launch (start us, length us, event | category | flops | bytes accessed | tf_op | source)
XLA Modules:
  0.0 117.5 jit_solution(13099393899373245867)
XLA Ops:
  0.6 2.5 %pack_runs.1 = bf16[16,16,2560]{2,1,0:T(8,128)(2,1)} custom-call(s32[1,8]{1,0:T(1,128)} %plan_ref.1, s32[1]{0:T(128)} %bitcast.1.who_ref, bf16[128,4096]{1,0:T(8,128)(2,1)} %q_ref.1, bf16[128,512]{1,0:T(8,128)(2,1)} %k_ref.1, bf16[128,512]{1,0:T(8,128)(2,1)} %v_ref.1), custom_call_target="tpu_custom_call" | custom-call | tf_op jit(solution)/shard_map/pack_runs/pallas_call | solution.py:336
  3.2 8.6 %all-to-all-start = ((bf16[16,16,2560]{2,1,0:T(8,128)(2,1)}), bf16[16,16,2560]{2,1,0:T(8,128)(2,1)S(1)}, u32[]{:S(2)}, u32[]{:S(2)}) async-start(bf16[16,16,2560]{2,1,0:T(8,128)(2,1)} %pack_runs.1), calls=%async_computation | async-start | bytes 2621440 | tf_op jit(solution)/shard_map/all_to_all | solution.py:345
  13.2 2.6 %collective-permute-start.4 = (s32[1,256]{1,0:T(1,128)S(1)}, s32[1,256]{1,0:T(1,128)S(1)}, u32[]{:S(2)}, u32[]{:S(2)}) collective-permute-start(s32[1,256]{1,0:T(1,128)S(1)} %bitcast.8), channel_id=1, source_target_pairs={{0,2},{2,4},{4,6},{6,8},{8,10},{10,12},{12,14},{1,3},{3,5},{5,7},{... | collective-permute-start | bytes 3080 | tf_op jit(solution)/shard_map/ppermute | solution.py:324
  15.8 3.1 %collective-permute-start.3 = (s32[1,256]{1,0:T(1,128)S(1)}, s32[1,256]{1,0:T(1,128)S(1)}, u32[]{:S(2)}, u32[]{:S(2)}) collective-permute-start(s32[1,256]{1,0:T(1,128)S(1)} %bitcast.9), channel_id=1, source_target_pairs={{0,4},{2,6},{4,8},{6,10},{8,12},{10,14},{1,5},{3,7},{5,9},{7,11},{... | collective-permute-start | bytes 3080 | tf_op jit(solution)/shard_map/ppermute | solution.py:324
  19.0 3.0 %collective-permute-start.2 = (s32[1,256]{1,0:T(1,128)S(1)}, s32[1,256]{1,0:T(1,128)S(1)}, u32[]{:S(2)}, u32[]{:S(2)}) collective-permute-start(s32[1,256]{1,0:T(1,128)S(1)} %bitcast.10), channel_id=1, source_target_pairs={{0,6},{2,8},{4,10},{6,12},{8,14},{1,7},{3,9},{5,11},{7,13},{9,15},... | collective-permute-start | bytes 3080 | tf_op jit(solution)/shard_map/ppermute | solution.py:324
  22.0 1.3 %collective-permute-start.1 = (s32[1,256]{1,0:T(1,128)S(1)}, s32[1,256]{1,0:T(1,128)S(1)}, u32[]{:S(2)}, u32[]{:S(2)}) collective-permute-start(s32[1,256]{1,0:T(1,128)S(1)} %bitcast.11), channel_id=1, source_target_pairs={{0,8},{2,10},{4,12},{6,14},{1,9},{3,11},{5,13},{7,15},{16,24},{18,... | collective-permute-start | bytes 3080 | tf_op jit(solution)/shard_map/ppermute | solution.py:324
  24.0 1.4 %rope_tables.1 = (f32[1280,128]{1,0:T(8,128)S(1)}, f32[1280,128]{1,0:T(8,128)S(1)}, bf16[2,1152,128]{2,1,0:T(8,128)(2,1)S(1)}) custom-call(s32[1]{0:T(128)} %bitcast.core_ref, s32[1,256]{1,0:T(1,128)S(1)} %collective-permute-done.1.id4, s32[1,256]{1,0:T(1,128)S(1)} %collective-permute-done.2.id3, s32[1,256]{1,0:T(1,128)S(1)} %collective-permute-done.3.id2, ...), custom_call_target="tpu_custom_call" | custom-call | tf_op jit(solution)/shard_map/rope_tables/pallas_call | solution.py:355
  26.2 0.8 copy-done.5
  27.9 3.9 %all-to-all-done.recv_ref = bf16[16,16,2560]{2,1,0:T(8,128)(2,1)S(1)} async-done(((bf16[16,16,2560]{2,1,0:T(8,128)(2,1)}), bf16[16,16,2560]{2,1,0:T(8,128)(2,1)S(1)}, u32[]{:S(2)}, u32[]{:S(2)}) %all-to-all-start) | async-done | bytes 1310752 | tf_op jit(solution)/shard_map/all_to_all | solution.py:345
  32.4 3.8 %collective-permute-start.5 = (bf16[256,512]{1,0:T(8,128)(2,1)S(1)}, bf16[256,512]{1,0:T(8,128)(2,1)S(1)}, u32[]{:S(2)}, u32[]{:S(2)}) collective-permute-start(bf16[256,512]{1,0:T(8,128)(2,1)S(1)} %own_keys.1.kv0.kv_ref), channel_id=1, source_target_pairs={{0,8},{2,10},{4,12},{6,14},{1,9},{3,11},{5,13},{7,15},{16,24},{18,... | collective-permute-start | bytes 786440 | tf_op jit(solution)/shard_map/ppermute | solution.py:324
  36.2 2.6 %collective-permute-start.9 = (bf16[256,512]{1,0:T(8,128)(2,1)S(1)}, bf16[256,512]{1,0:T(8,128)(2,1)S(1)}, u32[]{:S(2)}, u32[]{:S(2)}) collective-permute-start(bf16[256,512]{1,0:T(8,128)(2,1)S(1)} %own_keys.1.kv0.kv_ref), channel_id=1, source_target_pairs={{0,2},{2,4},{4,6},{6,8},{8,10},{10,12},{12,14},{1,3},{3,5},{5,7},{... | collective-permute-start | bytes 786440 | tf_op jit(solution)/shard_map/ppermute | solution.py:324
  38.8 1.9 %collective-permute-start.8 = (bf16[256,512]{1,0:T(8,128)(2,1)S(1)}, bf16[256,512]{1,0:T(8,128)(2,1)S(1)}, u32[]{:S(2)}, u32[]{:S(2)}) collective-permute-start(bf16[256,512]{1,0:T(8,128)(2,1)S(1)} %own_keys.1.kv0.kv_ref), channel_id=1, source_target_pairs={{0,4},{2,6},{4,8},{6,10},{8,12},{10,14},{1,5},{3,7},{5,9},{7,11},{... | collective-permute-start | bytes 786440 | tf_op jit(solution)/shard_map/ppermute | solution.py:324
  40.7 1.7 %collective-permute-start.6 = (bf16[256,512]{1,0:T(8,128)(2,1)S(1)}, bf16[256,512]{1,0:T(8,128)(2,1)S(1)}, u32[]{:S(2)}, u32[]{:S(2)}) collective-permute-start(bf16[256,512]{1,0:T(8,128)(2,1)S(1)} %own_keys.1.kv0.kv_ref), channel_id=1, source_target_pairs={{0,6},{4,10},{8,14},{1,7},{5,11},{9,15},{16,22},{20,26},{24,30},{1... | collective-permute-start | bytes 786440 | tf_op jit(solution)/shard_map/ppermute | solution.py:376
  42.5 0.9 collective-permute-start.7
  43.4 5.5 %collective-permute-done.9.kv1 = bf16[256,512]{1,0:T(8,128)(2,1)S(1)} collective-permute-done((bf16[256,512]{1,0:T(8,128)(2,1)S(1)}, bf16[256,512]{1,0:T(8,128)(2,1)S(1)}, u32[]{:S(2)}, u32[]{:S(2)}) %collective-permute-start.9) | collective-permute-done | bytes 262176 | tf_op jit(solution)/shard_map/ppermute | solution.py:324
  48.9 5.3 %collective-permute-done.6.kv3a = bf16[256,512]{1,0:T(8,128)(2,1)S(1)} collective-permute-done((bf16[256,512]{1,0:T(8,128)(2,1)S(1)}, bf16[256,512]{1,0:T(8,128)(2,1)S(1)}, u32[]{:S(2)}, u32[]{:S(2)}) %collective-permute-start.6) | collective-permute-done | bytes 262176 | tf_op jit(solution)/shard_map/ppermute | solution.py:376
  55.0 23.7 %head_grads.1 = (bf16[128,2048]{1,0:T(8,128)(2,1)}, bf16[128,2048]{1,0:T(8,128)(2,1)}, bf16[256,512]{1,0:T(8,128)(2,1)}, bf16[256,512]{1,0:T(8,128)(2,1)}, bf16[...) custom-call(s32[1]{0:T(128)} %bitcast.core_ref, s32[16]{0:T(128)} %copy-done.9, ...), custom_call_target="tpu_custom_call" | custom-call | flops 6000000000 | bytes 12000000 | tf_op jit(solution)/shard_map/head_grads/pallas_call | solution.py:270
  79.5 2.8 %collective-permute-start.13 = (bf16[256,512]{1,0:T(8,128)(2,1)}, bf16[256,512]{1,0:T(8,128)(2,1)S(1)}, u32[]{:S(2)}, u32[]{:S(2)}) collective-permute-start(bf16[256,512]{1,0:T(8,128)(2,1)} %get-tuple-element.40), channel_id=1, source_target_pairs={{2,0},{4,2},{6,4},{8,6},{10,8},{12,10},{14,12},{3,1},{5,3},{7,5},{... | collective-permute-start | bytes 786440 | tf_op jit(solution)/shard_map/ppermute | solution.py:327
  82.3 1.9 %collective-permute-start.14 = (bf16[256,512]{1,0:T(8,128)(2,1)}, bf16[256,512]{1,0:T(8,128)(2,1)S(1)}, u32[]{:S(2)}, u32[]{:S(2)}) collective-permute-start(bf16[256,512]{1,0:T(8,128)(2,1)} %get-tuple-element.41), channel_id=1, source_target_pairs={{4,0},{6,2},{8,4},{10,6},{12,8},{14,10},{5,1},{7,3},{9,5},{11,7},{... | collective-permute-start | bytes 786440 | tf_op jit(solution)/shard_map/ppermute | solution.py:327
  84.2 1.3 %collective-permute-start.15 = (bf16[256,512]{1,0:T(8,128)(2,1)}, bf16[256,512]{1,0:T(8,128)(2,1)S(1)}, u32[]{:S(2)}, u32[]{:S(2)}) collective-permute-start(bf16[256,512]{1,0:T(8,128)(2,1)} %get-tuple-element.42), channel_id=1, source_target_pairs={{6,0},{8,2},{10,4},{12,6},{14,8},{7,1},{9,3},{11,5},{13,7},{15,9},... | collective-permute-start | bytes 786440 | tf_op jit(solution)/shard_map/ppermute | solution.py:327
  85.5 1.3 %collective-permute-start.16 = (bf16[256,512]{1,0:T(8,128)(2,1)}, bf16[256,512]{1,0:T(8,128)(2,1)S(1)}, u32[]{:S(2)}, u32[]{:S(2)}) collective-permute-start(bf16[256,512]{1,0:T(8,128)(2,1)} %get-tuple-element.43), channel_id=1, source_target_pairs={{8,0},{10,2},{12,4},{14,6},{9,1},{11,3},{13,5},{15,7},{24,16},{26,... | collective-permute-start | bytes 786440 | tf_op jit(solution)/shard_map/ppermute | solution.py:327
  88.1 11.9 %all-to-all-start.1 = ((f32[64,1,256]{2,1,0:T(1,128)}), f32[64,1,256]{2,1,0:T(1,128)S(1)}, u32[]{:S(2)}, u32[]{:S(2)}) async-start(f32[64,1,256]{2,1,0:T(1,128)} %broadcast_in_dim.9), calls=%async_computation.1 | async-start | bytes 131072 | tf_op jit(solution)/shard_map/all_to_all | solution.py:387
  100.0 2.8 %maximum_select_fusion = bf16[128,4096]{1,0:T(8,128)(2,1)} fusion(bf16[128,2048]{1,0:T(8,128)(2,1)} %collective-permute-done.12, bf16[128,2048]{1,0:T(8,128)(2,1)} %get-tuple-element.33, pred[]{:T(512)S(6)} %eq.4), kind=kLoop, calls=%fused_computation | loop fusion | flops 4718592 | bytes 2097153 | tf_op jit(solution)/shard_map/jit(_where)/select_n | solution.py:330
  102.8 11.4 %all-to-all-done.1 = f32[64,1,256]{2,1,0:T(1,128)S(1)} async-done(((f32[64,1,256]{2,1,0:T(1,128)}), f32[64,1,256]{2,1,0:T(1,128)S(1)}, u32[]{:S(2)}, u32[]{:S(2)}) %all-to-all-start.1) | async-done | bytes 65568 | tf_op jit(solution)/shard_map/all_to_all | solution.py:387
  (78 shorter events, 10.4 us)
Async XLA Ops:
  3.2 28.6 %all-to-all-start = ((bf16[16,16,2560]{2,1,0:T(8,128)(2,1)}), bf16[16,16,2560]{2,1,0:T(8,128)(2,1)S(1)}, u32[]{:S(2)}, u32[]{:S(2)}) async-start(bf16[16,16,2560]{2,1,0:T(8,128)(2,1)} %pack_runs.1), calls=%async_computation | async-start | bytes 2621440 | tf_op jit(solution)/shard_map/all_to_all | solution.py:345
  11.9 1.2 collective-permute-start
  12.1 31.3 %collective-permute-start.10 = (bf16[128,2048]{1,0:T(8,128)(2,1)S(1)}, bf16[128,2048]{1,0:T(8,128)(2,1)S(1)}, u32[]{:S(2)}, u32[]{:S(2)}) collective-permute-start(bf16[128,2048]{1,0:T(8,128)(2,1)S(1)} %constant_dynamic-slice_fusion), channel_id=1, source_target_pairs={{0,1},{1,0},{2,3},{3,2},{4,5},{5,4},{6,7},{7,6},{8,9},{9,8},{10,11... | collective-permute-start | bytes 1572872 | tf_op jit(solution)/shard_map/ppermute | solution.py:321
  13.2 10.2 %collective-permute-start.4 = (s32[1,256]{1,0:T(1,128)S(1)}, s32[1,256]{1,0:T(1,128)S(1)}, u32[]{:S(2)}, u32[]{:S(2)}) collective-permute-start(s32[1,256]{1,0:T(1,128)S(1)} %bitcast.8), channel_id=1, source_target_pairs={{0,2},{2,4},{4,6},{6,8},{8,10},{10,12},{12,14},{1,3},{3,5},{5,7},{... | collective-permute-start | bytes 3080 | tf_op jit(solution)/shard_map/ppermute | solution.py:324
  15.8 7.5 %collective-permute-start.3 = (s32[1,256]{1,0:T(1,128)S(1)}, s32[1,256]{1,0:T(1,128)S(1)}, u32[]{:S(2)}, u32[]{:S(2)}) collective-permute-start(s32[1,256]{1,0:T(1,128)S(1)} %bitcast.9), channel_id=1, source_target_pairs={{0,4},{2,6},{4,8},{6,10},{8,12},{10,14},{1,5},{3,7},{5,9},{7,11},{... | collective-permute-start | bytes 3080 | tf_op jit(solution)/shard_map/ppermute | solution.py:324
  19.0 4.4 %collective-permute-start.2 = (s32[1,256]{1,0:T(1,128)S(1)}, s32[1,256]{1,0:T(1,128)S(1)}, u32[]{:S(2)}, u32[]{:S(2)}) collective-permute-start(s32[1,256]{1,0:T(1,128)S(1)} %bitcast.10), channel_id=1, source_target_pairs={{0,6},{2,8},{4,10},{6,12},{8,14},{1,7},{3,9},{5,11},{7,13},{9,15},... | collective-permute-start | bytes 3080 | tf_op jit(solution)/shard_map/ppermute | solution.py:324
  22.0 2.0 %collective-permute-start.1 = (s32[1,256]{1,0:T(1,128)S(1)}, s32[1,256]{1,0:T(1,128)S(1)}, u32[]{:S(2)}, u32[]{:S(2)}) collective-permute-start(s32[1,256]{1,0:T(1,128)S(1)} %bitcast.11), channel_id=1, source_target_pairs={{0,8},{2,10},{4,12},{6,14},{1,9},{3,11},{5,13},{7,15},{16,24},{18,... | collective-permute-start | bytes 3080 | tf_op jit(solution)/shard_map/ppermute | solution.py:324
  32.4 10.1 %collective-permute-start.5 = (bf16[256,512]{1,0:T(8,128)(2,1)S(1)}, bf16[256,512]{1,0:T(8,128)(2,1)S(1)}, u32[]{:S(2)}, u32[]{:S(2)}) collective-permute-start(bf16[256,512]{1,0:T(8,128)(2,1)S(1)} %own_keys.1.kv0.kv_ref), channel_id=1, source_target_pairs={{0,8},{2,10},{4,12},{6,14},{1,9},{3,11},{5,13},{7,15},{16,24},{18,... | collective-permute-start | bytes 786440 | tf_op jit(solution)/shard_map/ppermute | solution.py:324
  36.2 12.7 %collective-permute-start.9 = (bf16[256,512]{1,0:T(8,128)(2,1)S(1)}, bf16[256,512]{1,0:T(8,128)(2,1)S(1)}, u32[]{:S(2)}, u32[]{:S(2)}) collective-permute-start(bf16[256,512]{1,0:T(8,128)(2,1)S(1)} %own_keys.1.kv0.kv_ref), channel_id=1, source_target_pairs={{0,2},{2,4},{4,6},{6,8},{8,10},{10,12},{12,14},{1,3},{3,5},{5,7},{... | collective-permute-start | bytes 786440 | tf_op jit(solution)/shard_map/ppermute | solution.py:324
  38.8 10.1 %collective-permute-start.8 = (bf16[256,512]{1,0:T(8,128)(2,1)S(1)}, bf16[256,512]{1,0:T(8,128)(2,1)S(1)}, u32[]{:S(2)}, u32[]{:S(2)}) collective-permute-start(bf16[256,512]{1,0:T(8,128)(2,1)S(1)} %own_keys.1.kv0.kv_ref), channel_id=1, source_target_pairs={{0,4},{2,6},{4,8},{6,10},{8,12},{10,14},{1,5},{3,7},{5,9},{7,11},{... | collective-permute-start | bytes 786440 | tf_op jit(solution)/shard_map/ppermute | solution.py:324
  40.7 13.4 %collective-permute-start.6 = (bf16[256,512]{1,0:T(8,128)(2,1)S(1)}, bf16[256,512]{1,0:T(8,128)(2,1)S(1)}, u32[]{:S(2)}, u32[]{:S(2)}) collective-permute-start(bf16[256,512]{1,0:T(8,128)(2,1)S(1)} %own_keys.1.kv0.kv_ref), channel_id=1, source_target_pairs={{0,6},{4,10},{8,14},{1,7},{5,11},{9,15},{16,22},{20,26},{24,30},{1... | collective-permute-start | bytes 786440 | tf_op jit(solution)/shard_map/ppermute | solution.py:376
  42.5 11.7 %collective-permute-start.7 = (bf16[256,512]{1,0:T(8,128)(2,1)S(1)}, bf16[256,512]{1,0:T(8,128)(2,1)S(1)}, u32[]{:S(2)}, u32[]{:S(2)}) collective-permute-start(bf16[256,512]{1,0:T(8,128)(2,1)S(1)} %collective-permute-done.5.kv4), channel_id=1, source_target_pairs={{10,8},{14,12},{11,9},{15,13},{26,24},{30,28},{27,25},{31,29},{42,... | collective-permute-start | bytes 786440 | tf_op jit(solution)/shard_map/ppermute | solution.py:377
  78.7 35.7 %copy-start.4 = (f32[1280,128]{1,0:T(8,128)S(1)}, f32[1280,128]{1,0:T(8,128)}, u32[]{:S(2)}) copy-start(f32[1280,128]{1,0:T(8,128)} %copy-done.3) | copy-start | bytes 1966084
  78.7 35.7 %copy-start.6 = (f32[1280,128]{1,0:T(8,128)S(1)}, f32[1280,128]{1,0:T(8,128)}, u32[]{:S(2)}) copy-start(f32[1280,128]{1,0:T(8,128)} %copy-done.5) | copy-start | bytes 1966084
  78.7 35.7 %copy-start.7 = (f32[256,512]{1,0:T(8,128)S(1)}, f32[256,512]{1,0:T(8,128)}, u32[]{:S(2)}) copy-start(f32[256,512]{1,0:T(8,128)} %get-tuple-element.39.own_ref) | copy-start | bytes 1572868
  78.7 35.7 %copy-start.8 = (f32[128]{0:T(128)S(1)}, f32[128]{0:T(128)}, u32[]{:S(2)}) copy-start(f32[128]{0:T(128)} %param.13) | copy-start | bytes 1540
  78.7 8.8 %collective-permute-start.12 = (bf16[128,2048]{1,0:T(8,128)(2,1)}, bf16[128,2048]{1,0:T(8,128)(2,1)}, u32[]{:S(2)}, u32[]{:S(2)}) collective-permute-start(bf16[128,2048]{1,0:T(8,128)(2,1)} %get-tuple-element.35), channel_id=1, source_target_pairs={{0,1},{1,0},{2,3},{3,2},{4,5},{5,4},{6,7},{7,6},{8,9},{9,8},{10,11... | collective-permute-start | bytes 1572872 | tf_op jit(solution)/shard_map/ppermute | solution.py:321
  79.4 6.1 %collective-permute-start.11 = (f32[2,128]{1,0:T(2,128)}, f32[2,128]{1,0:T(2,128)S(1)}, u32[]{:S(2)}, u32[]{:S(2)}) collective-permute-start(f32[2,128]{1,0:T(2,128)} %get-tuple-element.34), channel_id=1, source_target_pairs={{0,1},{1,0},{2,3},{3,2},{4,5},{5,4},{6,7},{7,6},{8,9},{9,8},{10,11... | collective-permute-start | bytes 3080 | tf_op jit(solution)/shard_map/ppermute | solution.py:321
  79.5 34.8 %collective-permute-start.13 = (bf16[256,512]{1,0:T(8,128)(2,1)}, bf16[256,512]{1,0:T(8,128)(2,1)S(1)}, u32[]{:S(2)}, u32[]{:S(2)}) collective-permute-start(bf16[256,512]{1,0:T(8,128)(2,1)} %get-tuple-element.40), channel_id=1, source_target_pairs={{2,0},{4,2},{6,4},{8,6},{10,8},{12,10},{14,12},{3,1},{5,3},{7,5},{... | collective-permute-start | bytes 786440 | tf_op jit(solution)/shard_map/ppermute | solution.py:327
  82.3 32.0 %collective-permute-start.14 = (bf16[256,512]{1,0:T(8,128)(2,1)}, bf16[256,512]{1,0:T(8,128)(2,1)S(1)}, u32[]{:S(2)}, u32[]{:S(2)}) collective-permute-start(bf16[256,512]{1,0:T(8,128)(2,1)} %get-tuple-element.41), channel_id=1, source_target_pairs={{4,0},{6,2},{8,4},{10,6},{12,8},{14,10},{5,1},{7,3},{9,5},{11,7},{... | collective-permute-start | bytes 786440 | tf_op jit(solution)/shard_map/ppermute | solution.py:327
  84.2 30.1 %collective-permute-start.15 = (bf16[256,512]{1,0:T(8,128)(2,1)}, bf16[256,512]{1,0:T(8,128)(2,1)S(1)}, u32[]{:S(2)}, u32[]{:S(2)}) collective-permute-start(bf16[256,512]{1,0:T(8,128)(2,1)} %get-tuple-element.42), channel_id=1, source_target_pairs={{6,0},{8,2},{10,4},{12,6},{14,8},{7,1},{9,3},{11,5},{13,7},{15,9},... | collective-permute-start | bytes 786440 | tf_op jit(solution)/shard_map/ppermute | solution.py:327
  85.5 28.8 %collective-permute-start.16 = (bf16[256,512]{1,0:T(8,128)(2,1)}, bf16[256,512]{1,0:T(8,128)(2,1)S(1)}, u32[]{:S(2)}, u32[]{:S(2)}) collective-permute-start(bf16[256,512]{1,0:T(8,128)(2,1)} %get-tuple-element.43), channel_id=1, source_target_pairs={{8,0},{10,2},{12,4},{14,6},{9,1},{11,3},{13,5},{15,7},{24,16},{26,... | collective-permute-start | bytes 786440 | tf_op jit(solution)/shard_map/ppermute | solution.py:327
  88.1 26.0 %all-to-all-start.1 = ((f32[64,1,256]{2,1,0:T(1,128)}), f32[64,1,256]{2,1,0:T(1,128)S(1)}, u32[]{:S(2)}, u32[]{:S(2)}) async-start(f32[64,1,256]{2,1,0:T(1,128)} %broadcast_in_dim.9), calls=%async_computation.1 | async-start | bytes 131072 | tf_op jit(solution)/shard_map/all_to_all | solution.py:387
  114.9 1.7 %collective-permute-start.17 = (bf16[128,512]{1,0:T(8,128)(2,1)S(1)}, bf16[128,512]{1,0:T(8,128)(2,1)S(1)}, u32[]{:S(2)}, u32[]{:S(2)}) collective-permute-start(bf16[128,512]{1,0:T(8,128)(2,1)S(1)} %get-tuple-element.45), channel_id=1, source_target_pairs={{0,1},{1,0},{2,3},{3,2},{4,5},{5,4},{6,7},{7,6},{8,9},{9,8},{10,11... | collective-permute-start | bytes 393224 | tf_op jit(solution)/shard_map/ppermute | solution.py:321
  (16 other events, 174.0 us)
